TPU v7x, 256 devices: a whole 4x4x8 slice. The times are simulated.
256 devices in a mesh: ctx: 32 (over y, z), kvh: 8 (over x, core).
Axes of the slice: x: 4, y: 4, z: 8, core: 2. Of those that a mesh axis runs over, the one named last changes fastest.
Arguments:
- front_hidden: bfloat16 [8192, 4096], P('ctx', 'kvh'), may hold values from -6 to 6
- norm_gain: bfloat16 [4096], replicated, may hold values from 0.099609375 to 1.8984375
- w_qkv: bfloat16 [4096, 6144], P(None, 'kvh')
- block_span: int32 [32], replicated, may hold values from 0 to 31, each once
- back_pages: bfloat16 [8192, 8, 2, 16, 128], P('ctx', 'kvh'), may hold values from -6 to 6
- page_dest: int32 [8192], P('ctx'), may hold values from -1 to 31, as said below
Outputs:
- attn_out: bfloat16 [8192, 4096], P('ctx', 'kvh')
- front_cache: bfloat16 [8192, 8, 256], P('ctx', 'kvh')
- restored_pages: bfloat16 [8192, 8, 2, 16, 128], P('ctx', 'kvh')
- page_count: int32 [32], P('ctx')
Inputs may be any that keep to these rules, and one draw needn't show every extreme that they name: `block_span`: a permutation of the span numbers. `page_dest`: the slots of one store name each owner at most 8 times, and some store names some owner exactly 8 times; every owner receives at most 256 pages over all stores, and some owner exactly 256.
All inputs are finite; a program needn't handle non-finite values.
Results may differ from a plain program's by a relative error of at most 0.008.
The roundings to bfloat16 on the way count: a program that leaves them out, or rounds other values in their place, can miss the bound.
Values may be sent and summed in bfloat16 or wider, within the bound.
No kernel may reach another device: no remote copies, remote signals or barrier semaphores. Data moves between devices by JAX's collectives and lax.ppermute only.
A program may use at most 64 MiB of HBM per device.

v0:
```python
import functools

import jax
import jax.numpy as jnp
from jax import lax
from jax.experimental import pallas as pl
from jax.experimental.pallas import tpu as pltpu
from jax.sharding import PartitionSpec as P

HD = 128
GQ = 4
SPAN = 256
SEND_CAP = 8
NY = 4
NZ = 8
N_CTX = NY * NZ
OWN_CAP = N_CTX * SEND_CAP
FIRST = 3
SECOND = SEND_CAP - FIRST
D = 4096
ROWS = GQ * SPAN
PAGE_ROWS = 32
ROPE_BASE = 500000.0
MASK_FILL = -1e30
SCALE_LOG2 = HD**-0.5 * 1.4426950408889634
MARK = 64.0
STATS = 16
STEPS_X = (0, 1, 3, 2)
STEPS_Y = (0, -1, 1, 2)
STEPS_Z = (0, -1, -2, -3, 1, 2, 3, 4)

VMEM = pl.BlockSpec(memory_space=pltpu.VMEM)
SMEM = pl.BlockSpec(memory_space=pltpu.SMEM)
HBM = pl.BlockSpec(memory_space=pltpu.HBM)


def params(mib):
    return pltpu.CompilerParams(vmem_limit_bytes=mib * 2**20)


def cost(mib):
    return pl.CostEstimate(flops=0, bytes_accessed=mib * 2**20, transcendentals=0)


def bucket_kernel(dest_hbm, pages_hbm, first_out, second_out, *refs):
    dest_ref, pages_ref, held_ref, count_ref, in_sems, sems = refs
    loads = [
        pltpu.make_async_copy(dest_hbm, dest_ref, in_sems.at[0]),
        pltpu.make_async_copy(pages_hbm, pages_ref, in_sems.at[1]),
    ]
    for load in loads:
        load.start()
    for owner in range(N_CTX + 1):
        count_ref[owner] = 0
    for load in loads:
        load.wait()

    def put(page, carry):
        owner = dest_ref[page]
        held = owner >= 0
        entry = jnp.where(held, owner, N_CTX)
        rank = count_ref[entry]
        count_ref[entry] = rank + 1
        held_ref[entry, jnp.where(held, rank, 0)] = pages_ref[page]
        return carry

    lax.fori_loop(0, OWN_CAP, put, 0, unroll=16)

    for entry in range(N_CTX):
        count = count_ref[entry]
        value = jnp.full((16, HD), MARK + count.astype(jnp.float32), jnp.float32)
        here = held_ref[entry, SEND_CAP - 1, 0:16, :]
        marked = jnp.where(count < SEND_CAP, value.astype(jnp.bfloat16), here)
        held_ref[entry, SEND_CAP - 1, 0:16, :] = marked
    buckets = held_ref.at[pl.ds(0, N_CTX)]
    copies = [
        pltpu.make_async_copy(buckets.at[:, pl.ds(0, FIRST)], first_out, sems.at[0]),
        pltpu.make_async_copy(buckets.at[:, pl.ds(FIRST, SECOND)], second_out, sems.at[1]),
    ]
    for copy in copies:
        copy.start()
    for copy in copies:
        copy.wait()


def bucket(page_dest, pages):
    return pl.pallas_call(
        bucket_kernel,
        out_shape=tuple(
            jax.ShapeDtypeStruct((N_CTX, n, PAGE_ROWS, HD), jnp.bfloat16) for n in (FIRST, SECOND)
        ),
        in_specs=[HBM, HBM],
        out_specs=(HBM, HBM),
        scratch_shapes=[
            pltpu.SMEM((OWN_CAP,), jnp.int32),
            pltpu.VMEM((OWN_CAP, PAGE_ROWS, HD), jnp.bfloat16),
            pltpu.VMEM((N_CTX + 1, SEND_CAP, PAGE_ROWS, HD), jnp.bfloat16),
            pltpu.SMEM((N_CTX + 1,), jnp.int32),
            pltpu.SemaphoreType.DMA((2,)),
            pltpu.SemaphoreType.DMA((2,)),
        ],
        compiler_params=params(56),
        cost_estimate=cost(18),
        name="bucket",
    )(page_dest, pages)


def place_kernel(first_ref, second_ref, out_ref, total_ref, held_ref, placed_ref, sems):
    copies = [
        pltpu.make_async_copy(first_ref, held_ref.at[:, pl.ds(0, FIRST)], sems.at[0]),
        pltpu.make_async_copy(second_ref, held_ref.at[:, pl.ds(FIRST, SECOND)], sems.at[1]),
    ]
    for copy in copies:
        copy.start()
    for copy in copies:
        copy.wait()
    offset = jnp.int32(0)
    for store in range(N_CTX):
        last = held_ref[store, SEND_CAP - 1, 0:16, :].astype(jnp.float32)
        top = jnp.max(last)
        count = jnp.where(top > MARK / 2, (top - MARK).astype(jnp.int32), SEND_CAP)
        for rank in range(SEND_CAP):
            placed_ref[offset + rank] = held_ref[store, rank]
        offset = offset + count
    total_ref[0] = offset

    def clear(page, carry):
        placed_ref[page] = jnp.zeros((PAGE_ROWS, HD), jnp.bfloat16)
        return carry

    lax.fori_loop(offset, OWN_CAP, clear, 0)
    copy = pltpu.make_async_copy(placed_ref.at[pl.ds(0, OWN_CAP)], out_ref, sems.at[0])
    copy.start()
    copy.wait()


def place(first, second):
    return pl.pallas_call(
        place_kernel,
        out_shape=(
            jax.ShapeDtypeStruct((OWN_CAP, PAGE_ROWS, HD), jnp.bfloat16),
            jax.ShapeDtypeStruct((1,), jnp.int32),
        ),
        in_specs=[HBM, HBM],
        out_specs=(HBM, SMEM),
        scratch_shapes=[
            pltpu.VMEM((N_CTX, SEND_CAP, PAGE_ROWS, HD), jnp.bfloat16),
            pltpu.VMEM((OWN_CAP + SEND_CAP, PAGE_ROWS, HD), jnp.bfloat16),
            pltpu.SemaphoreType.DMA((2,)),
        ],
        compiler_params=params(16),
        cost_estimate=cost(10),
        name="place",
    )(first, second)


def project_kernel(gain_ref, cos_ref, sin_ref, w_hbm, *refs):
    blocks = refs[:8]
    qt_ref, cache_ref, msg_ref, w_ref, normed_ref, sems = refs[8:]
    width = blocks[0].shape[1]
    loads = [
        pltpu.make_async_copy(
            w_hbm.at[pl.ds(at * width, width)], w_ref.at[pl.ds(at * width, width)], sems.at[at]
        )
        for at in range(8)
    ]
    for load in loads:
        load.start()
    squares = jnp.zeros((SPAN, HD), jnp.float32)
    for block in blocks:
        for at in range(0, width, HD):
            part = block[:, at : at + HD].astype(jnp.float32)
            squares = squares + part * part
    inverse = lax.rsqrt(jnp.sum(squares, axis=1, keepdims=True) * (1.0 / D) + 1e-05)
    my_kvh = lax.axis_index("kvh")
    my_x, my_core = my_kvh // 2, my_kvh % 2
    for number, block in enumerate(blocks):
        source = (my_x - STEPS_X[number % 4]) & 3
        index = source * 2 + (my_core if number < 4 else 1 - my_core)
        gain = gain_ref[pl.ds(index, 1), :]
        normed = block[...].astype(jnp.float32) * inverse * gain
        start = pl.multiple_of(index * width, width)
        normed_ref[:, pl.ds(start, width)] = normed.astype(jnp.bfloat16)
    for load in loads:
        load.wait()
    projected = jnp.dot(normed_ref[...], w_ref[...], preferred_element_type=jnp.float32)
    cosine = cos_ref[...]
    sine = sin_ref[...]

    def rope(u):
        return u * cosine + pltpu.roll(u, HD // 2, 1) * sine

    for head in range(GQ):
        turned = rope(projected[:, head * HD : (head + 1) * HD])
        qt_ref[:, head * SPAN : (head + 1) * SPAN] = turned.T.astype(jnp.bfloat16)
    key = rope(projected[:, GQ * HD : (GQ + 1) * HD]).astype(jnp.bfloat16)
    value = projected[:, (GQ + 1) * HD :]
    cache_ref[:, :HD] = key
    cache_ref[:, HD:] = value.astype(jnp.bfloat16)
    msg_ref[:, :HD] = key
    for at in (0, HD):
        msg_ref[at : at + HD, HD:] = value[at : at + HD].T.astype(jnp.bfloat16)


def project(gain, cosine, sine, w_qkv, blocks):
    return pl.pallas_call(
        project_kernel,
        out_shape=(
            jax.ShapeDtypeStruct((HD, ROWS), jnp.bfloat16),
            jax.ShapeDtypeStruct((SPAN, 2 * HD), jnp.bfloat16),
            jax.ShapeDtypeStruct((SPAN, 2 * HD), jnp.bfloat16),
        ),
        in_specs=[VMEM] * 3 + [HBM] + [VMEM] * 8,
        out_specs=(VMEM, VMEM, VMEM),
        scratch_shapes=[
            pltpu.VMEM(w_qkv.shape, jnp.bfloat16),
            pltpu.VMEM((SPAN, D), jnp.bfloat16),
            pltpu.SemaphoreType.DMA((8,)),
        ],
        compiler_params=params(56),
        cost_estimate=cost(16),
        name="project",
    )(gain, cosine, sine, w_qkv, *blocks)


def attend_kernel(steps, span_ref, *refs):
    size = len(steps)
    queries = refs[:size]
    messages = refs[size : size + NZ]
    outs = refs[size + NZ : 2 * size + NZ]
    kv_ref, acc_ref, max_ref, sum_ref, list_ref = refs[2 * size + NZ :]
    my_index = lax.axis_index("ctx")
    my_y, my_z = my_index // NZ, my_index % NZ
    for number, message in enumerate(messages):
        kv_ref[number] = message[...]
    key_at = lax.broadcasted_iota(jnp.int32, (SPAN, SPAN), 0)
    query_at = lax.broadcasted_iota(jnp.int32, (SPAN, SPAN), 1)
    heads = [slice(head * SPAN, (head + 1) * SPAN) for head in range(GQ)]
    key_spans = [span_ref[my_y * NZ + ((my_z + step) & (NZ - 1))] for step in STEPS_Z]

    for number, away in enumerate(steps):
        query_ref = queries[number]
        query_span = span_ref[((my_y + away) & (NY - 1)) * NZ + my_z]
        acc_ref[...] = jnp.zeros_like(acc_ref)
        max_ref[...] = jnp.full_like(max_ref, MASK_FILL)
        sum_ref[...] = jnp.zeros_like(sum_ref)

        def update(parts, masked):
            keys, values = [], []
            for part in parts:
                keys.append(kv_ref[part, :, :HD])
                value = kv_ref[part, :, HD:]
                values += [value[:HD], value[HD:]]
            key = jnp.concatenate(keys, axis=0)
            value = jnp.concatenate(values, axis=1)
            scores = [
                jnp.dot(key, query_ref[:, lanes], preferred_element_type=jnp.float32)
                for lanes in heads
            ]
            if masked:
                scores = [jnp.where(key_at <= query_at, score, MASK_FILL) for score in scores]
            old = [max_ref[:, lanes] for lanes in heads]
            new = [
                jnp.maximum(top, jnp.max(score, axis=0, keepdims=True))
                for top, score in zip(old, scores)
            ]
            weights = [jnp.exp2((score - top) * SCALE_LOG2) for score, top in zip(scores, new)]
            fades = [jnp.exp2((before - top) * SCALE_LOG2) for before, top in zip(old, new)]
            products = [
                jnp.dot(value, weight.astype(jnp.bfloat16), preferred_element_type=jnp.float32)
                for weight in weights
            ]
            for head, lanes in enumerate(heads):
                total = jnp.sum(weights[head], axis=0, keepdims=True)
                sum_ref[:, lanes] = sum_ref[:, lanes] * fades[head] + total
                acc_ref[:, lanes] = acc_ref[:, lanes] * fades[head] + products[head]
                max_ref[:, lanes] = new[head]

        earlier = jnp.int32(0)
        for part, key_span in enumerate(key_spans):
            list_ref[earlier] = part
            earlier = earlier + (key_span < query_span).astype(jnp.int32)

        def step(pair, carry):
            update([list_ref[2 * pair], list_ref[2 * pair + 1]], False)
            return carry

        lax.fori_loop(0, earlier // 2, step, 0)

        @pl.when(earlier % 2 == 1)
        def _():
            update([list_ref[earlier - 1]], False)

        if away == 0:
            update([0], True)

        total = jnp.maximum(sum_ref[...], 1.0)
        outs[number][:HD, :] = (acc_ref[...] / total).astype(jnp.bfloat16)
        level = max_ref[...] * SCALE_LOG2 + jnp.log2(total)
        high = level.astype(jnp.bfloat16).astype(jnp.float32)
        middle = (level - high).astype(jnp.bfloat16).astype(jnp.float32)
        low = level - high - middle
        row = lax.broadcasted_iota(jnp.int32, (STATS, ROWS), 0)
        stats = jnp.where(row == 0, high, jnp.where(row == 1, middle, jnp.where(row == 2, low, 0.0)))
        outs[number][HD:, :] = stats.astype(jnp.bfloat16)


def attend(block_span, steps, queries, messages):
    part = jax.ShapeDtypeStruct((HD + STATS, ROWS), jnp.bfloat16)
    return pl.pallas_call(
        functools.partial(attend_kernel, steps),
        out_shape=(part,) * len(steps),
        in_specs=[SMEM] + [VMEM] * (len(steps) + NZ),
        out_specs=(VMEM,) * len(steps),
        scratch_shapes=[
            pltpu.VMEM((NZ, SPAN, 2 * HD), jnp.bfloat16),
            pltpu.VMEM((HD, ROWS), jnp.float32),
            pltpu.VMEM((1, ROWS), jnp.float32),
            pltpu.VMEM((1, ROWS), jnp.float32),
            pltpu.SMEM((NZ + 1,), jnp.int32),
        ],
        compiler_params=params(32),
        cost_estimate=cost(10 * len(steps)),
        name="attend",
    )(block_span, *queries, *messages)


def merge_kernel(*refs):
    parts, out_ref = refs[:NY], refs[NY]
    levels = []
    for part in parts:
        stats = part[HD:, :].astype(jnp.float32)
        levels.append(stats[0:1] + stats[1:2] + stats[2:3])
    top = levels[0]
    for level in levels[1:]:
        top = jnp.maximum(top, level)
    weights = [jnp.exp2(level - top) for level in levels]
    total = weights[0]
    for weight in weights[1:]:
        total = total + weight
    for head in range(GQ):
        lanes = slice(head * SPAN, (head + 1) * SPAN)
        context = jnp.zeros((HD, SPAN), jnp.float32)
        for part, weight in zip(parts, weights):
            context = context + part[:HD, lanes].astype(jnp.float32) * weight[:, lanes]
        context = context / total[:, lanes]
        out_ref[:, head * HD : (head + 1) * HD] = context.T.astype(jnp.bfloat16)


def merge(parts):
    return pl.pallas_call(
        merge_kernel,
        out_shape=jax.ShapeDtypeStruct((SPAN, GQ * HD), jnp.bfloat16),
        in_specs=[VMEM] * NY,
        out_specs=VMEM,
        compiler_params=params(16),
        cost_estimate=cost(4),
        name="merge",
    )(*parts)


def rotation(positions):
    half_dim = HD // 2
    inv_freq = ROPE_BASE ** (-(2 * jnp.arange(half_dim)).astype(jnp.float32) / HD)
    angles = positions.astype(jnp.float32)[:, None] * inv_freq[None, :]
    cosine = jnp.cos(angles)
    sine = jnp.sin(angles)
    return jnp.concatenate([cosine, cosine], axis=1), jnp.concatenate([-sine, sine], axis=1)


def along_x(value, step):
    return lax.ppermute(value, "kvh", [(i, ((i // 2 + step) % 4) * 2 + i % 2) for i in range(8)])


def across(value):
    return lax.ppermute(value, "kvh", [(i, i ^ 1) for i in range(8)])


def along_y(value, step):
    return lax.ppermute(
        value, "ctx", [(i, ((i // NZ + step) % NY) * NZ + i % NZ) for i in range(N_CTX)]
    )


def along_z(value, step):
    return lax.ppermute(
        value, "ctx", [(i, (i // NZ) * NZ + (i % NZ + step) % NZ) for i in range(N_CTX)]
    )


def to_owners(value):
    return lax.all_to_all(value, "ctx", split_axis=0, concat_axis=0, tiled=True)


def shards(front_hidden, norm_gain, w_qkv, block_span, back_pages, page_dest):
    my_index = lax.axis_index("ctx")
    my_core = lax.axis_index("kvh") % 2

    first, second = bucket(page_dest, back_pages.reshape(OWN_CAP, PAGE_ROWS, HD))
    low, high = along_x(front_hidden, 1), along_x(front_hidden, -1)
    first, low, high = lax.optimization_barrier((first, low, high))
    first = to_owners(first)

    opposite = lax.ppermute(
        jnp.where(my_core == 0, low, high),
        "kvh",
        [(i, ((i // 2 + 1 - 2 * (i % 2)) % 4) * 2 + i % 2) for i in range(8)],
    )
    same = [front_hidden, low, high, opposite]
    other = [across(block) for block in same]

    my_span = jnp.sum(jnp.where(jnp.arange(N_CTX) == my_index, block_span, 0))
    cosine, sine = rotation(my_span * SPAN + jnp.arange(SPAN))
    gain = norm_gain.astype(jnp.float32).reshape(8, D // 8)
    query, cache, message = project(gain, cosine, sine, w_qkv, same + other)

    from_up = along_y(query, -1)
    queries = [query, along_y(query, 1), from_up, along_y(from_up, -1)]

    up, down = [message], [message]
    for _ in range(3):
        up.append(along_z(up[-1], 1))
        down.append(along_z(down[-1], -1))
    down.append(along_z(down[-1], -1))
    messages = up + down[1:]

    held = lax.optimization_barrier((second, *messages, *queries))
    second, messages, queries = held[0], held[1 : 1 + NZ], held[1 + NZ :]
    second = to_owners(second)

    back = []
    for group in ((3,), (1, 2), (0,)):
        parts = attend(
            block_span, [STEPS_Y[at] for at in group], [queries[at] for at in group], messages
        )
        for at, part in zip(group, parts):
            back.append(along_y(part, STEPS_Y[at]) if at else part)
    attn_out = merge(back)

    restored, page_count = place(first, second)
    return (
        attn_out,
        cache.reshape(SPAN, 1, 2 * HD),
        restored.reshape(back_pages.shape),
        page_count,
    )


def solution(mesh):
    placed = (
        P("ctx", "kvh"),
        P(),
        P(None, "kvh"),
        P(),
        P("ctx", "kvh", None, None, None),
        P("ctx"),
    )
    return jax.shard_map(
        shards,
        mesh=mesh,
        in_specs=placed,
        out_specs=(
            P("ctx", "kvh"),
            P("ctx", "kvh", None),
            P("ctx", "kvh", None, None, None),
            P("ctx"),
        ),
        check_vma=False,
    )
```

profile of v0, /device:TPU:2, one launch (start us, length us, event | category | flops | bytes accessed | tf_op | source)
XLA Modules:
  0.0 106.4 jit_solution(2255866125601604871)
XLA Ops:
  0.6 0.0 copy-start.9
  0.6 1.6 %collective-permute-start = (bf16[256,512]{1,0:T(8,128)(2,1)}, bf16[256,512]{1,0:T(8,128)(2,1)S(1)}, u32[]{:S(2)}, u32[]{:S(2)}) collective-permute-start(bf16[256,512]{1,0:T(8,128)(2,1)} %refs_0_.1), channel_id=1, source_target_pairs={{0,2},{1,3},{2,4},{3,5},{4,6},{5,7},{6,0},{7,1},{8,10},{9,11},{10,... | collective-permute-start | bytes 786440 | tf_op jit(solution)/shard_map/ppermute | solution.py:372
  2.2 0.9 collective-permute-start.1
  3.1 4.2 %bucket.1 = (bf16[32,3,32,128]{3,2,1,0:T(8,128)(2,1)}, bf16[32,5,32,128]{3,2,1,0:T(8,128)(2,1)}) custom-call(s32[256]{0:T(256)} %dest_hbm.1, bf16[256,32,128]{2,1,0:T(8,128)(2,1)} %bitcast.5), custom_call_target="tpu_custom_call" | custom-call | bytes 18874368 | tf_op jit(solution)/shard_map/bucket/pallas_call | solution.py:87
  7.3 1.7 %collective-permute-done.refs_1_ = bf16[256,512]{1,0:T(8,128)(2,1)S(1)} collective-permute-done((bf16[256,512]{1,0:T(8,128)(2,1)}, bf16[256,512]{1,0:T(8,128)(2,1)S(1)}, u32[]{:S(2)}, u32[]{:S(2)}) %collective-permute-start) | collective-permute-done | bytes 262176 | tf_op jit(solution)/shard_map/ppermute | solution.py:372
  9.0 1.2 %collective-permute-done.1.refs_2_ = bf16[256,512]{1,0:T(8,128)(2,1)S(1)} collective-permute-done((bf16[256,512]{1,0:T(8,128)(2,1)}, bf16[256,512]{1,0:T(8,128)(2,1)S(1)}, u32[]{:S(2)}, u32[]{:S(2)}) %collective-permute-start.1) | collective-permute-done | bytes 262176 | tf_op jit(solution)/shard_map/ppermute | solution.py:372
  10.2 11.5 %all-to-all-start = ((bf16[32,3,32,128]{3,2,1,0:T(8,128)(2,1)}), bf16[32,3,32,128]{3,2,1,0:T(8,128)(2,1)S(1)}, u32[]{:S(2)}, u32[]{:S(2)}) async-start(bf16[32,3,32,128]{3,2,1,0:T(8,128)(2,1)} %get-tuple-element.50), calls=%async_computation | async-start | bytes 1572864 | tf_op jit(solution)/shard_map/all_to_all | solution.py:392
  21.7 0.1 collective-permute-start.3
  21.8 1.3 %collective-permute-start.2 = (bf16[256,512]{1,0:T(8,128)(2,1)S(1)}, bf16[256,512]{1,0:T(8,128)(2,1)S(1)}, u32[]{:S(2)}, u32[]{:S(2)}) collective-permute-start(bf16[256,512]{1,0:T(8,128)(2,1)S(1)} %broadcast_select_fusion), channel_id=1, source_target_pairs={{0,2},{1,7},{2,4},{3,1},{4,6},{5,3},{6,0},{7,5},{8,10},{9,15},{10,... | collective-permute-start | bytes 786440 | tf_op jit(solution)/shard_map/ppermute | solution.py:404
  23.1 0.6 fusion.1
  23.8 0.6 reshape.41.gain_ref
  25.1 0.1 collective-permute-start.4
  25.2 0.5 collective-permute-start.5
  25.7 2.6 %collective-permute-done.2.refs_3_ = bf16[256,512]{1,0:T(8,128)(2,1)S(1)} collective-permute-done((bf16[256,512]{1,0:T(8,128)(2,1)S(1)}, bf16[256,512]{1,0:T(8,128)(2,1)S(1)}, u32[]{:S(2)}, u32[]{:S(2)}) %collective-permute-start.2) | collective-permute-done | bytes 262176 | tf_op jit(solution)/shard_map/ppermute | solution.py:404
  28.3 0.0 collective-permute-start.6
  28.3 0.5 fusion
  28.8 0.8 pad_maximum_fusion
  29.7 0.0 collective-permute-done.3.refs_4_
  29.7 0.0 collective-permute-done.4.refs_5_
  29.7 0.0 collective-permute-done.5.refs_6_
  29.7 0.1 collective-permute-done.6.refs_7_
  29.8 0.5 copy-done.10
  30.4 0.1 copy-done.12
  30.5 0.1 copy-done.13
  30.6 0.1 copy-done.14
  30.7 7.3 %project.1 = (bf16[128,1024]{1,0:T(8,128)(2,1)}, bf16[256,256]{1,0:T(8,128)(2,1)}, bf16[256,256]{1,0:T(8,128)(2,1)}) custom-call(f32[8,512]{1,0:T(8,128)} %reshape.41.gain_ref, f32[256,128]{1,0:T(8,128)} %get-tuple-element.61.cos_ref, f32[256,128]{1,0:T(8,128)} %get-tuple-element.62.sin_ref, bf16[4096,768]{1,0:T(8,128)(2,1)} %w_hbm.1, ...), custom_call_target="tpu_custom_call" | custom-call | bytes 16777216 | tf_op jit(solution)/shard_map/project/pallas_call | solution.py:206
  38.0 3.1 %collective-permute-start.10 = (bf16[256,256]{1,0:T(8,128)(2,1)}, bf16[256,256]{1,0:T(8,128)(2,1)S(1)}, u32[]{:S(2)}, u32[]{:S(2)}) collective-permute-start(bf16[256,256]{1,0:T(8,128)(2,1)} %get-tuple-element.36.refs_1_.refs_2_), channel_id=1, source_target_pairs={{0,56},{8,0},{16,8},{24,16},{32,24},{40,32},{48,40},{56,48},{64,12... | collective-permute-start | bytes 393224 | tf_op jit(solution)/shard_map/ppermute | solution.py:386
  41.0 2.8 %collective-permute-start.15 = (bf16[128,1024]{1,0:T(8,128)(2,1)}, bf16[128,1024]{1,0:T(8,128)(2,1)S(1)}, u32[]{:S(2)}, u32[]{:S(2)}) collective-permute-start(bf16[128,1024]{1,0:T(8,128)(2,1)} %get-tuple-element.48.refs_0_), channel_id=1, source_target_pairs={{0,192},{8,200},{16,208},{24,216},{32,224},{40,232},{48,240},{56,2... | collective-permute-start | bytes 786440 | tf_op jit(solution)/shard_map/ppermute | solution.py:380
  43.8 0.0 collective-permute-start.7
  43.8 1.0 collective-permute-done.10.refs_5_.refs_6_
  44.8 3.6 %collective-permute-start.11 = (bf16[256,256]{1,0:T(8,128)(2,1)S(1)}, bf16[256,256]{1,0:T(8,128)(2,1)S(1)}, u32[]{:S(2)}, u32[]{:S(2)}) collective-permute-start(bf16[256,256]{1,0:T(8,128)(2,1)S(1)} %collective-permute-done.10.refs_5_.refs_6_), channel_id=1, source_target_pairs={{0,56},{8,0},{16,8},{24,16},{32,24},{40,32},{48,40},{56,48},{64,12... | collective-permute-start | bytes 393224 | tf_op jit(solution)/shard_map/ppermute | solution.py:386
  48.4 1.5 %collective-permute-start.14 = (bf16[128,1024]{1,0:T(8,128)(2,1)}, bf16[128,1024]{1,0:T(8,128)(2,1)S(1)}, u32[]{:S(2)}, u32[]{:S(2)}) collective-permute-start(bf16[128,1024]{1,0:T(8,128)(2,1)} %get-tuple-element.48.refs_0_), channel_id=1, source_target_pairs={{0,64},{8,72},{16,80},{24,88},{32,96},{40,104},{48,112},{56,120},{... | collective-permute-start | bytes 786440 | tf_op jit(solution)/shard_map/ppermute | solution.py:380
  49.8 0.7 collective-permute-done.7.refs_2_.refs_3_
  50.6 0.0 collective-permute-start.8
  50.6 0.4 collective-permute-done.11.refs_6_.refs_7_
  51.0 3.7 %collective-permute-start.12 = (bf16[256,256]{1,0:T(8,128)(2,1)S(1)}, bf16[256,256]{1,0:T(8,128)(2,1)S(1)}, u32[]{:S(2)}, u32[]{:S(2)}) collective-permute-start(bf16[256,256]{1,0:T(8,128)(2,1)S(1)} %collective-permute-done.11.refs_6_.refs_7_), channel_id=1, source_target_pairs={{0,56},{8,0},{16,8},{24,16},{32,24},{40,32},{48,40},{56,48},{64,12... | collective-permute-start | bytes 393224 | tf_op jit(solution)/shard_map/ppermute | solution.py:386
  54.7 0.0 collective-permute-done.15.refs_1_
  54.7 2.8 %collective-permute-start.16 = (bf16[128,1024]{1,0:T(8,128)(2,1)S(1)}, bf16[128,1024]{1,0:T(8,128)(2,1)S(1)}, u32[]{:S(2)}, u32[]{:S(2)}) collective-permute-start(bf16[128,1024]{1,0:T(8,128)(2,1)S(1)} %collective-permute-done.15.refs_1_), channel_id=1, source_target_pairs={{0,192},{8,200},{16,208},{24,216},{32,224},{40,232},{48,240},{56,2... | collective-permute-start | bytes 786440 | tf_op jit(solution)/shard_map/ppermute | solution.py:380
  57.5 0.0 collective-permute-done.8.refs_3_.refs_4_
  57.5 0.0 collective-permute-start.9
  57.5 0.0 collective-permute-done.12.refs_7_.refs_8_
  57.5 3.4 %collective-permute-start.13 = (bf16[256,256]{1,0:T(8,128)(2,1)S(1)}, bf16[256,256]{1,0:T(8,128)(2,1)S(1)}, u32[]{:S(2)}, u32[]{:S(2)}) collective-permute-start(bf16[256,256]{1,0:T(8,128)(2,1)S(1)} %collective-permute-done.12.refs_7_.refs_8_), channel_id=1, source_target_pairs={{0,56},{8,0},{16,8},{24,16},{32,24},{40,32},{48,40},{56,48},{64,12... | collective-permute-start | bytes 393224 | tf_op jit(solution)/shard_map/ppermute | solution.py:386
  60.9 0.0 collective-permute-done.14.refs_0_
  60.9 0.7 copy-done.2
  61.6 2.1 %collective-permute-done.9.refs_4_.refs_5_ = bf16[256,256]{1,0:T(8,128)(2,1)S(1)} collective-permute-done((bf16[256,256]{1,0:T(8,128)(2,1)S(1)}, bf16[256,256]{1,0:T(8,128)(2,1)S(1)}, u32[]{:S(2)}, u32[]{:S(2)}) %collective-permute-start.9) | collective-permute-done | bytes 131104 | tf_op jit(solution)/shard_map/ppermute | solution.py:386
  63.7 0.0 collective-permute-done.16.refs_0_
  63.7 0.7 copy-done.4
  64.4 0.0 all-to-all-done.first_ref
  64.4 8.1 %all-to-all-start.1 = ((bf16[32,5,32,128]{3,2,1,0:T(8,128)(2,1)}), bf16[32,5,32,128]{3,2,1,0:T(8,128)(2,1)S(1)}, u32[]{:S(2)}, u32[]{:S(2)}) async-start(bf16[32,5,32,128]{3,2,1,0:T(8,128)(2,1)} %get-tuple-element.51), calls=%async_computation.1 | async-start | bytes 2621440 | tf_op jit(solution)/shard_map/all_to_all | solution.py:392
  72.5 0.0 copy-start.5
  72.5 0.9 copy-done.5
  73.4 2.7 %attend.3 = bf16[144,1024]{1,0:T(8,128)(2,1)S(1)} custom-call(s32[32]{0:T(128)S(1)} %copy-done.6, bf16[128,1024]{1,0:T(8,128)(2,1)S(1)} %copy-done.5, bf16[256,256]{1,0:T(8,128)(2,1)S(1)} %copy-done, bf16[256,256]{1,0:T(8,128)(2,1)S(1)} %collective-permute-done.7.refs_2_.refs_3_, bf16[256,256]{1,0:T(8,128)(2,1)S(1)} %collective-permute-done.8.refs_3_.refs_4_, ...), custom_call_target="tpu_custom_call" | custom-call | bytes 10485760 | tf_op jit(solution)/shard_map/attend/pallas_call | solution.py:310
  76.1 5.4 %collective-permute-start.17 = (bf16[144,1024]{1,0:T(8,128)(2,1)S(1)}, bf16[144,1024]{1,0:T(8,128)(2,1)S(1)}, u32[]{:S(2)}, u32[]{:S(2)}) collective-permute-start(bf16[144,1024]{1,0:T(8,128)(2,1)S(1)} %attend.3), channel_id=1, source_target_pairs={{0,128},{8,136},{16,144},{24,152},{32,160},{40,168},{48,176},{56,1... | collective-permute-start | bytes 884744 | tf_op jit(solution)/shard_map/ppermute | solution.py:380
  81.6 0.9 copy-done.3
  82.5 3.8 %attend.4 = (bf16[144,1024]{1,0:T(8,128)(2,1)S(1)}, bf16[144,1024]{1,0:T(8,128)(2,1)S(1)}) custom-call(s32[32]{0:T(128)S(1)} %copy-done.6, bf16[128,1024]{1,0:T(8,128)(2,1)S(1)} %copy-done.3, bf16[128,1024]{1,0:T(8,128)(2,1)S(1)} %collective-permute-done.15.refs_1_, bf16[256,256]{1,0:T(8,128)(2,1)S(1)} %copy-done, ...), custom_call_target="tpu_custom_call" | custom-call | bytes 20971520 | tf_op jit(solution)/shard_map/attend/pallas_call | solution.py:310
  86.4 1.1 %collective-permute-start.18 = (bf16[144,1024]{1,0:T(8,128)(2,1)S(1)}, bf16[144,1024]{1,0:T(8,128)(2,1)S(1)}, u32[]{:S(2)}, u32[]{:S(2)}) collective-permute-start(bf16[144,1024]{1,0:T(8,128)(2,1)S(1)} %get-tuple-element.46), channel_id=1, source_target_pairs={{0,192},{8,200},{16,208},{24,216},{32,224},{40,232},{48,240},{56,2... | collective-permute-start | bytes 884744 | tf_op jit(solution)/shard_map/ppermute | solution.py:380
  87.5 1.3 %collective-permute-start.19 = (bf16[144,1024]{1,0:T(8,128)(2,1)S(1)}, bf16[144,1024]{1,0:T(8,128)(2,1)S(1)}, u32[]{:S(2)}, u32[]{:S(2)}) collective-permute-start(bf16[144,1024]{1,0:T(8,128)(2,1)S(1)} %get-tuple-element.47), channel_id=1, source_target_pairs={{0,64},{8,72},{16,80},{24,88},{32,96},{40,104},{48,112},{56,120},{... | collective-permute-start | bytes 884744 | tf_op jit(solution)/shard_map/ppermute | solution.py:380
  88.8 4.3 %attend.5.refs_3_ = bf16[144,1024]{1,0:T(8,128)(2,1)S(1)} custom-call(s32[32]{0:T(128)S(1)} %copy-done.6, bf16[128,1024]{1,0:T(8,128)(2,1)S(1)} %copy-done.1, bf16[256,256]{1,0:T(8,128)(2,1)S(1)} %copy-done, bf16[256,256]{1,0:T(8,128)(2,1)S(1)} %collective-permute-done.7.refs_2_.refs_3_, bf16[256,256]{1,0:T(8,128)(2,1)S(1)} %collective-permute-done.8.refs_3_.refs_4_, ...), custom_call_target="tpu_custom_call" | custom-call | bytes 10485760 | tf_op jit(solution)/shard_map/attend/pallas_call | solution.py:310
  93.1 2.3 %collective-permute-done.17.refs_0_ = bf16[144,1024]{1,0:T(8,128)(2,1)S(1)} collective-permute-done((bf16[144,1024]{1,0:T(8,128)(2,1)S(1)}, bf16[144,1024]{1,0:T(8,128)(2,1)S(1)}, u32[]{:S(2)}, u32[]{:S(2)}) %collective-permute-start.17) | collective-permute-done | bytes 294944 | tf_op jit(solution)/shard_map/ppermute | solution.py:380
  95.3 5.7 %collective-permute-done.18.refs_1_ = bf16[144,1024]{1,0:T(8,128)(2,1)S(1)} collective-permute-done((bf16[144,1024]{1,0:T(8,128)(2,1)S(1)}, bf16[144,1024]{1,0:T(8,128)(2,1)S(1)}, u32[]{:S(2)}, u32[]{:S(2)}) %collective-permute-start.18) | collective-permute-done | bytes 294944 | tf_op jit(solution)/shard_map/ppermute | solution.py:380
  101.0 0.7 collective-permute-done.19.refs_2_
  101.7 1.0 merge.1
  102.7 0.6 all-to-all-done.1.second_ref
  103.4 2.9 %place.1 = (bf16[256,32,128]{2,1,0:T(8,128)(2,1)}, s32[1]{0:T(128)}) custom-call(bf16[32,3,32,128]{3,2,1,0:T(8,128)(2,1)S(1)} %all-to-all-done.first_ref, bf16[32,5,32,128]{3,2,1,0:T(8,128)(2,1)S(1)} %all-to-all-done.1.second_ref), custom_call_target="tpu_custom_call" | custom-call | bytes 10485760 | tf_op jit(solution)/shard_map/place/pallas_call | solution.py:138
  (26 shorter events, 0.1 us)
Async XLA Ops:
  0.6 21.1 %copy-start.9 = (bf16[256,512]{1,0:T(8,128)(2,1)S(1)}, bf16[256,512]{1,0:T(8,128)(2,1)}, u32[]{:S(2)}) copy-start(bf16[256,512]{1,0:T(8,128)(2,1)} %refs_0_.1) | copy-start | bytes 786436
  0.6 8.3 %collective-permute-start = (bf16[256,512]{1,0:T(8,128)(2,1)}, bf16[256,512]{1,0:T(8,128)(2,1)S(1)}, u32[]{:S(2)}, u32[]{:S(2)}) collective-permute-start(bf16[256,512]{1,0:T(8,128)(2,1)} %refs_0_.1), channel_id=1, source_target_pairs={{0,2},{1,3},{2,4},{3,5},{4,6},{5,7},{6,0},{7,1},{8,10},{9,11},{10,... | collective-permute-start | bytes 786440 | tf_op jit(solution)/shard_map/ppermute | solution.py:372
  2.2 8.0 %collective-permute-start.1 = (bf16[256,512]{1,0:T(8,128)(2,1)}, bf16[256,512]{1,0:T(8,128)(2,1)S(1)}, u32[]{:S(2)}, u32[]{:S(2)}) collective-permute-start(bf16[256,512]{1,0:T(8,128)(2,1)} %refs_0_.1), channel_id=1, source_target_pairs={{0,6},{1,7},{2,0},{3,1},{4,2},{5,3},{6,4},{7,5},{8,14},{9,15},{10,... | collective-permute-start | bytes 786440 | tf_op jit(solution)/shard_map/ppermute | solution.py:372
  3.1 20.0 %copy-start.6 = (s32[32]{0:T(128)S(1)}, s32[32]{0:T(128)}, u32[]{:S(2)}) copy-start(s32[32]{0:T(128)} %span_ref.5) | copy-start | bytes 388
  3.1 20.7 %copy-start.15 = (bf16[4096]{0:T(1024)(128)(2,1)S(1)}, bf16[4096]{0:T(1024)(128)(2,1)}, u32[]{:S(2)}) copy-start(bf16[4096]{0:T(1024)(128)(2,1)} %param.7) | copy-start | bytes 24580
  9.0 20.9 %copy-start.7 = (bf16[256,512]{1,0:T(8,128)(2,1)}, bf16[256,512]{1,0:T(8,128)(2,1)S(1)}, u32[]{:S(2)}) copy-start(bf16[256,512]{1,0:T(8,128)(2,1)S(1)} %collective-permute-done.refs_1_) | copy-start | bytes 786436
  10.2 19.7 %copy-start.8 = (bf16[256,512]{1,0:T(8,128)(2,1)}, bf16[256,512]{1,0:T(8,128)(2,1)S(1)}, u32[]{:S(2)}) copy-start(bf16[256,512]{1,0:T(8,128)(2,1)S(1)} %collective-permute-done.1.refs_2_) | copy-start | bytes 786436
  10.2 54.2 %all-to-all-start = ((bf16[32,3,32,128]{3,2,1,0:T(8,128)(2,1)}), bf16[32,3,32,128]{3,2,1,0:T(8,128)(2,1)S(1)}, u32[]{:S(2)}, u32[]{:S(2)}) async-start(bf16[32,3,32,128]{3,2,1,0:T(8,128)(2,1)} %get-tuple-element.50), calls=%async_computation | async-start | bytes 1572864 | tf_op jit(solution)/shard_map/all_to_all | solution.py:392
  21.7 8.0 %collective-permute-start.3 = (bf16[256,512]{1,0:T(8,128)(2,1)S(1)}, bf16[256,512]{1,0:T(8,128)(2,1)S(1)}, u32[]{:S(2)}, u32[]{:S(2)}) collective-permute-start(bf16[256,512]{1,0:T(8,128)(2,1)S(1)} %copy-done.9), channel_id=1, source_target_pairs={{0,1},{1,0},{2,3},{3,2},{4,5},{5,4},{6,7},{7,6},{8,9},{9,8},{10,11... | collective-permute-start | bytes 786440 | tf_op jit(solution)/shard_map/ppermute | solution.py:376
  21.8 6.4 %collective-permute-start.2 = (bf16[256,512]{1,0:T(8,128)(2,1)S(1)}, bf16[256,512]{1,0:T(8,128)(2,1)S(1)}, u32[]{:S(2)}, u32[]{:S(2)}) collective-permute-start(bf16[256,512]{1,0:T(8,128)(2,1)S(1)} %broadcast_select_fusion), channel_id=1, source_target_pairs={{0,2},{1,7},{2,4},{3,1},{4,6},{5,3},{6,0},{7,5},{8,10},{9,15},{10,... | collective-permute-start | bytes 786440 | tf_op jit(solution)/shard_map/ppermute | solution.py:404
  25.1 4.6 %collective-permute-start.4 = (bf16[256,512]{1,0:T(8,128)(2,1)S(1)}, bf16[256,512]{1,0:T(8,128)(2,1)S(1)}, u32[]{:S(2)}, u32[]{:S(2)}) collective-permute-start(bf16[256,512]{1,0:T(8,128)(2,1)S(1)} %collective-permute-done.refs_1_), channel_id=1, source_target_pairs={{0,1},{1,0},{2,3},{3,2},{4,5},{5,4},{6,7},{7,6},{8,9},{9,8},{10,11... | collective-permute-start | bytes 786440 | tf_op jit(solution)/shard_map/ppermute | solution.py:376
  25.2 4.6 %collective-permute-start.5 = (bf16[256,512]{1,0:T(8,128)(2,1)S(1)}, bf16[256,512]{1,0:T(8,128)(2,1)S(1)}, u32[]{:S(2)}, u32[]{:S(2)}) collective-permute-start(bf16[256,512]{1,0:T(8,128)(2,1)S(1)} %collective-permute-done.1.refs_2_), channel_id=1, source_target_pairs={{0,1},{1,0},{2,3},{3,2},{4,5},{5,4},{6,7},{7,6},{8,9},{9,8},{10,11... | collective-permute-start | bytes 786440 | tf_op jit(solution)/shard_map/ppermute | solution.py:376
  28.3 1.5 %copy-start.11 = (bf16[256,512]{1,0:T(8,128)(2,1)}, bf16[256,512]{1,0:T(8,128)(2,1)S(1)}, u32[]{:S(2)}) copy-start(bf16[256,512]{1,0:T(8,128)(2,1)S(1)} %collective-permute-done.2.refs_3_) | copy-start | bytes 786436
  28.3 1.5 %collective-permute-start.6 = (bf16[256,512]{1,0:T(8,128)(2,1)S(1)}, bf16[256,512]{1,0:T(8,128)(2,1)S(1)}, u32[]{:S(2)}, u32[]{:S(2)}) collective-permute-start(bf16[256,512]{1,0:T(8,128)(2,1)S(1)} %collective-permute-done.2.refs_3_), channel_id=1, source_target_pairs={{0,1},{1,0},{2,3},{3,2},{4,5},{5,4},{6,7},{7,6},{8,9},{9,8},{10,11... | collective-permute-start | bytes 786440 | tf_op jit(solution)/shard_map/ppermute | solution.py:376
  29.7 0.7 copy-start.10
  29.7 0.8 copy-start.12
  29.7 0.9 copy-start.13
  29.8 0.8 copy-start.14
  38.0 34.5 %copy-start = (bf16[256,256]{1,0:T(8,128)(2,1)S(1)}, bf16[256,256]{1,0:T(8,128)(2,1)}, u32[]{:S(2)}) copy-start(bf16[256,256]{1,0:T(8,128)(2,1)} %get-tuple-element.36.refs_1_.refs_2_) | copy-start | bytes 393220
  38.0 6.8 %collective-permute-start.10 = (bf16[256,256]{1,0:T(8,128)(2,1)}, bf16[256,256]{1,0:T(8,128)(2,1)S(1)}, u32[]{:S(2)}, u32[]{:S(2)}) collective-permute-start(bf16[256,256]{1,0:T(8,128)(2,1)} %get-tuple-element.36.refs_1_.refs_2_), channel_id=1, source_target_pairs={{0,56},{8,0},{16,8},{24,16},{32,24},{40,32},{48,40},{56,48},{64,12... | collective-permute-start | bytes 393224 | tf_op jit(solution)/shard_map/ppermute | solution.py:386
  41.0 13.7 %collective-permute-start.15 = (bf16[128,1024]{1,0:T(8,128)(2,1)}, bf16[128,1024]{1,0:T(8,128)(2,1)S(1)}, u32[]{:S(2)}, u32[]{:S(2)}) collective-permute-start(bf16[128,1024]{1,0:T(8,128)(2,1)} %get-tuple-element.48.refs_0_), channel_id=1, source_target_pairs={{0,192},{8,200},{16,208},{24,216},{32,224},{40,232},{48,240},{56,2... | collective-permute-start | bytes 786440 | tf_op jit(solution)/shard_map/ppermute | solution.py:380
  43.8 6.8 %collective-permute-start.7 = (bf16[256,256]{1,0:T(8,128)(2,1)}, bf16[256,256]{1,0:T(8,128)(2,1)S(1)}, u32[]{:S(2)}, u32[]{:S(2)}) collective-permute-start(bf16[256,256]{1,0:T(8,128)(2,1)} %get-tuple-element.36.refs_1_.refs_2_), channel_id=1, source_target_pairs={{0,8},{8,16},{16,24},{24,32},{32,40},{40,48},{48,56},{56,0},{64,72... | collective-permute-start | bytes 393224 | tf_op jit(solution)/shard_map/ppermute | solution.py:386
  44.8 6.2 %collective-permute-start.11 = (bf16[256,256]{1,0:T(8,128)(2,1)S(1)}, bf16[256,256]{1,0:T(8,128)(2,1)S(1)}, u32[]{:S(2)}, u32[]{:S(2)}) collective-permute-start(bf16[256,256]{1,0:T(8,128)(2,1)S(1)} %collective-permute-done.10.refs_5_.refs_6_), channel_id=1, source_target_pairs={{0,56},{8,0},{16,8},{24,16},{32,24},{40,32},{48,40},{56,48},{64,12... | collective-permute-start | bytes 393224 | tf_op jit(solution)/shard_map/ppermute | solution.py:386
  48.4 12.5 %collective-permute-start.14 = (bf16[128,1024]{1,0:T(8,128)(2,1)}, bf16[128,1024]{1,0:T(8,128)(2,1)S(1)}, u32[]{:S(2)}, u32[]{:S(2)}) collective-permute-start(bf16[128,1024]{1,0:T(8,128)(2,1)} %get-tuple-element.48.refs_0_), channel_id=1, source_target_pairs={{0,64},{8,72},{16,80},{24,88},{32,96},{40,104},{48,112},{56,120},{... | collective-permute-start | bytes 786440 | tf_op jit(solution)/shard_map/ppermute | solution.py:380
  50.6 6.9 %collective-permute-start.8 = (bf16[256,256]{1,0:T(8,128)(2,1)S(1)}, bf16[256,256]{1,0:T(8,128)(2,1)S(1)}, u32[]{:S(2)}, u32[]{:S(2)}) collective-permute-start(bf16[256,256]{1,0:T(8,128)(2,1)S(1)} %collective-permute-done.7.refs_2_.refs_3_), channel_id=1, source_target_pairs={{0,8},{8,16},{16,24},{24,32},{32,40},{40,48},{48,56},{56,0},{64,72... | collective-permute-start | bytes 393224 | tf_op jit(solution)/shard_map/ppermute | solution.py:386
  51.0 6.5 %collective-permute-start.12 = (bf16[256,256]{1,0:T(8,128)(2,1)S(1)}, bf16[256,256]{1,0:T(8,128)(2,1)S(1)}, u32[]{:S(2)}, u32[]{:S(2)}) collective-permute-start(bf16[256,256]{1,0:T(8,128)(2,1)S(1)} %collective-permute-done.11.refs_6_.refs_7_), channel_id=1, source_target_pairs={{0,56},{8,0},{16,8},{24,16},{32,24},{40,32},{48,40},{56,48},{64,12... | collective-permute-start | bytes 393224 | tf_op jit(solution)/shard_map/ppermute | solution.py:386
  54.7 9.0 %collective-permute-start.16 = (bf16[128,1024]{1,0:T(8,128)(2,1)S(1)}, bf16[128,1024]{1,0:T(8,128)(2,1)S(1)}, u32[]{:S(2)}, u32[]{:S(2)}) collective-permute-start(bf16[128,1024]{1,0:T(8,128)(2,1)S(1)} %collective-permute-done.15.refs_1_), channel_id=1, source_target_pairs={{0,192},{8,200},{16,208},{24,216},{32,224},{40,232},{48,240},{56,2... | collective-permute-start | bytes 786440 | tf_op jit(solution)/shard_map/ppermute | solution.py:380
  57.5 6.2 %collective-permute-start.9 = (bf16[256,256]{1,0:T(8,128)(2,1)S(1)}, bf16[256,256]{1,0:T(8,128)(2,1)S(1)}, u32[]{:S(2)}, u32[]{:S(2)}) collective-permute-start(bf16[256,256]{1,0:T(8,128)(2,1)S(1)} %collective-permute-done.8.refs_3_.refs_4_), channel_id=1, source_target_pairs={{0,8},{8,16},{16,24},{24,32},{32,40},{40,48},{48,56},{56,0},{64,72... | collective-permute-start | bytes 393224 | tf_op jit(solution)/shard_map/ppermute | solution.py:386
  57.5 6.2 %collective-permute-start.13 = (bf16[256,256]{1,0:T(8,128)(2,1)S(1)}, bf16[256,256]{1,0:T(8,128)(2,1)S(1)}, u32[]{:S(2)}, u32[]{:S(2)}) collective-permute-start(bf16[256,256]{1,0:T(8,128)(2,1)S(1)} %collective-permute-done.12.refs_7_.refs_8_), channel_id=1, source_target_pairs={{0,56},{8,0},{16,8},{24,16},{32,24},{40,32},{48,40},{56,48},{64,12... | collective-permute-start | bytes 393224 | tf_op jit(solution)/shard_map/ppermute | solution.py:386
  60.9 0.7 copy-start.2
  63.7 0.7 copy-start.4
  64.4 39.0 %all-to-all-start.1 = ((bf16[32,5,32,128]{3,2,1,0:T(8,128)(2,1)}), bf16[32,5,32,128]{3,2,1,0:T(8,128)(2,1)S(1)}, u32[]{:S(2)}, u32[]{:S(2)}) async-start(bf16[32,5,32,128]{3,2,1,0:T(8,128)(2,1)} %get-tuple-element.51), calls=%async_computation.1 | async-start | bytes 2621440 | tf_op jit(solution)/shard_map/all_to_all | solution.py:392
  72.5 1.0 copy-start.5
  73.4 15.4 %copy-start.1 = (bf16[128,1024]{1,0:T(8,128)(2,1)S(1)}, bf16[128,1024]{1,0:T(8,128)(2,1)}, u32[]{:S(2)}) copy-start(bf16[128,1024]{1,0:T(8,128)(2,1)} %get-tuple-element.48.refs_0_) | copy-start | bytes 786436
  76.1 19.2 %collective-permute-start.17 = (bf16[144,1024]{1,0:T(8,128)(2,1)S(1)}, bf16[144,1024]{1,0:T(8,128)(2,1)S(1)}, u32[]{:S(2)}, u32[]{:S(2)}) collective-permute-start(bf16[144,1024]{1,0:T(8,128)(2,1)S(1)} %attend.3), channel_id=1, source_target_pairs={{0,128},{8,136},{16,144},{24,152},{32,160},{40,168},{48,176},{56,1... | collective-permute-start | bytes 884744 | tf_op jit(solution)/shard_map/ppermute | solution.py:380
  81.6 0.9 copy-start.3
  86.4 14.6 %collective-permute-start.18 = (bf16[144,1024]{1,0:T(8,128)(2,1)S(1)}, bf16[144,1024]{1,0:T(8,128)(2,1)S(1)}, u32[]{:S(2)}, u32[]{:S(2)}) collective-permute-start(bf16[144,1024]{1,0:T(8,128)(2,1)S(1)} %get-tuple-element.46), channel_id=1, source_target_pairs={{0,192},{8,200},{16,208},{24,216},{32,224},{40,232},{48,240},{56,2... | collective-permute-start | bytes 884744 | tf_op jit(solution)/shard_map/ppermute | solution.py:380
  87.5 14.3 %collective-permute-start.19 = (bf16[144,1024]{1,0:T(8,128)(2,1)S(1)}, bf16[144,1024]{1,0:T(8,128)(2,1)S(1)}, u32[]{:S(2)}, u32[]{:S(2)}) collective-permute-start(bf16[144,1024]{1,0:T(8,128)(2,1)S(1)} %get-tuple-element.47), channel_id=1, source_target_pairs={{0,64},{8,72},{16,80},{24,88},{32,96},{40,104},{48,112},{56,120},{... | collective-permute-start | bytes 884744 | tf_op jit(solution)/shard_map/ppermute | solution.py:380
where the time goes:
time: 108 us; the launch traced here: 106 us
  starting transfers between devices  52.5 us (49%)
  Pallas kernels  26.2 us (24%)
  waiting for transfers between devices  19.2 us (18%)
  local copies, waits for them, and re-layouts  4.78 us (4%)
  other arithmetic  2.06 us (2%)
  between operations  1.65 us (2%)
    all_to_all x2, starting transfers between devices, to_owners(): return lax.all_to_all(value, 'ctx', split_axis=0, concat_axis=0, tiled=True)  19.6 us
    ppermute x6, starting transfers between devices, along_y(): lax.ppermute(value, 'ctx', [(i, (i // NZ + step) % NY * NZ + i % NZ) for...  14.8 us
    ppermute x7, starting transfers between devices, along_z(): lax.ppermute(value, 'ctx', [(i, i // NZ * NZ + (i % NZ + step) % NZ) for...  13.8 us
    pallas_call x3, Pallas kernels, attend(): pl.pallas_call(functools.partial(attend_kernel, steps), out_shape=(part,)...  10.8 us
    ppermute x6, waiting for transfers between devices, along_y(): lax.ppermute(value, 'ctx', [(i, (i // NZ + step) % NY * NZ + i % NZ) for...  8.67 us
    pallas_call x1, Pallas kernels, project(): pl.pallas_call(project_kernel, out_shape=(jax.ShapeDtypeStruct((HD, ROWS)...  7.27 us
    ppermute x7, waiting for transfers between devices, along_z(): lax.ppermute(value, 'ctx', [(i, i // NZ * NZ + (i % NZ + step) % NZ) for...  4.22 us
    pallas_call x1, Pallas kernels, bucket(): pl.pallas_call(bucket_kernel, out_shape=tuple((jax.ShapeDtypeStruct((N_CT...  4.18 us
  transfers between devices with their start and end apart: 22, of which 12 were waited for; matrix products, arithmetic and copies ran while one was open for 3% of the time, Pallas kernels for 22%

commit v1 on v0

--- a/solution.py
+++ b/solution.py
@@ -15,7 +15,7 @@
 NZ = 8
 N_CTX = NY * NZ
 OWN_CAP = N_CTX * SEND_CAP
-FIRST = 3
+FIRST = 4
 SECOND = SEND_CAP - FIRST
 D = 4096
 ROWS = GQ * SPAN
@@ -181,9 +181,12 @@
         normed = block[...].astype(jnp.float32) * inverse * gain
         start = pl.multiple_of(index * width, width)
         normed_ref[:, pl.ds(start, width)] = normed.astype(jnp.bfloat16)
-    for load in loads:
-        load.wait()
-    projected = jnp.dot(normed_ref[...], w_ref[...], preferred_element_type=jnp.float32)
+    projected = jnp.zeros((SPAN, w_ref.shape[1]), jnp.float32)
+    for at in range(0, 8, 2):
+        loads[at].wait()
+        loads[at + 1].wait()
+        part = slice(at * width, (at + 2) * width)
+        projected += jnp.dot(normed_ref[:, part], w_ref[part], preferred_element_type=jnp.float32)
     cosine = cos_ref[...]
     sine = sin_ref[...]
 
@@ -281,13 +284,18 @@
             list_ref[earlier] = part
             earlier = earlier + (key_span < query_span).astype(jnp.int32)
 
-        def step(pair, carry):
-            update([list_ref[2 * pair], list_ref[2 * pair + 1]], False)
+        def step(group, carry):
+            update([list_ref[4 * group + at] for at in range(4)], False)
             return carry
 
-        lax.fori_loop(0, earlier // 2, step, 0)
-
-        @pl.when(earlier % 2 == 1)
+        lax.fori_loop(0, earlier // 4, step, 0)
+        rest = earlier % 4
+
+        @pl.when(rest >= 2)
+        def _():
+            update([list_ref[earlier - rest + at] for at in range(2)], False)
+
+        @pl.when(rest % 2 == 1)
         def _():
             update([list_ref[earlier - 1]], False)
 
@@ -361,11 +369,11 @@
 
 def rotation(positions):
     half_dim = HD // 2
-    inv_freq = ROPE_BASE ** (-(2 * jnp.arange(half_dim)).astype(jnp.float32) / HD)
+    lane = jnp.arange(HD)
+    inv_freq = ROPE_BASE ** (-(2 * (lane % half_dim)).astype(jnp.float32) / HD)
     angles = positions.astype(jnp.float32)[:, None] * inv_freq[None, :]
-    cosine = jnp.cos(angles)
     sine = jnp.sin(angles)
-    return jnp.concatenate([cosine, cosine], axis=1), jnp.concatenate([-sine, sine], axis=1)
+    return jnp.cos(angles), jnp.where(lane[None, :] < half_dim, -sine, sine)
 
 
 def along_x(value, step):
@@ -394,24 +402,18 @@
 
 def shards(front_hidden, norm_gain, w_qkv, block_span, back_pages, page_dest):
     my_index = lax.axis_index("ctx")
-    my_core = lax.axis_index("kvh") % 2
 
     first, second = bucket(page_dest, back_pages.reshape(OWN_CAP, PAGE_ROWS, HD))
-    low, high = along_x(front_hidden, 1), along_x(front_hidden, -1)
-    first, low, high = lax.optimization_barrier((first, low, high))
     first = to_owners(first)
-
-    opposite = lax.ppermute(
-        jnp.where(my_core == 0, low, high),
-        "kvh",
-        [(i, ((i // 2 + 1 - 2 * (i % 2)) % 4) * 2 + i % 2) for i in range(8)],
-    )
-    same = [front_hidden, low, high, opposite]
-    other = [across(block) for block in same]
 
     my_span = jnp.sum(jnp.where(jnp.arange(N_CTX) == my_index, block_span, 0))
     cosine, sine = rotation(my_span * SPAN + jnp.arange(SPAN))
     gain = norm_gain.astype(jnp.float32).reshape(8, D // 8)
+
+    same = [front_hidden] + [along_x(front_hidden, step) for step in STEPS_X[1:]]
+    held = lax.optimization_barrier((same[3], cosine, sine, gain))
+    same[3], cosine, sine, gain = held
+    other = [across(block) for block in same]
     query, cache, message = project(gain, cosine, sine, w_qkv, same + other)
 
     from_up = along_y(query, -1)

time: 108 us -> 106 us (0.981); the launches traced: 106 us -> 106 us
  Pallas kernels: 26.2 us -> 23.6 us
  starting transfers between devices: 52.5 us -> 53.8 us
    ppermute x2 -> x3, waiting for transfers between devices: 2.91 us -> 7.61 us  [along_x(): lax.ppermute(value, 'kvh', [(i, (i // 2 + step) % 4 * 2 + i % 2) for i in...]
    ppermute x1 -> x0, waiting for transfers between devices: 2.64 us -> none  [shards(): lax.ppermute(jnp.where(my_core == 0, low, high), 'kvh', [(i, (i // 2 + 1...]
    pallas_call x3, Pallas kernels: 10.8 us -> 8.75 us  [attend(): pl.pallas_call(functools.partial(attend_kernel, steps), out_shape=(part,)...]
    ppermute x6, waiting for transfers between devices: 8.67 us -> 6.84 us  [along_y(): lax.ppermute(value, 'ctx', [(i, (i // NZ + step) % NY * NZ + i % NZ) for...]
    ppermute x2 -> x3, starting transfers between devices: 2.44 us -> 4.24 us  [along_x(): lax.ppermute(value, 'kvh', [(i, (i // 2 + step) % 4 * 2 + i % 2) for i in...]
    ppermute x4, waiting for transfers between devices: 0.11 us -> 1.66 us  [across(): return lax.ppermute(value, 'kvh', [(i, i ^ 1) for i in range(8)])]
    ppermute x1 -> x0, starting transfers between devices: 1.27 us -> none  [shards(): lax.ppermute(jnp.where(my_core == 0, low, high), 'kvh', [(i, (i // 2 + 1...]
    select_n x1, other arithmetic: 0.03 us -> 1.25 us  [rotation(): return (jnp.cos(angles), jnp.where(lane[None, :] < half_dim, -sine, sine))]
  transfers between devices with their start and end apart: 22 -> 22, of which waited for: 12 -> 12; matrix products, arithmetic and copies ran while one was open for 3% -> 2% of each run, Pallas kernels for 22% -> 16%
where the time goes in v1:
time: 106 us
  starting transfers between devices  53.8 us (51%)
  Pallas kernels  23.6 us (22%)
  waiting for transfers between devices  19.8 us (19%)
  local copies, waits for them, and re-layouts  4.98 us (5%)
  other arithmetic  1.9 us (2%)
  between operations  1.67 us (2%)
    all_to_all x2, starting transfers between devices, to_owners(): return lax.all_to_all(value, 'ctx', split_axis=0, concat_axis=0, tiled=True)  19.6 us
    ppermute x6, starting transfers between devices, along_y(): lax.ppermute(value, 'ctx', [(i, (i // NZ + step) % NY * NZ + i % NZ) for...  15.9 us
    ppermute x7, starting transfers between devices, along_z(): lax.ppermute(value, 'ctx', [(i, i // NZ * NZ + (i % NZ + step) % NZ) for...  13.4 us
    pallas_call x3, Pallas kernels, attend(): pl.pallas_call(functools.partial(attend_kernel, steps), out_shape=(part,)...  8.75 us
    ppermute x3, waiting for transfers between devices, along_x(): lax.ppermute(value, 'kvh', [(i, (i // 2 + step) % 4 * 2 + i % 2) for i in...  7.61 us
    ppermute x6, waiting for transfers between devices, along_y(): lax.ppermute(value, 'ctx', [(i, (i // NZ + step) % NY * NZ + i % NZ) for...  6.84 us
    pallas_call x1, Pallas kernels, project(): pl.pallas_call(project_kernel, out_shape=(jax.ShapeDtypeStruct((HD, ROWS)...  6.75 us
    unnamed x32, local copies, waits for them, and re-layouts  4.36 us
  transfers between devices with their start and end apart: 22, of which 12 were waited for; matrix products, arithmetic and copies ran while one was open for 2% of the time, Pallas kernels for 16%

profile of v1, /device:TPU:2, one launch (start us, length us, event | category | flops | bytes accessed | tf_op | source)
XLA Modules:
  0.0 105.8 jit_solution(12864091162846713985)
XLA Ops:
  0.6 0.0 copy-start.7
  0.7 4.2 %bucket.1 = (bf16[32,4,32,128]{3,2,1,0:T(8,128)(2,1)}, bf16[32,4,32,128]{3,2,1,0:T(8,128)(2,1)}) custom-call(s32[256]{0:T(256)} %dest_hbm.1, bf16[256,32,128]{2,1,0:T(8,128)(2,1)} %bitcast.5), custom_call_target="tpu_custom_call" | custom-call | bytes 18874368 | tf_op jit(solution)/shard_map/bucket/pallas_call | solution.py:87
  4.9 11.5 %all-to-all-start = ((bf16[32,4,32,128]{3,2,1,0:T(8,128)(2,1)}), bf16[32,4,32,128]{3,2,1,0:T(8,128)(2,1)S(1)}, u32[]{:S(2)}, u32[]{:S(2)}) async-start(bf16[32,4,32,128]{3,2,1,0:T(8,128)(2,1)} %get-tuple-element.52), calls=%async_computation | async-start | bytes 2097152 | tf_op jit(solution)/shard_map/all_to_all | solution.py:400
  16.4 2.2 %collective-permute-start = (bf16[256,512]{1,0:T(8,128)(2,1)S(1)}, bf16[256,512]{1,0:T(8,128)(2,1)S(1)}, u32[]{:S(2)}, u32[]{:S(2)}) collective-permute-start(bf16[256,512]{1,0:T(8,128)(2,1)S(1)} %copy-done.7), channel_id=1, source_target_pairs={{0,4},{1,5},{2,6},{3,7},{4,0},{5,1},{6,2},{7,3},{8,12},{9,13},{10,... | collective-permute-start | bytes 786440 | tf_op jit(solution)/shard_map/ppermute | solution.py:380
  18.6 0.0 collective-permute-start.1
  18.6 2.0 %collective-permute-start.2 = (bf16[256,512]{1,0:T(8,128)(2,1)S(1)}, bf16[256,512]{1,0:T(8,128)(2,1)S(1)}, u32[]{:S(2)}, u32[]{:S(2)}) collective-permute-start(bf16[256,512]{1,0:T(8,128)(2,1)S(1)} %copy-done.7), channel_id=1, source_target_pairs={{0,6},{1,7},{2,0},{3,1},{4,2},{5,3},{6,4},{7,5},{8,14},{9,15},{10,... | collective-permute-start | bytes 786440 | tf_op jit(solution)/shard_map/ppermute | solution.py:380
  20.6 0.0 collective-permute-start.3
  20.6 0.6 fusion
  22.0 0.0 copy-done.15
  22.0 0.6 reshape.53.gain_ref
  22.6 1.2 %negate_select_fusion = (f32[256,128]{1,0:T(8,128)}, f32[256,128]{1,0:T(8,128)}) fusion(f32[128]{0:T(128)S(1)} %fusion.5, f32[256]{0:T(256)S(1)} %add_convert_fusion, pred[128]{0:T(512)(128)(4,1)S(1)} %iota_compare_fusion), kind=kLoop, calls=%fused_computation | loop fusion | flops 98304 | bytes 263808 | tf_op jit(solution)/shard_map/jit(_where)/select_n | solution.py:376
  23.8 3.4 %collective-permute-done.refs_3_ = bf16[256,512]{1,0:T(8,128)(2,1)S(1)} collective-permute-done((bf16[256,512]{1,0:T(8,128)(2,1)S(1)}, bf16[256,512]{1,0:T(8,128)(2,1)S(1)}, u32[]{:S(2)}, u32[]{:S(2)}) %collective-permute-start) | collective-permute-done | bytes 262176 | tf_op jit(solution)/shard_map/ppermute | solution.py:380
  27.3 4.2 %collective-permute-done.1.refs_1_ = bf16[256,512]{1,0:T(8,128)(2,1)S(1)} collective-permute-done((bf16[256,512]{1,0:T(8,128)(2,1)S(1)}, bf16[256,512]{1,0:T(8,128)(2,1)S(1)}, u32[]{:S(2)}, u32[]{:S(2)}) %collective-permute-start.1) | collective-permute-done | bytes 262176 | tf_op jit(solution)/shard_map/ppermute | solution.py:380
  31.5 0.0 collective-permute-start.4
  31.5 0.0 collective-permute-done.2.refs_2_
  31.5 0.0 copy-start.10
  31.5 0.5 collective-permute-start.5
  32.0 0.1 collective-permute-start.6
  32.1 0.0 collective-permute-done.3.refs_4_
  32.1 0.9 collective-permute-done.4.refs_5_
  33.0 0.4 collective-permute-done.5.refs_6_
  33.4 0.4 collective-permute-done.6.refs_7_
  33.8 0.3 copy-done.13
  34.1 0.7 copy-done.14
  34.8 6.7 %project.1 = (bf16[128,1024]{1,0:T(8,128)(2,1)}, bf16[256,256]{1,0:T(8,128)(2,1)}, bf16[256,256]{1,0:T(8,128)(2,1)}) custom-call(f32[8,512]{1,0:T(8,128)} %reshape.53.gain_ref, f32[256,128]{1,0:T(8,128)} %get-tuple-element.32.cos_ref, f32[256,128]{1,0:T(8,128)} %get-tuple-element.33.sin_ref, bf16[4096,768]{1,0:T(8,128)(2,1)} %w_hbm.1, ...), custom_call_target="tpu_custom_call" | custom-call | bytes 16777216 | tf_op jit(solution)/shard_map/project/pallas_call | solution.py:209
  41.5 2.8 %collective-permute-start.10 = (bf16[256,256]{1,0:T(8,128)(2,1)}, bf16[256,256]{1,0:T(8,128)(2,1)S(1)}, u32[]{:S(2)}, u32[]{:S(2)}) collective-permute-start(bf16[256,256]{1,0:T(8,128)(2,1)} %get-tuple-element.38.refs_1_.refs_2_), channel_id=1, source_target_pairs={{0,56},{8,0},{16,8},{24,16},{32,24},{40,32},{48,40},{56,48},{64,12... | collective-permute-start | bytes 393224 | tf_op jit(solution)/shard_map/ppermute | solution.py:394
  44.3 2.8 %collective-permute-start.15 = (bf16[128,1024]{1,0:T(8,128)(2,1)}, bf16[128,1024]{1,0:T(8,128)(2,1)S(1)}, u32[]{:S(2)}, u32[]{:S(2)}) collective-permute-start(bf16[128,1024]{1,0:T(8,128)(2,1)} %get-tuple-element.50.refs_0_), channel_id=1, source_target_pairs={{0,192},{8,200},{16,208},{24,216},{32,224},{40,232},{48,240},{56,2... | collective-permute-start | bytes 786440 | tf_op jit(solution)/shard_map/ppermute | solution.py:388
  47.1 0.0 collective-permute-start.7
  47.1 0.6 collective-permute-done.10.refs_5_.refs_6_
  47.7 3.6 %collective-permute-start.11 = (bf16[256,256]{1,0:T(8,128)(2,1)S(1)}, bf16[256,256]{1,0:T(8,128)(2,1)S(1)}, u32[]{:S(2)}, u32[]{:S(2)}) collective-permute-start(bf16[256,256]{1,0:T(8,128)(2,1)S(1)} %collective-permute-done.10.refs_5_.refs_6_), channel_id=1, source_target_pairs={{0,56},{8,0},{16,8},{24,16},{32,24},{40,32},{48,40},{56,48},{64,12... | collective-permute-start | bytes 393224 | tf_op jit(solution)/shard_map/ppermute | solution.py:394
  51.3 1.5 %collective-permute-start.14 = (bf16[128,1024]{1,0:T(8,128)(2,1)}, bf16[128,1024]{1,0:T(8,128)(2,1)S(1)}, u32[]{:S(2)}, u32[]{:S(2)}) collective-permute-start(bf16[128,1024]{1,0:T(8,128)(2,1)} %get-tuple-element.50.refs_0_), channel_id=1, source_target_pairs={{0,64},{8,72},{16,80},{24,88},{32,96},{40,104},{48,112},{56,120},{... | collective-permute-start | bytes 786440 | tf_op jit(solution)/shard_map/ppermute | solution.py:388
  52.8 0.7 collective-permute-done.7.refs_2_.refs_3_
  53.5 0.0 collective-permute-start.8
  53.5 0.3 collective-permute-done.11.refs_6_.refs_7_
  53.8 3.7 %collective-permute-start.12 = (bf16[256,256]{1,0:T(8,128)(2,1)S(1)}, bf16[256,256]{1,0:T(8,128)(2,1)S(1)}, u32[]{:S(2)}, u32[]{:S(2)}) collective-permute-start(bf16[256,256]{1,0:T(8,128)(2,1)S(1)} %collective-permute-done.11.refs_6_.refs_7_), channel_id=1, source_target_pairs={{0,56},{8,0},{16,8},{24,16},{32,24},{40,32},{48,40},{56,48},{64,12... | collective-permute-start | bytes 393224 | tf_op jit(solution)/shard_map/ppermute | solution.py:394
  57.5 0.0 collective-permute-done.15.refs_1_
  57.5 2.8 %collective-permute-start.16 = (bf16[128,1024]{1,0:T(8,128)(2,1)S(1)}, bf16[128,1024]{1,0:T(8,128)(2,1)S(1)}, u32[]{:S(2)}, u32[]{:S(2)}) collective-permute-start(bf16[128,1024]{1,0:T(8,128)(2,1)S(1)} %collective-permute-done.15.refs_1_), channel_id=1, source_target_pairs={{0,192},{8,200},{16,208},{24,216},{32,224},{40,232},{48,240},{56,2... | collective-permute-start | bytes 786440 | tf_op jit(solution)/shard_map/ppermute | solution.py:388
  60.3 0.0 collective-permute-done.8.refs_3_.refs_4_
  60.3 0.0 collective-permute-start.9
  60.3 0.0 collective-permute-done.12.refs_7_.refs_8_
  60.3 3.4 %collective-permute-start.13 = (bf16[256,256]{1,0:T(8,128)(2,1)S(1)}, bf16[256,256]{1,0:T(8,128)(2,1)S(1)}, u32[]{:S(2)}, u32[]{:S(2)}) collective-permute-start(bf16[256,256]{1,0:T(8,128)(2,1)S(1)} %collective-permute-done.12.refs_7_.refs_8_), channel_id=1, source_target_pairs={{0,56},{8,0},{16,8},{24,16},{32,24},{40,32},{48,40},{56,48},{64,12... | collective-permute-start | bytes 393224 | tf_op jit(solution)/shard_map/ppermute | solution.py:394
  63.7 0.0 collective-permute-done.14.refs_0_
  63.7 0.7 copy-done.2
  64.4 2.0 %collective-permute-done.9.refs_4_.refs_5_ = bf16[256,256]{1,0:T(8,128)(2,1)S(1)} collective-permute-done((bf16[256,256]{1,0:T(8,128)(2,1)S(1)}, bf16[256,256]{1,0:T(8,128)(2,1)S(1)}, u32[]{:S(2)}, u32[]{:S(2)}) %collective-permute-start.9) | collective-permute-done | bytes 131104 | tf_op jit(solution)/shard_map/ppermute | solution.py:394
  66.4 0.0 collective-permute-done.13.refs_8_.refs_9_
  66.4 0.0 collective-permute-done.16.refs_0_
  66.4 0.7 copy-done.4
  67.1 0.0 all-to-all-done.first_ref
  67.1 8.1 %all-to-all-start.1 = ((bf16[32,4,32,128]{3,2,1,0:T(8,128)(2,1)}), bf16[32,4,32,128]{3,2,1,0:T(8,128)(2,1)S(1)}, u32[]{:S(2)}, u32[]{:S(2)}) async-start(bf16[32,4,32,128]{3,2,1,0:T(8,128)(2,1)} %get-tuple-element.53), calls=%async_computation.1 | async-start | bytes 2097152 | tf_op jit(solution)/shard_map/all_to_all | solution.py:400
  75.2 0.0 copy-start.5
  75.2 0.9 copy-done.5
  76.2 0.7 attend.3
  76.9 6.8 %collective-permute-start.17 = (bf16[144,1024]{1,0:T(8,128)(2,1)S(1)}, bf16[144,1024]{1,0:T(8,128)(2,1)S(1)}, u32[]{:S(2)}, u32[]{:S(2)}) collective-permute-start(bf16[144,1024]{1,0:T(8,128)(2,1)S(1)} %attend.3), channel_id=1, source_target_pairs={{0,128},{8,136},{16,144},{24,152},{32,160},{40,168},{48,176},{56,1... | collective-permute-start | bytes 884744 | tf_op jit(solution)/shard_map/ppermute | solution.py:388
  83.8 0.9 copy-done.3
  84.7 3.4 %attend.4 = (bf16[144,1024]{1,0:T(8,128)(2,1)S(1)}, bf16[144,1024]{1,0:T(8,128)(2,1)S(1)}) custom-call(s32[32]{0:T(128)S(1)} %copy-done.6, bf16[128,1024]{1,0:T(8,128)(2,1)S(1)} %copy-done.3, bf16[128,1024]{1,0:T(8,128)(2,1)S(1)} %collective-permute-done.15.refs_1_, bf16[256,256]{1,0:T(8,128)(2,1)S(1)} %copy-done, ...), custom_call_target="tpu_custom_call" | custom-call | bytes 20971520 | tf_op jit(solution)/shard_map/attend/pallas_call | solution.py:318
  88.1 0.1 collective-permute-start.18
  88.2 2.0 %collective-permute-start.19 = (bf16[144,1024]{1,0:T(8,128)(2,1)S(1)}, bf16[144,1024]{1,0:T(8,128)(2,1)S(1)}, u32[]{:S(2)}, u32[]{:S(2)}) collective-permute-start(bf16[144,1024]{1,0:T(8,128)(2,1)S(1)} %get-tuple-element.49), channel_id=1, source_target_pairs={{0,64},{8,72},{16,80},{24,88},{32,96},{40,104},{48,112},{56,120},{... | collective-permute-start | bytes 884744 | tf_op jit(solution)/shard_map/ppermute | solution.py:388
  90.2 4.6 %attend.5.refs_3_ = bf16[144,1024]{1,0:T(8,128)(2,1)S(1)} custom-call(s32[32]{0:T(128)S(1)} %copy-done.6, bf16[128,1024]{1,0:T(8,128)(2,1)S(1)} %copy-done.1, bf16[256,256]{1,0:T(8,128)(2,1)S(1)} %copy-done, bf16[256,256]{1,0:T(8,128)(2,1)S(1)} %collective-permute-done.7.refs_2_.refs_3_, bf16[256,256]{1,0:T(8,128)(2,1)S(1)} %collective-permute-done.8.refs_3_.refs_4_, ...), custom_call_target="tpu_custom_call" | custom-call | bytes 10485760 | tf_op jit(solution)/shard_map/attend/pallas_call | solution.py:318
  94.8 2.4 %collective-permute-done.17.refs_0_ = bf16[144,1024]{1,0:T(8,128)(2,1)S(1)} collective-permute-done((bf16[144,1024]{1,0:T(8,128)(2,1)S(1)}, bf16[144,1024]{1,0:T(8,128)(2,1)S(1)}, u32[]{:S(2)}, u32[]{:S(2)}) %collective-permute-start.17) | collective-permute-done | bytes 294944 | tf_op jit(solution)/shard_map/ppermute | solution.py:388
  97.2 3.3 %collective-permute-done.18.refs_1_ = bf16[144,1024]{1,0:T(8,128)(2,1)S(1)} collective-permute-done((bf16[144,1024]{1,0:T(8,128)(2,1)S(1)}, bf16[144,1024]{1,0:T(8,128)(2,1)S(1)}, u32[]{:S(2)}, u32[]{:S(2)}) %collective-permute-start.18) | collective-permute-done | bytes 294944 | tf_op jit(solution)/shard_map/ppermute | solution.py:388
  100.5 1.2 %collective-permute-done.19.refs_2_ = bf16[144,1024]{1,0:T(8,128)(2,1)S(1)} collective-permute-done((bf16[144,1024]{1,0:T(8,128)(2,1)S(1)}, bf16[144,1024]{1,0:T(8,128)(2,1)S(1)}, u32[]{:S(2)}, u32[]{:S(2)}) %collective-permute-start.19) | collective-permute-done | bytes 294944 | tf_op jit(solution)/shard_map/ppermute | solution.py:388
  101.7 1.0 merge.1
  102.7 0.0 all-to-all-done.1.second_ref
  102.7 2.9 %place.1 = (bf16[256,32,128]{2,1,0:T(8,128)(2,1)}, s32[1]{0:T(128)}) custom-call(bf16[32,4,32,128]{3,2,1,0:T(8,128)(2,1)S(1)} %all-to-all-done.first_ref, bf16[32,4,32,128]{3,2,1,0:T(8,128)(2,1)S(1)} %all-to-all-done.1.second_ref), custom_call_target="tpu_custom_call" | custom-call | bytes 10485760 | tf_op jit(solution)/shard_map/place/pallas_call | solution.py:138
  (25 shorter events, 0.1 us)
Async XLA Ops:
  0.6 15.8 %copy-start.7 = (bf16[256,512]{1,0:T(8,128)(2,1)S(1)}, bf16[256,512]{1,0:T(8,128)(2,1)}, u32[]{:S(2)}) copy-start(bf16[256,512]{1,0:T(8,128)(2,1)} %refs_0_.1) | copy-start | bytes 786436
  0.6 20.0 %copy-start.6 = (s32[32]{0:T(128)S(1)}, s32[32]{0:T(128)}, u32[]{:S(2)}) copy-start(s32[32]{0:T(128)} %span_ref.5) | copy-start | bytes 388
  0.7 21.3 %copy-start.15 = (bf16[4096]{0:T(1024)(128)(2,1)S(1)}, bf16[4096]{0:T(1024)(128)(2,1)}, u32[]{:S(2)}) copy-start(bf16[4096]{0:T(1024)(128)(2,1)} %param.7) | copy-start | bytes 24580
  4.9 62.3 %all-to-all-start = ((bf16[32,4,32,128]{3,2,1,0:T(8,128)(2,1)}), bf16[32,4,32,128]{3,2,1,0:T(8,128)(2,1)S(1)}, u32[]{:S(2)}, u32[]{:S(2)}) async-start(bf16[32,4,32,128]{3,2,1,0:T(8,128)(2,1)} %get-tuple-element.52), calls=%async_computation | async-start | bytes 2097152 | tf_op jit(solution)/shard_map/all_to_all | solution.py:400
  16.4 10.9 %collective-permute-start = (bf16[256,512]{1,0:T(8,128)(2,1)S(1)}, bf16[256,512]{1,0:T(8,128)(2,1)S(1)}, u32[]{:S(2)}, u32[]{:S(2)}) collective-permute-start(bf16[256,512]{1,0:T(8,128)(2,1)S(1)} %copy-done.7), channel_id=1, source_target_pairs={{0,4},{1,5},{2,6},{3,7},{4,0},{5,1},{6,2},{7,3},{8,12},{9,13},{10,... | collective-permute-start | bytes 786440 | tf_op jit(solution)/shard_map/ppermute | solution.py:380
  18.6 12.8 %collective-permute-start.1 = (bf16[256,512]{1,0:T(8,128)(2,1)S(1)}, bf16[256,512]{1,0:T(8,128)(2,1)S(1)}, u32[]{:S(2)}, u32[]{:S(2)}) collective-permute-start(bf16[256,512]{1,0:T(8,128)(2,1)S(1)} %copy-done.7), channel_id=1, source_target_pairs={{0,2},{1,3},{2,4},{3,5},{4,6},{5,7},{6,0},{7,1},{8,10},{9,11},{10,... | collective-permute-start | bytes 786440 | tf_op jit(solution)/shard_map/ppermute | solution.py:380
  18.6 12.8 %collective-permute-start.2 = (bf16[256,512]{1,0:T(8,128)(2,1)S(1)}, bf16[256,512]{1,0:T(8,128)(2,1)S(1)}, u32[]{:S(2)}, u32[]{:S(2)}) collective-permute-start(bf16[256,512]{1,0:T(8,128)(2,1)S(1)} %copy-done.7), channel_id=1, source_target_pairs={{0,6},{1,7},{2,0},{3,1},{4,2},{5,3},{6,4},{7,5},{8,14},{9,15},{10,... | collective-permute-start | bytes 786440 | tf_op jit(solution)/shard_map/ppermute | solution.py:380
  20.6 11.4 %collective-permute-start.3 = (bf16[256,512]{1,0:T(8,128)(2,1)S(1)}, bf16[256,512]{1,0:T(8,128)(2,1)S(1)}, u32[]{:S(2)}, u32[]{:S(2)}) collective-permute-start(bf16[256,512]{1,0:T(8,128)(2,1)S(1)} %copy-done.7), channel_id=1, source_target_pairs={{0,1},{1,0},{2,3},{3,2},{4,5},{5,4},{6,7},{7,6},{8,9},{9,8},{10,11... | collective-permute-start | bytes 786440 | tf_op jit(solution)/shard_map/ppermute | solution.py:384
  27.3 6.5 %copy-start.8 = (bf16[256,512]{1,0:T(8,128)(2,1)}, bf16[256,512]{1,0:T(8,128)(2,1)S(1)}, u32[]{:S(2)}) copy-start(bf16[256,512]{1,0:T(8,128)(2,1)S(1)} %collective-permute-done.refs_3_) | copy-start | bytes 786436
  31.5 2.3 %copy-start.9 = (bf16[256,512]{1,0:T(8,128)(2,1)}, bf16[256,512]{1,0:T(8,128)(2,1)S(1)}, u32[]{:S(2)}) copy-start(bf16[256,512]{1,0:T(8,128)(2,1)S(1)} %collective-permute-done.1.refs_1_) | copy-start | bytes 786436
  31.5 1.5 %collective-permute-start.4 = (bf16[256,512]{1,0:T(8,128)(2,1)S(1)}, bf16[256,512]{1,0:T(8,128)(2,1)S(1)}, u32[]{:S(2)}, u32[]{:S(2)}) collective-permute-start(bf16[256,512]{1,0:T(8,128)(2,1)S(1)} %collective-permute-done.1.refs_1_), channel_id=1, source_target_pairs={{0,1},{1,0},{2,3},{3,2},{4,5},{5,4},{6,7},{7,6},{8,9},{9,8},{10,11... | collective-permute-start | bytes 786440 | tf_op jit(solution)/shard_map/ppermute | solution.py:384
  31.5 2.3 %copy-start.10 = (bf16[256,512]{1,0:T(8,128)(2,1)}, bf16[256,512]{1,0:T(8,128)(2,1)S(1)}, u32[]{:S(2)}) copy-start(bf16[256,512]{1,0:T(8,128)(2,1)S(1)} %collective-permute-done.2.refs_2_) | copy-start | bytes 786436
  31.5 1.9 %collective-permute-start.5 = (bf16[256,512]{1,0:T(8,128)(2,1)S(1)}, bf16[256,512]{1,0:T(8,128)(2,1)S(1)}, u32[]{:S(2)}, u32[]{:S(2)}) collective-permute-start(bf16[256,512]{1,0:T(8,128)(2,1)S(1)} %collective-permute-done.2.refs_2_), channel_id=1, source_target_pairs={{0,1},{1,0},{2,3},{3,2},{4,5},{5,4},{6,7},{7,6},{8,9},{9,8},{10,11... | collective-permute-start | bytes 786440 | tf_op jit(solution)/shard_map/ppermute | solution.py:384
  32.0 1.8 %collective-permute-start.6 = (bf16[256,512]{1,0:T(8,128)(2,1)S(1)}, bf16[256,512]{1,0:T(8,128)(2,1)S(1)}, u32[]{:S(2)}, u32[]{:S(2)}) collective-permute-start(bf16[256,512]{1,0:T(8,128)(2,1)S(1)} %collective-permute-done.refs_3_), channel_id=1, source_target_pairs={{0,1},{1,0},{2,3},{3,2},{4,5},{5,4},{6,7},{7,6},{8,9},{9,8},{10,11... | collective-permute-start | bytes 786440 | tf_op jit(solution)/shard_map/ppermute | solution.py:384
  32.1 1.7 %copy-start.11 = (bf16[256,512]{1,0:T(8,128)(2,1)}, bf16[256,512]{1,0:T(8,128)(2,1)S(1)}, u32[]{:S(2)}) copy-start(bf16[256,512]{1,0:T(8,128)(2,1)S(1)} %collective-permute-done.3.refs_4_) | copy-start | bytes 786436
  33.0 0.8 copy-start.12
  33.4 0.7 copy-start.13
  34.1 0.7 copy-start.14
  41.5 33.7 %copy-start = (bf16[256,256]{1,0:T(8,128)(2,1)S(1)}, bf16[256,256]{1,0:T(8,128)(2,1)}, u32[]{:S(2)}) copy-start(bf16[256,256]{1,0:T(8,128)(2,1)} %get-tuple-element.38.refs_1_.refs_2_) | copy-start | bytes 393220
  41.5 6.2 %collective-permute-start.10 = (bf16[256,256]{1,0:T(8,128)(2,1)}, bf16[256,256]{1,0:T(8,128)(2,1)S(1)}, u32[]{:S(2)}, u32[]{:S(2)}) collective-permute-start(bf16[256,256]{1,0:T(8,128)(2,1)} %get-tuple-element.38.refs_1_.refs_2_), channel_id=1, source_target_pairs={{0,56},{8,0},{16,8},{24,16},{32,24},{40,32},{48,40},{56,48},{64,12... | collective-permute-start | bytes 393224 | tf_op jit(solution)/shard_map/ppermute | solution.py:394
  44.3 13.1 %collective-permute-start.15 = (bf16[128,1024]{1,0:T(8,128)(2,1)}, bf16[128,1024]{1,0:T(8,128)(2,1)S(1)}, u32[]{:S(2)}, u32[]{:S(2)}) collective-permute-start(bf16[128,1024]{1,0:T(8,128)(2,1)} %get-tuple-element.50.refs_0_), channel_id=1, source_target_pairs={{0,192},{8,200},{16,208},{24,216},{32,224},{40,232},{48,240},{56,2... | collective-permute-start | bytes 786440 | tf_op jit(solution)/shard_map/ppermute | solution.py:388
  47.1 6.4 %collective-permute-start.7 = (bf16[256,256]{1,0:T(8,128)(2,1)}, bf16[256,256]{1,0:T(8,128)(2,1)S(1)}, u32[]{:S(2)}, u32[]{:S(2)}) collective-permute-start(bf16[256,256]{1,0:T(8,128)(2,1)} %get-tuple-element.38.refs_1_.refs_2_), channel_id=1, source_target_pairs={{0,8},{8,16},{16,24},{24,32},{32,40},{40,48},{48,56},{56,0},{64,72... | collective-permute-start | bytes 393224 | tf_op jit(solution)/shard_map/ppermute | solution.py:394
  47.7 6.1 %collective-permute-start.11 = (bf16[256,256]{1,0:T(8,128)(2,1)S(1)}, bf16[256,256]{1,0:T(8,128)(2,1)S(1)}, u32[]{:S(2)}, u32[]{:S(2)}) collective-permute-start(bf16[256,256]{1,0:T(8,128)(2,1)S(1)} %collective-permute-done.10.refs_5_.refs_6_), channel_id=1, source_target_pairs={{0,56},{8,0},{16,8},{24,16},{32,24},{40,32},{48,40},{56,48},{64,12... | collective-permute-start | bytes 393224 | tf_op jit(solution)/shard_map/ppermute | solution.py:394
  51.3 12.4 %collective-permute-start.14 = (bf16[128,1024]{1,0:T(8,128)(2,1)}, bf16[128,1024]{1,0:T(8,128)(2,1)S(1)}, u32[]{:S(2)}, u32[]{:S(2)}) collective-permute-start(bf16[128,1024]{1,0:T(8,128)(2,1)} %get-tuple-element.50.refs_0_), channel_id=1, source_target_pairs={{0,64},{8,72},{16,80},{24,88},{32,96},{40,104},{48,112},{56,120},{... | collective-permute-start | bytes 786440 | tf_op jit(solution)/shard_map/ppermute | solution.py:388
  53.5 6.7 %collective-permute-start.8 = (bf16[256,256]{1,0:T(8,128)(2,1)S(1)}, bf16[256,256]{1,0:T(8,128)(2,1)S(1)}, u32[]{:S(2)}, u32[]{:S(2)}) collective-permute-start(bf16[256,256]{1,0:T(8,128)(2,1)S(1)} %collective-permute-done.7.refs_2_.refs_3_), channel_id=1, source_target_pairs={{0,8},{8,16},{16,24},{24,32},{32,40},{40,48},{48,56},{56,0},{64,72... | collective-permute-start | bytes 393224 | tf_op jit(solution)/shard_map/ppermute | solution.py:394
  53.8 6.4 %collective-permute-start.12 = (bf16[256,256]{1,0:T(8,128)(2,1)S(1)}, bf16[256,256]{1,0:T(8,128)(2,1)S(1)}, u32[]{:S(2)}, u32[]{:S(2)}) collective-permute-start(bf16[256,256]{1,0:T(8,128)(2,1)S(1)} %collective-permute-done.11.refs_6_.refs_7_), channel_id=1, source_target_pairs={{0,56},{8,0},{16,8},{24,16},{32,24},{40,32},{48,40},{56,48},{64,12... | collective-permute-start | bytes 393224 | tf_op jit(solution)/shard_map/ppermute | solution.py:394
  57.5 9.0 %collective-permute-start.16 = (bf16[128,1024]{1,0:T(8,128)(2,1)S(1)}, bf16[128,1024]{1,0:T(8,128)(2,1)S(1)}, u32[]{:S(2)}, u32[]{:S(2)}) collective-permute-start(bf16[128,1024]{1,0:T(8,128)(2,1)S(1)} %collective-permute-done.15.refs_1_), channel_id=1, source_target_pairs={{0,192},{8,200},{16,208},{24,216},{32,224},{40,232},{48,240},{56,2... | collective-permute-start | bytes 786440 | tf_op jit(solution)/shard_map/ppermute | solution.py:388
  60.3 6.2 %collective-permute-start.9 = (bf16[256,256]{1,0:T(8,128)(2,1)S(1)}, bf16[256,256]{1,0:T(8,128)(2,1)S(1)}, u32[]{:S(2)}, u32[]{:S(2)}) collective-permute-start(bf16[256,256]{1,0:T(8,128)(2,1)S(1)} %collective-permute-done.8.refs_3_.refs_4_), channel_id=1, source_target_pairs={{0,8},{8,16},{16,24},{24,32},{32,40},{40,48},{48,56},{56,0},{64,72... | collective-permute-start | bytes 393224 | tf_op jit(solution)/shard_map/ppermute | solution.py:394
  60.3 6.2 %collective-permute-start.13 = (bf16[256,256]{1,0:T(8,128)(2,1)S(1)}, bf16[256,256]{1,0:T(8,128)(2,1)S(1)}, u32[]{:S(2)}, u32[]{:S(2)}) collective-permute-start(bf16[256,256]{1,0:T(8,128)(2,1)S(1)} %collective-permute-done.12.refs_7_.refs_8_), channel_id=1, source_target_pairs={{0,56},{8,0},{16,8},{24,16},{32,24},{40,32},{48,40},{56,48},{64,12... | collective-permute-start | bytes 393224 | tf_op jit(solution)/shard_map/ppermute | solution.py:394
  63.7 0.7 copy-start.2
  66.4 0.7 copy-start.4
  67.1 35.6 %all-to-all-start.1 = ((bf16[32,4,32,128]{3,2,1,0:T(8,128)(2,1)}), bf16[32,4,32,128]{3,2,1,0:T(8,128)(2,1)S(1)}, u32[]{:S(2)}, u32[]{:S(2)}) async-start(bf16[32,4,32,128]{3,2,1,0:T(8,128)(2,1)} %get-tuple-element.53), calls=%async_computation.1 | async-start | bytes 2097152 | tf_op jit(solution)/shard_map/all_to_all | solution.py:400
  75.2 1.0 copy-start.5
  76.2 14.0 %copy-start.1 = (bf16[128,1024]{1,0:T(8,128)(2,1)S(1)}, bf16[128,1024]{1,0:T(8,128)(2,1)}, u32[]{:S(2)}) copy-start(bf16[128,1024]{1,0:T(8,128)(2,1)} %get-tuple-element.50.refs_0_) | copy-start | bytes 786436
  76.9 20.3 %collective-permute-start.17 = (bf16[144,1024]{1,0:T(8,128)(2,1)S(1)}, bf16[144,1024]{1,0:T(8,128)(2,1)S(1)}, u32[]{:S(2)}, u32[]{:S(2)}) collective-permute-start(bf16[144,1024]{1,0:T(8,128)(2,1)S(1)} %attend.3), channel_id=1, source_target_pairs={{0,128},{8,136},{16,144},{24,152},{32,160},{40,168},{48,176},{56,1... | collective-permute-start | bytes 884744 | tf_op jit(solution)/shard_map/ppermute | solution.py:388
  83.8 0.9 copy-start.3
  88.1 12.4 %collective-permute-start.18 = (bf16[144,1024]{1,0:T(8,128)(2,1)S(1)}, bf16[144,1024]{1,0:T(8,128)(2,1)S(1)}, u32[]{:S(2)}, u32[]{:S(2)}) collective-permute-start(bf16[144,1024]{1,0:T(8,128)(2,1)S(1)} %get-tuple-element.48), channel_id=1, source_target_pairs={{0,192},{8,200},{16,208},{24,216},{32,224},{40,232},{48,240},{56,2... | collective-permute-start | bytes 884744 | tf_op jit(solution)/shard_map/ppermute | solution.py:388
  88.2 13.5 %collective-permute-start.19 = (bf16[144,1024]{1,0:T(8,128)(2,1)S(1)}, bf16[144,1024]{1,0:T(8,128)(2,1)S(1)}, u32[]{:S(2)}, u32[]{:S(2)}) collective-permute-start(bf16[144,1024]{1,0:T(8,128)(2,1)S(1)} %get-tuple-element.49), channel_id=1, source_target_pairs={{0,64},{8,72},{16,80},{24,88},{32,96},{40,104},{48,112},{56,120},{... | collective-permute-start | bytes 884744 | tf_op jit(solution)/shard_map/ppermute | solution.py:388

commit v2 on v1

--- a/solution.py
+++ b/solution.py
@@ -220,7 +220,7 @@
             pltpu.VMEM((SPAN, D), jnp.bfloat16),
             pltpu.SemaphoreType.DMA((8,)),
         ],
-        compiler_params=params(56),
+        compiler_params=params(50),
         cost_estimate=cost(16),
         name="project",
     )(gain, cosine, sine, w_qkv, *blocks)

time: 106 us -> 103 us (0.972)
  waiting for transfers between devices: 19.8 us -> 23.4 us
  Pallas kernels: 23.6 us -> 20.3 us
  starting transfers between devices: 53.8 us -> 50.5 us
    ppermute x6, starting transfers between devices: 15.9 us -> 13.5 us  [along_y(): lax.ppermute(value, 'ctx', [(i, (i // NZ + step) % NY * NZ + i % NZ) for...]
    ppermute x6, waiting for transfers between devices: 6.84 us -> 9.15 us  [along_y(): lax.ppermute(value, 'ctx', [(i, (i // NZ + step) % NY * NZ + i % NZ) for...]
    pallas_call x1, Pallas kernels: 6.75 us -> 5.09 us  [project(): pl.pallas_call(project_kernel, out_shape=(jax.ShapeDtypeStruct((HD, ROWS)...]
    pallas_call x3, Pallas kernels: 8.75 us -> 7.12 us  [attend(): pl.pallas_call(functools.partial(attend_kernel, steps), out_shape=(part,)...]
    ppermute x3, waiting for transfers between devices: 7.61 us -> 8.9 us  [along_x(): lax.ppermute(value, 'kvh', [(i, (i // 2 + step) % 4 * 2 + i % 2) for i in...]
    unnamed x32 -> x18, local copies, waits for them, and re-layouts: 4.36 us -> 4.97 us
  transfers between devices with their start and end apart: 22 -> 22, of which waited for: 12 -> 11; matrix products, arithmetic and copies ran while one was open for 2% -> 1% of each run, Pallas kernels for 16% -> 13%
where the time goes in v2:
time: 103 us; the launch traced here: 102 us
  starting transfers between devices  50.5 us (49%)
  waiting for transfers between devices  23.4 us (23%)
  Pallas kernels  20.3 us (20%)
  local copies, waits for them, and re-layouts  4.99 us (5%)
  between operations  1.62 us (2%)
  other arithmetic  1.2 us (1%)
    all_to_all x2, starting transfers between devices, to_owners(): return lax.all_to_all(value, 'ctx', split_axis=0, concat_axis=0, tiled=True)  18.9 us
    ppermute x6, starting transfers between devices, along_y(): lax.ppermute(value, 'ctx', [(i, (i // NZ + step) % NY * NZ + i % NZ) for...  13.5 us
    ppermute x7, starting transfers between devices, along_z(): lax.ppermute(value, 'ctx', [(i, i // NZ * NZ + (i % NZ + step) % NZ) for...  13.4 us
    ppermute x6, waiting for transfers between devices, along_y(): lax.ppermute(value, 'ctx', [(i, (i // NZ + step) % NY * NZ + i % NZ) for...  9.15 us
    ppermute x3, waiting for transfers between devices, along_x(): lax.ppermute(value, 'kvh', [(i, (i // 2 + step) % 4 * 2 + i % 2) for i in...  8.9 us
    pallas_call x3, Pallas kernels, attend(): pl.pallas_call(functools.partial(attend_kernel, steps), out_shape=(part,)...  7.12 us
    pallas_call x1, Pallas kernels, project(): pl.pallas_call(project_kernel, out_shape=(jax.ShapeDtypeStruct((HD, ROWS)...  5.09 us
    unnamed x18, local copies, waits for them, and re-layouts  4.97 us
  transfers between devices with their start and end apart: 22, of which 11 were waited for; matrix products, arithmetic and copies ran while one was open for 1% of the time, Pallas kernels for 13%

profile of v2, /device:TPU:2, one launch (start us, length us, event | category | flops | bytes accessed | tf_op | source)
XLA Modules:
  0.0 102.0 jit_solution(13208763336684494082)
XLA Ops:
  0.6 0.0 copy-start
  0.6 0.0 copy-start.7
  0.7 0.0 copy-start.8
  0.7 4.2 %bucket.1 = (bf16[32,4,32,128]{3,2,1,0:T(8,128)(2,1)}, bf16[32,4,32,128]{3,2,1,0:T(8,128)(2,1)}) custom-call(s32[256]{0:T(256)} %dest_hbm.1, bf16[256,32,128]{2,1,0:T(8,128)(2,1)} %bitcast.5), custom_call_target="tpu_custom_call" | custom-call | bytes 18874368 | tf_op jit(solution)/shard_map/bucket/pallas_call | solution.py:87
  4.9 11.5 %all-to-all-start = ((bf16[32,4,32,128]{3,2,1,0:T(8,128)(2,1)}), bf16[32,4,32,128]{3,2,1,0:T(8,128)(2,1)S(1)}, u32[]{:S(2)}, u32[]{:S(2)}) async-start(bf16[32,4,32,128]{3,2,1,0:T(8,128)(2,1)} %get-tuple-element.52), calls=%async_computation | async-start | bytes 2097152 | tf_op jit(solution)/shard_map/all_to_all | solution.py:400
  16.4 2.2 %collective-permute-start = (bf16[256,512]{1,0:T(8,128)(2,1)S(1)}, bf16[256,512]{1,0:T(8,128)(2,1)S(1)}, u32[]{:S(2)}, u32[]{:S(2)}) collective-permute-start(bf16[256,512]{1,0:T(8,128)(2,1)S(1)} %copy-done), channel_id=1, source_target_pairs={{0,4},{1,5},{2,6},{3,7},{4,0},{5,1},{6,2},{7,3},{8,12},{9,13},{10,... | collective-permute-start | bytes 786440 | tf_op jit(solution)/shard_map/ppermute | solution.py:380
  18.6 0.0 collective-permute-start.1
  18.6 2.0 %collective-permute-start.2 = (bf16[256,512]{1,0:T(8,128)(2,1)S(1)}, bf16[256,512]{1,0:T(8,128)(2,1)S(1)}, u32[]{:S(2)}, u32[]{:S(2)}) collective-permute-start(bf16[256,512]{1,0:T(8,128)(2,1)S(1)} %copy-done), channel_id=1, source_target_pairs={{0,6},{1,7},{2,0},{3,1},{4,2},{5,3},{6,4},{7,5},{8,14},{9,15},{10,... | collective-permute-start | bytes 786440 | tf_op jit(solution)/shard_map/ppermute | solution.py:380
  20.6 0.0 collective-permute-start.3
  20.6 0.6 fusion
  22.0 0.0 copy-done.8
  22.0 0.5 negate_select_fusion
  22.5 4.7 %collective-permute-done.refs_3_ = bf16[256,512]{1,0:T(8,128)(2,1)S(1)} collective-permute-done((bf16[256,512]{1,0:T(8,128)(2,1)S(1)}, bf16[256,512]{1,0:T(8,128)(2,1)S(1)}, u32[]{:S(2)}, u32[]{:S(2)}) %collective-permute-start) | collective-permute-done | bytes 262176 | tf_op jit(solution)/shard_map/ppermute | solution.py:380
  27.3 4.2 %collective-permute-done.1.refs_1_ = bf16[256,512]{1,0:T(8,128)(2,1)S(1)} collective-permute-done((bf16[256,512]{1,0:T(8,128)(2,1)S(1)}, bf16[256,512]{1,0:T(8,128)(2,1)S(1)}, u32[]{:S(2)}, u32[]{:S(2)}) %collective-permute-start.1) | collective-permute-done | bytes 262176 | tf_op jit(solution)/shard_map/ppermute | solution.py:380
  31.4 0.0 collective-permute-start.4
  31.4 0.0 collective-permute-done.2.refs_2_
  31.4 0.5 collective-permute-start.5
  32.0 0.0 collective-permute-start.6
  32.0 0.0 collective-permute-done.3.refs_4_
  32.0 1.0 collective-permute-done.4.refs_5_
  33.0 0.4 collective-permute-done.5.refs_6_
  33.3 0.4 collective-permute-done.6.refs_7_
  33.7 5.1 %project.1 = (bf16[128,1024]{1,0:T(8,128)(2,1)S(1)}, bf16[256,256]{1,0:T(8,128)(2,1)}, bf16[256,256]{1,0:T(8,128)(2,1)S(1)}) custom-call(f32[8,512]{1,0:T(8,128)S(1)} %reshape.53.gain_ref, f32[256,128]{1,0:T(8,128)S(1)} %get-tuple-element.32.cos_ref, f32[256,128]{1,0:T(8,128)S(1)} %get-tuple-element.33.sin_ref, bf16[4096,768]{1,0:T(8,128)(2,1)} %w_hbm.1, ...), custom_call_target="tpu_custom_call" | custom-call | bytes 16777216 | tf_op jit(solution)/shard_map/project/pallas_call | solution.py:209
  38.8 2.8 %collective-permute-start.10 = (bf16[256,256]{1,0:T(8,128)(2,1)S(1)}, bf16[256,256]{1,0:T(8,128)(2,1)S(1)}, u32[]{:S(2)}, u32[]{:S(2)}) collective-permute-start(bf16[256,256]{1,0:T(8,128)(2,1)S(1)} %get-tuple-element.38.refs_1_.refs_2_), channel_id=1, source_target_pairs={{0,56},{8,0},{16,8},{24,16},{32,24},{40,32},{48,40},{56,48},{64,12... | collective-permute-start | bytes 393224 | tf_op jit(solution)/shard_map/ppermute | solution.py:394
  41.6 2.8 %collective-permute-start.15 = (bf16[128,1024]{1,0:T(8,128)(2,1)S(1)}, bf16[128,1024]{1,0:T(8,128)(2,1)S(1)}, u32[]{:S(2)}, u32[]{:S(2)}) collective-permute-start(bf16[128,1024]{1,0:T(8,128)(2,1)S(1)} %get-tuple-element.50.refs_0_), channel_id=1, source_target_pairs={{0,192},{8,200},{16,208},{24,216},{32,224},{40,232},{48,240},{56,2... | collective-permute-start | bytes 786440 | tf_op jit(solution)/shard_map/ppermute | solution.py:388
  44.4 0.0 collective-permute-start.7
  44.4 0.3 collective-permute-done.10.refs_5_.refs_6_
  44.7 3.7 %collective-permute-start.11 = (bf16[256,256]{1,0:T(8,128)(2,1)S(1)}, bf16[256,256]{1,0:T(8,128)(2,1)S(1)}, u32[]{:S(2)}, u32[]{:S(2)}) collective-permute-start(bf16[256,256]{1,0:T(8,128)(2,1)S(1)} %collective-permute-done.10.refs_5_.refs_6_), channel_id=1, source_target_pairs={{0,56},{8,0},{16,8},{24,16},{32,24},{40,32},{48,40},{56,48},{64,12... | collective-permute-start | bytes 393224 | tf_op jit(solution)/shard_map/ppermute | solution.py:394
  48.4 1.5 %collective-permute-start.14 = (bf16[128,1024]{1,0:T(8,128)(2,1)S(1)}, bf16[128,1024]{1,0:T(8,128)(2,1)S(1)}, u32[]{:S(2)}, u32[]{:S(2)}) collective-permute-start(bf16[128,1024]{1,0:T(8,128)(2,1)S(1)} %get-tuple-element.50.refs_0_), channel_id=1, source_target_pairs={{0,64},{8,72},{16,80},{24,88},{32,96},{40,104},{48,112},{56,120},{... | collective-permute-start | bytes 786440 | tf_op jit(solution)/shard_map/ppermute | solution.py:388
  49.8 0.7 collective-permute-done.7.refs_2_.refs_3_
  50.6 0.0 collective-permute-start.8
  50.6 0.3 collective-permute-done.11.refs_6_.refs_7_
  50.9 3.7 %collective-permute-start.12 = (bf16[256,256]{1,0:T(8,128)(2,1)S(1)}, bf16[256,256]{1,0:T(8,128)(2,1)S(1)}, u32[]{:S(2)}, u32[]{:S(2)}) collective-permute-start(bf16[256,256]{1,0:T(8,128)(2,1)S(1)} %collective-permute-done.11.refs_6_.refs_7_), channel_id=1, source_target_pairs={{0,56},{8,0},{16,8},{24,16},{32,24},{40,32},{48,40},{56,48},{64,12... | collective-permute-start | bytes 393224 | tf_op jit(solution)/shard_map/ppermute | solution.py:394
  54.6 0.0 collective-permute-done.15.refs_1_
  54.6 2.8 %collective-permute-start.16 = (bf16[128,1024]{1,0:T(8,128)(2,1)S(1)}, bf16[128,1024]{1,0:T(8,128)(2,1)S(1)}, u32[]{:S(2)}, u32[]{:S(2)}) collective-permute-start(bf16[128,1024]{1,0:T(8,128)(2,1)S(1)} %collective-permute-done.15.refs_1_), channel_id=1, source_target_pairs={{0,192},{8,200},{16,208},{24,216},{32,224},{40,232},{48,240},{56,2... | collective-permute-start | bytes 786440 | tf_op jit(solution)/shard_map/ppermute | solution.py:388
  57.3 0.7 copy-done.1
  58.0 0.0 collective-permute-done.8.refs_3_.refs_4_
  58.0 0.0 collective-permute-start.9
  58.0 0.0 collective-permute-done.12.refs_7_.refs_8_
  58.0 3.2 %collective-permute-start.13 = (bf16[256,256]{1,0:T(8,128)(2,1)S(1)}, bf16[256,256]{1,0:T(8,128)(2,1)S(1)}, u32[]{:S(2)}, u32[]{:S(2)}) collective-permute-start(bf16[256,256]{1,0:T(8,128)(2,1)S(1)} %collective-permute-done.12.refs_7_.refs_8_), channel_id=1, source_target_pairs={{0,56},{8,0},{16,8},{24,16},{32,24},{40,32},{48,40},{56,48},{64,12... | collective-permute-start | bytes 393224 | tf_op jit(solution)/shard_map/ppermute | solution.py:394
  61.3 0.0 collective-permute-done.14.refs_0_
  61.3 0.7 copy-done.3
  62.0 2.2 %collective-permute-done.9.refs_4_.refs_5_ = bf16[256,256]{1,0:T(8,128)(2,1)S(1)} collective-permute-done((bf16[256,256]{1,0:T(8,128)(2,1)S(1)}, bf16[256,256]{1,0:T(8,128)(2,1)S(1)}, u32[]{:S(2)}, u32[]{:S(2)}) %collective-permute-start.9) | collective-permute-done | bytes 131104 | tf_op jit(solution)/shard_map/ppermute | solution.py:394
  64.2 0.0 collective-permute-done.13.refs_8_.refs_9_
  64.2 0.0 collective-permute-done.16.refs_0_
  64.2 0.7 copy-done.5
  64.9 0.0 all-to-all-done.first_ref
  64.9 7.4 %all-to-all-start.1 = ((bf16[32,4,32,128]{3,2,1,0:T(8,128)(2,1)}), bf16[32,4,32,128]{3,2,1,0:T(8,128)(2,1)S(1)}, u32[]{:S(2)}, u32[]{:S(2)}) async-start(bf16[32,4,32,128]{3,2,1,0:T(8,128)(2,1)} %get-tuple-element.53), calls=%async_computation.1 | async-start | bytes 2097152 | tf_op jit(solution)/shard_map/all_to_all | solution.py:400
  72.3 0.0 copy-start.6
  72.3 0.9 copy-done.6
  73.3 0.7 attend.3
  74.0 4.4 %collective-permute-start.17 = (bf16[144,1024]{1,0:T(8,128)(2,1)S(1)}, bf16[144,1024]{1,0:T(8,128)(2,1)S(1)}, u32[]{:S(2)}, u32[]{:S(2)}) collective-permute-start(bf16[144,1024]{1,0:T(8,128)(2,1)S(1)} %attend.3), channel_id=1, source_target_pairs={{0,128},{8,136},{16,144},{24,152},{32,160},{40,168},{48,176},{56,1... | collective-permute-start | bytes 884744 | tf_op jit(solution)/shard_map/ppermute | solution.py:388
  78.4 0.9 copy-done.2
  79.3 0.9 copy-done.4
  80.3 4.5 %attend.4 = (bf16[144,1024]{1,0:T(8,128)(2,1)S(1)}, bf16[144,1024]{1,0:T(8,128)(2,1)S(1)}) custom-call(s32[32]{0:T(128)S(1)} %copy-done.7, bf16[128,1024]{1,0:T(8,128)(2,1)S(1)} %copy-done.4, bf16[128,1024]{1,0:T(8,128)(2,1)S(1)} %copy-done.2, bf16[256,256]{1,0:T(8,128)(2,1)S(1)} %get-tuple-element.38.refs_1_.refs_2_, ...), custom_call_target="tpu_custom_call" | custom-call | bytes 20971520 | tf_op jit(solution)/shard_map/attend/pallas_call | solution.py:318
  84.8 0.8 collective-permute-start.18
  85.5 1.3 %collective-permute-start.19 = (bf16[144,1024]{1,0:T(8,128)(2,1)S(1)}, bf16[144,1024]{1,0:T(8,128)(2,1)S(1)}, u32[]{:S(2)}, u32[]{:S(2)}) collective-permute-start(bf16[144,1024]{1,0:T(8,128)(2,1)S(1)} %get-tuple-element.49), channel_id=1, source_target_pairs={{0,64},{8,72},{16,80},{24,88},{32,96},{40,104},{48,112},{56,120},{... | collective-permute-start | bytes 884744 | tf_op jit(solution)/shard_map/ppermute | solution.py:388
  86.9 1.9 %attend.5.refs_3_ = bf16[144,1024]{1,0:T(8,128)(2,1)S(1)} custom-call(s32[32]{0:T(128)S(1)} %copy-done.7, bf16[128,1024]{1,0:T(8,128)(2,1)S(1)} %get-tuple-element.50.refs_0_, bf16[256,256]{1,0:T(8,128)(2,1)S(1)} %get-tuple-element.38.refs_1_.refs_2_, bf16[256,256]{1,0:T(8,128)(2,1)S(1)} %collective-permute-done.7.refs_2_.refs_3_, ...), custom_call_target="tpu_custom_call" | custom-call | bytes 10485760 | tf_op jit(solution)/shard_map/attend/pallas_call | solution.py:318
  88.8 2.1 %collective-permute-done.17.refs_0_ = bf16[144,1024]{1,0:T(8,128)(2,1)S(1)} collective-permute-done((bf16[144,1024]{1,0:T(8,128)(2,1)S(1)}, bf16[144,1024]{1,0:T(8,128)(2,1)S(1)}, u32[]{:S(2)}, u32[]{:S(2)}) %collective-permute-start.17) | collective-permute-done | bytes 294944 | tf_op jit(solution)/shard_map/ppermute | solution.py:388
  90.8 7.1 %collective-permute-done.18.refs_1_ = bf16[144,1024]{1,0:T(8,128)(2,1)S(1)} collective-permute-done((bf16[144,1024]{1,0:T(8,128)(2,1)S(1)}, bf16[144,1024]{1,0:T(8,128)(2,1)S(1)}, u32[]{:S(2)}, u32[]{:S(2)}) %collective-permute-start.18) | collective-permute-done | bytes 294944 | tf_op jit(solution)/shard_map/ppermute | solution.py:388
  97.9 0.0 collective-permute-done.19.refs_2_
  97.9 1.0 %merge.1 = bf16[256,512]{1,0:T(8,128)(2,1)} custom-call(bf16[144,1024]{1,0:T(8,128)(2,1)S(1)} %collective-permute-done.17.refs_0_, bf16[144,1024]{1,0:T(8,128)(2,1)S(1)} %collective-permute-done.18.refs_1_, bf16[144,1024]{1,0:T(8,128)(2,1)S(1)} %collective-permute-done.19.refs_2_, bf16[144,1024]{1,0:T(8,128)(2,1)S(1)} %attend.5.refs_3_), custom_call_target="tpu_custom_call" | custom-call | bytes 4194304 | tf_op jit(solution)/shard_map/merge/pallas_call | solution.py:359
  99.0 0.0 all-to-all-done.1.second_ref
  99.0 2.9 %place.1 = (bf16[256,32,128]{2,1,0:T(8,128)(2,1)}, s32[1]{0:T(128)}) custom-call(bf16[32,4,32,128]{3,2,1,0:T(8,128)(2,1)S(1)} %all-to-all-done.first_ref, bf16[32,4,32,128]{3,2,1,0:T(8,128)(2,1)S(1)} %all-to-all-done.1.second_ref), custom_call_target="tpu_custom_call" | custom-call | bytes 10485760 | tf_op jit(solution)/shard_map/place/pallas_call | solution.py:138
  (11 shorter events, 0.1 us)
Async XLA Ops:
  0.6 15.7 %copy-start = (bf16[256,512]{1,0:T(8,128)(2,1)S(1)}, bf16[256,512]{1,0:T(8,128)(2,1)}, u32[]{:S(2)}) copy-start(bf16[256,512]{1,0:T(8,128)(2,1)} %refs_0_.1) | copy-start | bytes 786436
  0.6 20.0 %copy-start.7 = (s32[32]{0:T(128)S(1)}, s32[32]{0:T(128)}, u32[]{:S(2)}) copy-start(s32[32]{0:T(128)} %span_ref.5) | copy-start | bytes 388
  0.7 21.3 %copy-start.8 = (bf16[4096]{0:T(1024)(128)(2,1)S(1)}, bf16[4096]{0:T(1024)(128)(2,1)}, u32[]{:S(2)}) copy-start(bf16[4096]{0:T(1024)(128)(2,1)} %param.7) | copy-start | bytes 24580
  4.9 60.1 %all-to-all-start = ((bf16[32,4,32,128]{3,2,1,0:T(8,128)(2,1)}), bf16[32,4,32,128]{3,2,1,0:T(8,128)(2,1)S(1)}, u32[]{:S(2)}, u32[]{:S(2)}) async-start(bf16[32,4,32,128]{3,2,1,0:T(8,128)(2,1)} %get-tuple-element.52), calls=%async_computation | async-start | bytes 2097152 | tf_op jit(solution)/shard_map/all_to_all | solution.py:400
  16.4 10.9 %collective-permute-start = (bf16[256,512]{1,0:T(8,128)(2,1)S(1)}, bf16[256,512]{1,0:T(8,128)(2,1)S(1)}, u32[]{:S(2)}, u32[]{:S(2)}) collective-permute-start(bf16[256,512]{1,0:T(8,128)(2,1)S(1)} %copy-done), channel_id=1, source_target_pairs={{0,4},{1,5},{2,6},{3,7},{4,0},{5,1},{6,2},{7,3},{8,12},{9,13},{10,... | collective-permute-start | bytes 786440 | tf_op jit(solution)/shard_map/ppermute | solution.py:380
  18.6 12.8 %collective-permute-start.1 = (bf16[256,512]{1,0:T(8,128)(2,1)S(1)}, bf16[256,512]{1,0:T(8,128)(2,1)S(1)}, u32[]{:S(2)}, u32[]{:S(2)}) collective-permute-start(bf16[256,512]{1,0:T(8,128)(2,1)S(1)} %copy-done), channel_id=1, source_target_pairs={{0,2},{1,3},{2,4},{3,5},{4,6},{5,7},{6,0},{7,1},{8,10},{9,11},{10,... | collective-permute-start | bytes 786440 | tf_op jit(solution)/shard_map/ppermute | solution.py:380
  18.6 12.8 %collective-permute-start.2 = (bf16[256,512]{1,0:T(8,128)(2,1)S(1)}, bf16[256,512]{1,0:T(8,128)(2,1)S(1)}, u32[]{:S(2)}, u32[]{:S(2)}) collective-permute-start(bf16[256,512]{1,0:T(8,128)(2,1)S(1)} %copy-done), channel_id=1, source_target_pairs={{0,6},{1,7},{2,0},{3,1},{4,2},{5,3},{6,4},{7,5},{8,14},{9,15},{10,... | collective-permute-start | bytes 786440 | tf_op jit(solution)/shard_map/ppermute | solution.py:380
  20.6 11.3 %collective-permute-start.3 = (bf16[256,512]{1,0:T(8,128)(2,1)S(1)}, bf16[256,512]{1,0:T(8,128)(2,1)S(1)}, u32[]{:S(2)}, u32[]{:S(2)}) collective-permute-start(bf16[256,512]{1,0:T(8,128)(2,1)S(1)} %copy-done), channel_id=1, source_target_pairs={{0,1},{1,0},{2,3},{3,2},{4,5},{5,4},{6,7},{7,6},{8,9},{9,8},{10,11... | collective-permute-start | bytes 786440 | tf_op jit(solution)/shard_map/ppermute | solution.py:384
  31.4 1.5 %collective-permute-start.4 = (bf16[256,512]{1,0:T(8,128)(2,1)S(1)}, bf16[256,512]{1,0:T(8,128)(2,1)S(1)}, u32[]{:S(2)}, u32[]{:S(2)}) collective-permute-start(bf16[256,512]{1,0:T(8,128)(2,1)S(1)} %collective-permute-done.1.refs_1_), channel_id=1, source_target_pairs={{0,1},{1,0},{2,3},{3,2},{4,5},{5,4},{6,7},{7,6},{8,9},{9,8},{10,11... | collective-permute-start | bytes 786440 | tf_op jit(solution)/shard_map/ppermute | solution.py:384
  31.4 1.9 %collective-permute-start.5 = (bf16[256,512]{1,0:T(8,128)(2,1)S(1)}, bf16[256,512]{1,0:T(8,128)(2,1)S(1)}, u32[]{:S(2)}, u32[]{:S(2)}) collective-permute-start(bf16[256,512]{1,0:T(8,128)(2,1)S(1)} %collective-permute-done.2.refs_2_), channel_id=1, source_target_pairs={{0,1},{1,0},{2,3},{3,2},{4,5},{5,4},{6,7},{7,6},{8,9},{9,8},{10,11... | collective-permute-start | bytes 786440 | tf_op jit(solution)/shard_map/ppermute | solution.py:384
  32.0 1.8 %collective-permute-start.6 = (bf16[256,512]{1,0:T(8,128)(2,1)S(1)}, bf16[256,512]{1,0:T(8,128)(2,1)S(1)}, u32[]{:S(2)}, u32[]{:S(2)}) collective-permute-start(bf16[256,512]{1,0:T(8,128)(2,1)S(1)} %collective-permute-done.refs_3_), channel_id=1, source_target_pairs={{0,1},{1,0},{2,3},{3,2},{4,5},{5,4},{6,7},{7,6},{8,9},{9,8},{10,11... | collective-permute-start | bytes 786440 | tf_op jit(solution)/shard_map/ppermute | solution.py:384
  38.8 5.9 %collective-permute-start.10 = (bf16[256,256]{1,0:T(8,128)(2,1)S(1)}, bf16[256,256]{1,0:T(8,128)(2,1)S(1)}, u32[]{:S(2)}, u32[]{:S(2)}) collective-permute-start(bf16[256,256]{1,0:T(8,128)(2,1)S(1)} %get-tuple-element.38.refs_1_.refs_2_), channel_id=1, source_target_pairs={{0,56},{8,0},{16,8},{24,16},{32,24},{40,32},{48,40},{56,48},{64,12... | collective-permute-start | bytes 393224 | tf_op jit(solution)/shard_map/ppermute | solution.py:394
  41.6 12.9 %collective-permute-start.15 = (bf16[128,1024]{1,0:T(8,128)(2,1)S(1)}, bf16[128,1024]{1,0:T(8,128)(2,1)S(1)}, u32[]{:S(2)}, u32[]{:S(2)}) collective-permute-start(bf16[128,1024]{1,0:T(8,128)(2,1)S(1)} %get-tuple-element.50.refs_0_), channel_id=1, source_target_pairs={{0,192},{8,200},{16,208},{24,216},{32,224},{40,232},{48,240},{56,2... | collective-permute-start | bytes 786440 | tf_op jit(solution)/shard_map/ppermute | solution.py:388
  44.4 6.2 %collective-permute-start.7 = (bf16[256,256]{1,0:T(8,128)(2,1)S(1)}, bf16[256,256]{1,0:T(8,128)(2,1)S(1)}, u32[]{:S(2)}, u32[]{:S(2)}) collective-permute-start(bf16[256,256]{1,0:T(8,128)(2,1)S(1)} %get-tuple-element.38.refs_1_.refs_2_), channel_id=1, source_target_pairs={{0,8},{8,16},{16,24},{24,32},{32,40},{40,48},{48,56},{56,0},{64,72... | collective-permute-start | bytes 393224 | tf_op jit(solution)/shard_map/ppermute | solution.py:394
  44.7 6.2 %collective-permute-start.11 = (bf16[256,256]{1,0:T(8,128)(2,1)S(1)}, bf16[256,256]{1,0:T(8,128)(2,1)S(1)}, u32[]{:S(2)}, u32[]{:S(2)}) collective-permute-start(bf16[256,256]{1,0:T(8,128)(2,1)S(1)} %collective-permute-done.10.refs_5_.refs_6_), channel_id=1, source_target_pairs={{0,56},{8,0},{16,8},{24,16},{32,24},{40,32},{48,40},{56,48},{64,12... | collective-permute-start | bytes 393224 | tf_op jit(solution)/shard_map/ppermute | solution.py:394
  48.4 12.9 %collective-permute-start.14 = (bf16[128,1024]{1,0:T(8,128)(2,1)S(1)}, bf16[128,1024]{1,0:T(8,128)(2,1)S(1)}, u32[]{:S(2)}, u32[]{:S(2)}) collective-permute-start(bf16[128,1024]{1,0:T(8,128)(2,1)S(1)} %get-tuple-element.50.refs_0_), channel_id=1, source_target_pairs={{0,64},{8,72},{16,80},{24,88},{32,96},{40,104},{48,112},{56,120},{... | collective-permute-start | bytes 786440 | tf_op jit(solution)/shard_map/ppermute | solution.py:388
  50.6 7.5 %collective-permute-start.8 = (bf16[256,256]{1,0:T(8,128)(2,1)S(1)}, bf16[256,256]{1,0:T(8,128)(2,1)S(1)}, u32[]{:S(2)}, u32[]{:S(2)}) collective-permute-start(bf16[256,256]{1,0:T(8,128)(2,1)S(1)} %collective-permute-done.7.refs_2_.refs_3_), channel_id=1, source_target_pairs={{0,8},{8,16},{16,24},{24,32},{32,40},{40,48},{48,56},{56,0},{64,72... | collective-permute-start | bytes 393224 | tf_op jit(solution)/shard_map/ppermute | solution.py:394
  50.9 7.1 %collective-permute-start.12 = (bf16[256,256]{1,0:T(8,128)(2,1)S(1)}, bf16[256,256]{1,0:T(8,128)(2,1)S(1)}, u32[]{:S(2)}, u32[]{:S(2)}) collective-permute-start(bf16[256,256]{1,0:T(8,128)(2,1)S(1)} %collective-permute-done.11.refs_6_.refs_7_), channel_id=1, source_target_pairs={{0,56},{8,0},{16,8},{24,16},{32,24},{40,32},{48,40},{56,48},{64,12... | collective-permute-start | bytes 393224 | tf_op jit(solution)/shard_map/ppermute | solution.py:394
  54.6 9.7 %collective-permute-start.16 = (bf16[128,1024]{1,0:T(8,128)(2,1)S(1)}, bf16[128,1024]{1,0:T(8,128)(2,1)S(1)}, u32[]{:S(2)}, u32[]{:S(2)}) collective-permute-start(bf16[128,1024]{1,0:T(8,128)(2,1)S(1)} %collective-permute-done.15.refs_1_), channel_id=1, source_target_pairs={{0,192},{8,200},{16,208},{24,216},{32,224},{40,232},{48,240},{56,2... | collective-permute-start | bytes 786440 | tf_op jit(solution)/shard_map/ppermute | solution.py:388
  57.3 0.7 copy-start.1
  58.0 6.2 %collective-permute-start.9 = (bf16[256,256]{1,0:T(8,128)(2,1)S(1)}, bf16[256,256]{1,0:T(8,128)(2,1)S(1)}, u32[]{:S(2)}, u32[]{:S(2)}) collective-permute-start(bf16[256,256]{1,0:T(8,128)(2,1)S(1)} %collective-permute-done.8.refs_3_.refs_4_), channel_id=1, source_target_pairs={{0,8},{8,16},{16,24},{24,32},{32,40},{40,48},{48,56},{56,0},{64,72... | collective-permute-start | bytes 393224 | tf_op jit(solution)/shard_map/ppermute | solution.py:394
  58.0 6.2 %collective-permute-start.13 = (bf16[256,256]{1,0:T(8,128)(2,1)S(1)}, bf16[256,256]{1,0:T(8,128)(2,1)S(1)}, u32[]{:S(2)}, u32[]{:S(2)}) collective-permute-start(bf16[256,256]{1,0:T(8,128)(2,1)S(1)} %collective-permute-done.12.refs_7_.refs_8_), channel_id=1, source_target_pairs={{0,56},{8,0},{16,8},{24,16},{32,24},{40,32},{48,40},{56,48},{64,12... | collective-permute-start | bytes 393224 | tf_op jit(solution)/shard_map/ppermute | solution.py:394
  61.3 0.7 copy-start.3
  64.2 0.7 copy-start.5
  64.9 34.0 %all-to-all-start.1 = ((bf16[32,4,32,128]{3,2,1,0:T(8,128)(2,1)}), bf16[32,4,32,128]{3,2,1,0:T(8,128)(2,1)S(1)}, u32[]{:S(2)}, u32[]{:S(2)}) async-start(bf16[32,4,32,128]{3,2,1,0:T(8,128)(2,1)} %get-tuple-element.53), calls=%async_computation.1 | async-start | bytes 2097152 | tf_op jit(solution)/shard_map/all_to_all | solution.py:400
  72.3 1.0 copy-start.6
  74.0 16.9 %collective-permute-start.17 = (bf16[144,1024]{1,0:T(8,128)(2,1)S(1)}, bf16[144,1024]{1,0:T(8,128)(2,1)S(1)}, u32[]{:S(2)}, u32[]{:S(2)}) collective-permute-start(bf16[144,1024]{1,0:T(8,128)(2,1)S(1)} %attend.3), channel_id=1, source_target_pairs={{0,128},{8,136},{16,144},{24,152},{32,160},{40,168},{48,176},{56,1... | collective-permute-start | bytes 884744 | tf_op jit(solution)/shard_map/ppermute | solution.py:388
  78.4 0.9 copy-start.2
  79.3 0.9 copy-start.4
  84.8 13.2 %collective-permute-start.18 = (bf16[144,1024]{1,0:T(8,128)(2,1)S(1)}, bf16[144,1024]{1,0:T(8,128)(2,1)S(1)}, u32[]{:S(2)}, u32[]{:S(2)}) collective-permute-start(bf16[144,1024]{1,0:T(8,128)(2,1)S(1)} %get-tuple-element.48), channel_id=1, source_target_pairs={{0,192},{8,200},{16,208},{24,216},{32,224},{40,232},{48,240},{56,2... | collective-permute-start | bytes 884744 | tf_op jit(solution)/shard_map/ppermute | solution.py:388
  85.5 12.4 %collective-permute-start.19 = (bf16[144,1024]{1,0:T(8,128)(2,1)S(1)}, bf16[144,1024]{1,0:T(8,128)(2,1)S(1)}, u32[]{:S(2)}, u32[]{:S(2)}) collective-permute-start(bf16[144,1024]{1,0:T(8,128)(2,1)S(1)} %get-tuple-element.49), channel_id=1, source_target_pairs={{0,64},{8,72},{16,80},{24,88},{32,96},{40,104},{48,112},{56,120},{... | collective-permute-start | bytes 884744 | tf_op jit(solution)/shard_map/ppermute | solution.py:388

commit v3 on v2

--- a/solution.py
+++ b/solution.py
@@ -25,6 +25,7 @@
 SCALE_LOG2 = HD**-0.5 * 1.4426950408889634
 MARK = 64.0
 STATS = 16
+PARTS = 4
 STEPS_X = (0, 1, 3, 2)
 STEPS_Y = (0, -1, 1, 2)
 STEPS_Z = (0, -1, -2, -3, 1, 2, 3, 4)
@@ -44,16 +45,18 @@
 
 def bucket_kernel(dest_hbm, pages_hbm, first_out, second_out, *refs):
     dest_ref, pages_ref, held_ref, count_ref, in_sems, sems = refs
-    loads = [
-        pltpu.make_async_copy(dest_hbm, dest_ref, in_sems.at[0]),
-        pltpu.make_async_copy(pages_hbm, pages_ref, in_sems.at[1]),
-    ]
+    size = OWN_CAP // PARTS
+    loads = [pltpu.make_async_copy(dest_hbm, dest_ref, in_sems.at[PARTS])]
+    for part in range(PARTS):
+        rows = pl.ds(part * size, size)
+        loads.append(
+            pltpu.make_async_copy(pages_hbm.at[rows], pages_ref.at[rows], in_sems.at[part])
+        )
     for load in loads:
         load.start()
     for owner in range(N_CTX + 1):
         count_ref[owner] = 0
-    for load in loads:
-        load.wait()
+    loads[0].wait()
 
     def put(page, carry):
         owner = dest_ref[page]
@@ -64,7 +67,15 @@
         held_ref[entry, jnp.where(held, rank, 0)] = pages_ref[page]
         return carry
 
-    lax.fori_loop(0, OWN_CAP, put, 0, unroll=16)
+    for part in range(PARTS):
+        loads[1 + part].wait()
+        lax.fori_loop(part * size, (part + 1) * size, put, 0, unroll=16)
+    buckets = held_ref.at[pl.ds(0, N_CTX)]
+    copies = [
+        pltpu.make_async_copy(buckets.at[:, pl.ds(0, FIRST)], first_out, sems.at[0]),
+        pltpu.make_async_copy(buckets.at[:, pl.ds(FIRST, SECOND)], second_out, sems.at[1]),
+    ]
+    copies[0].start()
 
     for entry in range(N_CTX):
         count = count_ref[entry]
@@ -72,13 +83,7 @@
         here = held_ref[entry, SEND_CAP - 1, 0:16, :]
         marked = jnp.where(count < SEND_CAP, value.astype(jnp.bfloat16), here)
         held_ref[entry, SEND_CAP - 1, 0:16, :] = marked
-    buckets = held_ref.at[pl.ds(0, N_CTX)]
-    copies = [
-        pltpu.make_async_copy(buckets.at[:, pl.ds(0, FIRST)], first_out, sems.at[0]),
-        pltpu.make_async_copy(buckets.at[:, pl.ds(FIRST, SECOND)], second_out, sems.at[1]),
-    ]
-    for copy in copies:
-        copy.start()
+    copies[1].start()
     for copy in copies:
         copy.wait()
 
@@ -96,7 +101,7 @@
             pltpu.VMEM((OWN_CAP, PAGE_ROWS, HD), jnp.bfloat16),
             pltpu.VMEM((N_CTX + 1, SEND_CAP, PAGE_ROWS, HD), jnp.bfloat16),
             pltpu.SMEM((N_CTX + 1,), jnp.int32),
-            pltpu.SemaphoreType.DMA((2,)),
+            pltpu.SemaphoreType.DMA((PARTS + 1,)),
             pltpu.SemaphoreType.DMA((2,)),
         ],
         compiler_params=params(56),
@@ -114,11 +119,13 @@
         copy.start()
     for copy in copies:
         copy.wait()
-    offset = jnp.int32(0)
+    counts = []
     for store in range(N_CTX):
         last = held_ref[store, SEND_CAP - 1, 0:16, :].astype(jnp.float32)
         top = jnp.max(last)
-        count = jnp.where(top > MARK / 2, (top - MARK).astype(jnp.int32), SEND_CAP)
+        counts.append(jnp.where(top > MARK / 2, (top - MARK).astype(jnp.int32), SEND_CAP))
+    offset = jnp.int32(0)
+    for store, count in enumerate(counts):
         for rank in range(SEND_CAP):
             placed_ref[offset + rank] = held_ref[store, rank]
         offset = offset + count

time: 103 us -> 102 us (level); the launches traced: 102 us -> 102 us
  waiting for transfers between devices: 23.4 us -> 18.9 us
  Pallas kernels: 20.3 us -> 24.2 us
    ppermute x6, waiting for transfers between devices: 9.15 us -> 4.65 us  [along_y(): lax.ppermute(value, 'ctx', [(i, (i // NZ + step) % NY * NZ + i % NZ) for...]
    pallas_call x3, Pallas kernels: 7.12 us -> 11.6 us  [attend(): pl.pallas_call(functools.partial(attend_kernel, steps), out_shape=(part,)...]
  transfers between devices with their start and end apart: 22 -> 22, of which waited for: 11 -> 11; matrix products, arithmetic and copies ran while one was open for 1% -> 1% of each run, Pallas kernels for 13% -> 17%
where the time goes in v3:
time: 102 us
  starting transfers between devices  51.2 us (50%)
  Pallas kernels  24.2 us (24%)
  waiting for transfers between devices  18.9 us (19%)
  local copies, waits for them, and re-layouts  4.99 us (5%)
  between operations  1.63 us (2%)
  other arithmetic  1.2 us (1%)
    all_to_all x2, starting transfers between devices, to_owners(): return lax.all_to_all(value, 'ctx', split_axis=0, concat_axis=0, tiled=True)  18.9 us
    ppermute x6, starting transfers between devices, along_y(): lax.ppermute(value, 'ctx', [(i, (i // NZ + step) % NY * NZ + i % NZ) for...  14.2 us
    ppermute x7, starting transfers between devices, along_z(): lax.ppermute(value, 'ctx', [(i, i // NZ * NZ + (i % NZ + step) % NZ) for...  13.4 us
    pallas_call x3, Pallas kernels, attend(): pl.pallas_call(functools.partial(attend_kernel, steps), out_shape=(part,)...  11.6 us
    ppermute x3, waiting for transfers between devices, along_x(): lax.ppermute(value, 'kvh', [(i, (i // 2 + step) % 4 * 2 + i % 2) for i in...  8.9 us
    pallas_call x1, Pallas kernels, project(): pl.pallas_call(project_kernel, out_shape=(jax.ShapeDtypeStruct((HD, ROWS)...  5.1 us
    unnamed x18, local copies, waits for them, and re-layouts  4.97 us
    ppermute x6, waiting for transfers between devices, along_y(): lax.ppermute(value, 'ctx', [(i, (i // NZ + step) % NY * NZ + i % NZ) for...  4.65 us
  transfers between devices with their start and end apart: 22, of which 11 were waited for; matrix products, arithmetic and copies ran while one was open for 1% of the time, Pallas kernels for 17%

profile of v3, /device:TPU:2, one launch (start us, length us, event | category | flops | bytes accessed | tf_op | source)
XLA Modules:
  0.0 102.1 jit_solution(14400164111109319796)
XLA Ops:
  0.6 0.0 copy-start
  0.6 0.0 copy-start.7
  0.7 0.0 copy-start.8
  0.7 3.6 %bucket.1 = (bf16[32,4,32,128]{3,2,1,0:T(8,128)(2,1)}, bf16[32,4,32,128]{3,2,1,0:T(8,128)(2,1)}) custom-call(s32[256]{0:T(256)} %dest_hbm.1, bf16[256,32,128]{2,1,0:T(8,128)(2,1)} %bitcast.5), custom_call_target="tpu_custom_call" | custom-call | bytes 18874368 | tf_op jit(solution)/shard_map/bucket/pallas_call | solution.py:92
  4.3 11.5 %all-to-all-start = ((bf16[32,4,32,128]{3,2,1,0:T(8,128)(2,1)}), bf16[32,4,32,128]{3,2,1,0:T(8,128)(2,1)S(1)}, u32[]{:S(2)}, u32[]{:S(2)}) async-start(bf16[32,4,32,128]{3,2,1,0:T(8,128)(2,1)} %get-tuple-element.52), calls=%async_computation | async-start | bytes 2097152 | tf_op jit(solution)/shard_map/all_to_all | solution.py:407
  15.8 2.2 %collective-permute-start = (bf16[256,512]{1,0:T(8,128)(2,1)S(1)}, bf16[256,512]{1,0:T(8,128)(2,1)S(1)}, u32[]{:S(2)}, u32[]{:S(2)}) collective-permute-start(bf16[256,512]{1,0:T(8,128)(2,1)S(1)} %copy-done), channel_id=1, source_target_pairs={{0,4},{1,5},{2,6},{3,7},{4,0},{5,1},{6,2},{7,3},{8,12},{9,13},{10,... | collective-permute-start | bytes 786440 | tf_op jit(solution)/shard_map/ppermute | solution.py:387
  18.0 0.0 collective-permute-start.1
  18.0 2.0 %collective-permute-start.2 = (bf16[256,512]{1,0:T(8,128)(2,1)S(1)}, bf16[256,512]{1,0:T(8,128)(2,1)S(1)}, u32[]{:S(2)}, u32[]{:S(2)}) collective-permute-start(bf16[256,512]{1,0:T(8,128)(2,1)S(1)} %copy-done), channel_id=1, source_target_pairs={{0,6},{1,7},{2,0},{3,1},{4,2},{5,3},{6,4},{7,5},{8,14},{9,15},{10,... | collective-permute-start | bytes 786440 | tf_op jit(solution)/shard_map/ppermute | solution.py:387
  20.1 0.0 collective-permute-start.3
  20.1 0.6 fusion
  21.4 0.0 copy-done.8
  21.4 0.5 negate_select_fusion
  22.0 4.7 %collective-permute-done.refs_3_ = bf16[256,512]{1,0:T(8,128)(2,1)S(1)} collective-permute-done((bf16[256,512]{1,0:T(8,128)(2,1)S(1)}, bf16[256,512]{1,0:T(8,128)(2,1)S(1)}, u32[]{:S(2)}, u32[]{:S(2)}) %collective-permute-start) | collective-permute-done | bytes 262176 | tf_op jit(solution)/shard_map/ppermute | solution.py:387
  26.7 4.2 %collective-permute-done.1.refs_1_ = bf16[256,512]{1,0:T(8,128)(2,1)S(1)} collective-permute-done((bf16[256,512]{1,0:T(8,128)(2,1)S(1)}, bf16[256,512]{1,0:T(8,128)(2,1)S(1)}, u32[]{:S(2)}, u32[]{:S(2)}) %collective-permute-start.1) | collective-permute-done | bytes 262176 | tf_op jit(solution)/shard_map/ppermute | solution.py:387
  30.9 0.0 collective-permute-start.4
  30.9 0.0 collective-permute-done.2.refs_2_
  30.9 0.5 collective-permute-start.5
  31.4 0.0 collective-permute-start.6
  31.4 0.0 collective-permute-done.3.refs_4_
  31.4 1.0 collective-permute-done.4.refs_5_
  32.4 0.4 collective-permute-done.5.refs_6_
  32.8 0.4 collective-permute-done.6.refs_7_
  33.1 5.1 %project.1 = (bf16[128,1024]{1,0:T(8,128)(2,1)S(1)}, bf16[256,256]{1,0:T(8,128)(2,1)}, bf16[256,256]{1,0:T(8,128)(2,1)S(1)}) custom-call(f32[8,512]{1,0:T(8,128)S(1)} %reshape.53.gain_ref, f32[256,128]{1,0:T(8,128)S(1)} %get-tuple-element.32.cos_ref, f32[256,128]{1,0:T(8,128)S(1)} %get-tuple-element.33.sin_ref, bf16[4096,768]{1,0:T(8,128)(2,1)} %w_hbm.1, ...), custom_call_target="tpu_custom_call" | custom-call | bytes 16777216 | tf_op jit(solution)/shard_map/project/pallas_call | solution.py:216
  38.3 2.8 %collective-permute-start.10 = (bf16[256,256]{1,0:T(8,128)(2,1)S(1)}, bf16[256,256]{1,0:T(8,128)(2,1)S(1)}, u32[]{:S(2)}, u32[]{:S(2)}) collective-permute-start(bf16[256,256]{1,0:T(8,128)(2,1)S(1)} %get-tuple-element.38.refs_1_.refs_2_), channel_id=1, source_target_pairs={{0,56},{8,0},{16,8},{24,16},{32,24},{40,32},{48,40},{56,48},{64,12... | collective-permute-start | bytes 393224 | tf_op jit(solution)/shard_map/ppermute | solution.py:401
  41.1 2.8 %collective-permute-start.15 = (bf16[128,1024]{1,0:T(8,128)(2,1)S(1)}, bf16[128,1024]{1,0:T(8,128)(2,1)S(1)}, u32[]{:S(2)}, u32[]{:S(2)}) collective-permute-start(bf16[128,1024]{1,0:T(8,128)(2,1)S(1)} %get-tuple-element.50.refs_0_), channel_id=1, source_target_pairs={{0,192},{8,200},{16,208},{24,216},{32,224},{40,232},{48,240},{56,2... | collective-permute-start | bytes 786440 | tf_op jit(solution)/shard_map/ppermute | solution.py:395
  43.8 0.0 collective-permute-start.7
  43.8 0.3 collective-permute-done.10.refs_5_.refs_6_
  44.1 3.7 %collective-permute-start.11 = (bf16[256,256]{1,0:T(8,128)(2,1)S(1)}, bf16[256,256]{1,0:T(8,128)(2,1)S(1)}, u32[]{:S(2)}, u32[]{:S(2)}) collective-permute-start(bf16[256,256]{1,0:T(8,128)(2,1)S(1)} %collective-permute-done.10.refs_5_.refs_6_), channel_id=1, source_target_pairs={{0,56},{8,0},{16,8},{24,16},{32,24},{40,32},{48,40},{56,48},{64,12... | collective-permute-start | bytes 393224 | tf_op jit(solution)/shard_map/ppermute | solution.py:401
  47.8 1.5 %collective-permute-start.14 = (bf16[128,1024]{1,0:T(8,128)(2,1)S(1)}, bf16[128,1024]{1,0:T(8,128)(2,1)S(1)}, u32[]{:S(2)}, u32[]{:S(2)}) collective-permute-start(bf16[128,1024]{1,0:T(8,128)(2,1)S(1)} %get-tuple-element.50.refs_0_), channel_id=1, source_target_pairs={{0,64},{8,72},{16,80},{24,88},{32,96},{40,104},{48,112},{56,120},{... | collective-permute-start | bytes 786440 | tf_op jit(solution)/shard_map/ppermute | solution.py:395
  49.3 0.7 collective-permute-done.7.refs_2_.refs_3_
  50.0 0.0 collective-permute-start.8
  50.0 0.3 collective-permute-done.11.refs_6_.refs_7_
  50.3 3.7 %collective-permute-start.12 = (bf16[256,256]{1,0:T(8,128)(2,1)S(1)}, bf16[256,256]{1,0:T(8,128)(2,1)S(1)}, u32[]{:S(2)}, u32[]{:S(2)}) collective-permute-start(bf16[256,256]{1,0:T(8,128)(2,1)S(1)} %collective-permute-done.11.refs_6_.refs_7_), channel_id=1, source_target_pairs={{0,56},{8,0},{16,8},{24,16},{32,24},{40,32},{48,40},{56,48},{64,12... | collective-permute-start | bytes 393224 | tf_op jit(solution)/shard_map/ppermute | solution.py:401
  54.0 0.0 collective-permute-done.15.refs_1_
  54.0 2.8 %collective-permute-start.16 = (bf16[128,1024]{1,0:T(8,128)(2,1)S(1)}, bf16[128,1024]{1,0:T(8,128)(2,1)S(1)}, u32[]{:S(2)}, u32[]{:S(2)}) collective-permute-start(bf16[128,1024]{1,0:T(8,128)(2,1)S(1)} %collective-permute-done.15.refs_1_), channel_id=1, source_target_pairs={{0,192},{8,200},{16,208},{24,216},{32,224},{40,232},{48,240},{56,2... | collective-permute-start | bytes 786440 | tf_op jit(solution)/shard_map/ppermute | solution.py:395
  56.8 0.7 copy-done.1
  57.5 0.0 collective-permute-done.8.refs_3_.refs_4_
  57.5 0.0 collective-permute-start.9
  57.5 0.0 collective-permute-done.12.refs_7_.refs_8_
  57.5 3.2 %collective-permute-start.13 = (bf16[256,256]{1,0:T(8,128)(2,1)S(1)}, bf16[256,256]{1,0:T(8,128)(2,1)S(1)}, u32[]{:S(2)}, u32[]{:S(2)}) collective-permute-start(bf16[256,256]{1,0:T(8,128)(2,1)S(1)} %collective-permute-done.12.refs_7_.refs_8_), channel_id=1, source_target_pairs={{0,56},{8,0},{16,8},{24,16},{32,24},{40,32},{48,40},{56,48},{64,12... | collective-permute-start | bytes 393224 | tf_op jit(solution)/shard_map/ppermute | solution.py:401
  60.7 0.0 collective-permute-done.14.refs_0_
  60.7 0.7 copy-done.3
  61.4 2.2 %collective-permute-done.9.refs_4_.refs_5_ = bf16[256,256]{1,0:T(8,128)(2,1)S(1)} collective-permute-done((bf16[256,256]{1,0:T(8,128)(2,1)S(1)}, bf16[256,256]{1,0:T(8,128)(2,1)S(1)}, u32[]{:S(2)}, u32[]{:S(2)}) %collective-permute-start.9) | collective-permute-done | bytes 131104 | tf_op jit(solution)/shard_map/ppermute | solution.py:401
  63.6 0.0 collective-permute-done.13.refs_8_.refs_9_
  63.6 0.0 collective-permute-done.16.refs_0_
  63.6 0.7 copy-done.5
  64.4 0.0 all-to-all-done.first_ref
  64.4 7.4 %all-to-all-start.1 = ((bf16[32,4,32,128]{3,2,1,0:T(8,128)(2,1)}), bf16[32,4,32,128]{3,2,1,0:T(8,128)(2,1)S(1)}, u32[]{:S(2)}, u32[]{:S(2)}) async-start(bf16[32,4,32,128]{3,2,1,0:T(8,128)(2,1)} %get-tuple-element.53), calls=%async_computation.1 | async-start | bytes 2097152 | tf_op jit(solution)/shard_map/all_to_all | solution.py:407
  71.7 0.0 copy-start.6
  71.7 0.9 copy-done.6
  72.7 2.4 %attend.3 = bf16[144,1024]{1,0:T(8,128)(2,1)S(1)} custom-call(s32[32]{0:T(128)S(1)} %copy-done.7, bf16[128,1024]{1,0:T(8,128)(2,1)S(1)} %copy-done.6, bf16[256,256]{1,0:T(8,128)(2,1)S(1)} %get-tuple-element.38.refs_1_.refs_2_, bf16[256,256]{1,0:T(8,128)(2,1)S(1)} %collective-permute-done.7.refs_2_.refs_3_, ...), custom_call_target="tpu_custom_call" | custom-call | bytes 10485760 | tf_op jit(solution)/shard_map/attend/pallas_call | solution.py:325
  75.1 3.4 %collective-permute-start.17 = (bf16[144,1024]{1,0:T(8,128)(2,1)S(1)}, bf16[144,1024]{1,0:T(8,128)(2,1)S(1)}, u32[]{:S(2)}, u32[]{:S(2)}) collective-permute-start(bf16[144,1024]{1,0:T(8,128)(2,1)S(1)} %attend.3), channel_id=1, source_target_pairs={{0,128},{8,136},{16,144},{24,152},{32,160},{40,168},{48,176},{56,1... | collective-permute-start | bytes 884744 | tf_op jit(solution)/shard_map/ppermute | solution.py:395
  78.5 0.9 copy-done.2
  79.5 0.9 copy-done.4
  80.4 5.5 %attend.4 = (bf16[144,1024]{1,0:T(8,128)(2,1)S(1)}, bf16[144,1024]{1,0:T(8,128)(2,1)S(1)}) custom-call(s32[32]{0:T(128)S(1)} %copy-done.7, bf16[128,1024]{1,0:T(8,128)(2,1)S(1)} %copy-done.4, bf16[128,1024]{1,0:T(8,128)(2,1)S(1)} %copy-done.2, bf16[256,256]{1,0:T(8,128)(2,1)S(1)} %get-tuple-element.38.refs_1_.refs_2_, ...), custom_call_target="tpu_custom_call" | custom-call | bytes 20971520 | tf_op jit(solution)/shard_map/attend/pallas_call | solution.py:325
  85.9 3.8 %collective-permute-start.18 = (bf16[144,1024]{1,0:T(8,128)(2,1)S(1)}, bf16[144,1024]{1,0:T(8,128)(2,1)S(1)}, u32[]{:S(2)}, u32[]{:S(2)}) collective-permute-start(bf16[144,1024]{1,0:T(8,128)(2,1)S(1)} %get-tuple-element.48), channel_id=1, source_target_pairs={{0,192},{8,200},{16,208},{24,216},{32,224},{40,232},{48,240},{56,2... | collective-permute-start | bytes 884744 | tf_op jit(solution)/shard_map/ppermute | solution.py:395
  89.8 0.0 collective-permute-start.19
  89.8 3.6 %attend.5.refs_3_ = bf16[144,1024]{1,0:T(8,128)(2,1)S(1)} custom-call(s32[32]{0:T(128)S(1)} %copy-done.7, bf16[128,1024]{1,0:T(8,128)(2,1)S(1)} %get-tuple-element.50.refs_0_, bf16[256,256]{1,0:T(8,128)(2,1)S(1)} %get-tuple-element.38.refs_1_.refs_2_, bf16[256,256]{1,0:T(8,128)(2,1)S(1)} %collective-permute-done.7.refs_2_.refs_3_, ...), custom_call_target="tpu_custom_call" | custom-call | bytes 10485760 | tf_op jit(solution)/shard_map/attend/pallas_call | solution.py:325
  93.4 0.0 collective-permute-done.17.refs_0_
  93.4 4.2 %collective-permute-done.18.refs_1_ = bf16[144,1024]{1,0:T(8,128)(2,1)S(1)} collective-permute-done((bf16[144,1024]{1,0:T(8,128)(2,1)S(1)}, bf16[144,1024]{1,0:T(8,128)(2,1)S(1)}, u32[]{:S(2)}, u32[]{:S(2)}) %collective-permute-start.18) | collective-permute-done | bytes 294944 | tf_op jit(solution)/shard_map/ppermute | solution.py:395
  97.6 0.4 collective-permute-done.19.refs_2_
  98.0 1.0 %merge.1 = bf16[256,512]{1,0:T(8,128)(2,1)} custom-call(bf16[144,1024]{1,0:T(8,128)(2,1)S(1)} %collective-permute-done.17.refs_0_, bf16[144,1024]{1,0:T(8,128)(2,1)S(1)} %collective-permute-done.18.refs_1_, bf16[144,1024]{1,0:T(8,128)(2,1)S(1)} %collective-permute-done.19.refs_2_, bf16[144,1024]{1,0:T(8,128)(2,1)S(1)} %attend.5.refs_3_), custom_call_target="tpu_custom_call" | custom-call | bytes 4194304 | tf_op jit(solution)/shard_map/merge/pallas_call | solution.py:366
  99.1 0.0 all-to-all-done.1.second_ref
  99.1 2.9 %place.1 = (bf16[256,32,128]{2,1,0:T(8,128)(2,1)}, s32[1]{0:T(128)}) custom-call(bf16[32,4,32,128]{3,2,1,0:T(8,128)(2,1)S(1)} %all-to-all-done.first_ref, bf16[32,4,32,128]{3,2,1,0:T(8,128)(2,1)S(1)} %all-to-all-done.1.second_ref), custom_call_target="tpu_custom_call" | custom-call | bytes 10485760 | tf_op jit(solution)/shard_map/place/pallas_call | solution.py:145
  (11 shorter events, 0.1 us)
Async XLA Ops:
  0.6 15.2 %copy-start = (bf16[256,512]{1,0:T(8,128)(2,1)S(1)}, bf16[256,512]{1,0:T(8,128)(2,1)}, u32[]{:S(2)}) copy-start(bf16[256,512]{1,0:T(8,128)(2,1)} %refs_0_.1) | copy-start | bytes 786436
  0.6 19.4 %copy-start.7 = (s32[32]{0:T(128)S(1)}, s32[32]{0:T(128)}, u32[]{:S(2)}) copy-start(s32[32]{0:T(128)} %span_ref.5) | copy-start | bytes 388
  0.7 20.7 %copy-start.8 = (bf16[4096]{0:T(1024)(128)(2,1)S(1)}, bf16[4096]{0:T(1024)(128)(2,1)}, u32[]{:S(2)}) copy-start(bf16[4096]{0:T(1024)(128)(2,1)} %param.7) | copy-start | bytes 24580
  4.3 60.1 %all-to-all-start = ((bf16[32,4,32,128]{3,2,1,0:T(8,128)(2,1)}), bf16[32,4,32,128]{3,2,1,0:T(8,128)(2,1)S(1)}, u32[]{:S(2)}, u32[]{:S(2)}) async-start(bf16[32,4,32,128]{3,2,1,0:T(8,128)(2,1)} %get-tuple-element.52), calls=%async_computation | async-start | bytes 2097152 | tf_op jit(solution)/shard_map/all_to_all | solution.py:407
  15.8 10.9 %collective-permute-start = (bf16[256,512]{1,0:T(8,128)(2,1)S(1)}, bf16[256,512]{1,0:T(8,128)(2,1)S(1)}, u32[]{:S(2)}, u32[]{:S(2)}) collective-permute-start(bf16[256,512]{1,0:T(8,128)(2,1)S(1)} %copy-done), channel_id=1, source_target_pairs={{0,4},{1,5},{2,6},{3,7},{4,0},{5,1},{6,2},{7,3},{8,12},{9,13},{10,... | collective-permute-start | bytes 786440 | tf_op jit(solution)/shard_map/ppermute | solution.py:387
  18.0 12.8 %collective-permute-start.1 = (bf16[256,512]{1,0:T(8,128)(2,1)S(1)}, bf16[256,512]{1,0:T(8,128)(2,1)S(1)}, u32[]{:S(2)}, u32[]{:S(2)}) collective-permute-start(bf16[256,512]{1,0:T(8,128)(2,1)S(1)} %copy-done), channel_id=1, source_target_pairs={{0,2},{1,3},{2,4},{3,5},{4,6},{5,7},{6,0},{7,1},{8,10},{9,11},{10,... | collective-permute-start | bytes 786440 | tf_op jit(solution)/shard_map/ppermute | solution.py:387
  18.0 12.8 %collective-permute-start.2 = (bf16[256,512]{1,0:T(8,128)(2,1)S(1)}, bf16[256,512]{1,0:T(8,128)(2,1)S(1)}, u32[]{:S(2)}, u32[]{:S(2)}) collective-permute-start(bf16[256,512]{1,0:T(8,128)(2,1)S(1)} %copy-done), channel_id=1, source_target_pairs={{0,6},{1,7},{2,0},{3,1},{4,2},{5,3},{6,4},{7,5},{8,14},{9,15},{10,... | collective-permute-start | bytes 786440 | tf_op jit(solution)/shard_map/ppermute | solution.py:387
  20.1 11.3 %collective-permute-start.3 = (bf16[256,512]{1,0:T(8,128)(2,1)S(1)}, bf16[256,512]{1,0:T(8,128)(2,1)S(1)}, u32[]{:S(2)}, u32[]{:S(2)}) collective-permute-start(bf16[256,512]{1,0:T(8,128)(2,1)S(1)} %copy-done), channel_id=1, source_target_pairs={{0,1},{1,0},{2,3},{3,2},{4,5},{5,4},{6,7},{7,6},{8,9},{9,8},{10,11... | collective-permute-start | bytes 786440 | tf_op jit(solution)/shard_map/ppermute | solution.py:391
  30.9 1.5 %collective-permute-start.4 = (bf16[256,512]{1,0:T(8,128)(2,1)S(1)}, bf16[256,512]{1,0:T(8,128)(2,1)S(1)}, u32[]{:S(2)}, u32[]{:S(2)}) collective-permute-start(bf16[256,512]{1,0:T(8,128)(2,1)S(1)} %collective-permute-done.1.refs_1_), channel_id=1, source_target_pairs={{0,1},{1,0},{2,3},{3,2},{4,5},{5,4},{6,7},{7,6},{8,9},{9,8},{10,11... | collective-permute-start | bytes 786440 | tf_op jit(solution)/shard_map/ppermute | solution.py:391
  30.9 1.9 %collective-permute-start.5 = (bf16[256,512]{1,0:T(8,128)(2,1)S(1)}, bf16[256,512]{1,0:T(8,128)(2,1)S(1)}, u32[]{:S(2)}, u32[]{:S(2)}) collective-permute-start(bf16[256,512]{1,0:T(8,128)(2,1)S(1)} %collective-permute-done.2.refs_2_), channel_id=1, source_target_pairs={{0,1},{1,0},{2,3},{3,2},{4,5},{5,4},{6,7},{7,6},{8,9},{9,8},{10,11... | collective-permute-start | bytes 786440 | tf_op jit(solution)/shard_map/ppermute | solution.py:391
  31.4 1.8 %collective-permute-start.6 = (bf16[256,512]{1,0:T(8,128)(2,1)S(1)}, bf16[256,512]{1,0:T(8,128)(2,1)S(1)}, u32[]{:S(2)}, u32[]{:S(2)}) collective-permute-start(bf16[256,512]{1,0:T(8,128)(2,1)S(1)} %collective-permute-done.refs_3_), channel_id=1, source_target_pairs={{0,1},{1,0},{2,3},{3,2},{4,5},{5,4},{6,7},{7,6},{8,9},{9,8},{10,11... | collective-permute-start | bytes 786440 | tf_op jit(solution)/shard_map/ppermute | solution.py:391
  38.3 5.9 %collective-permute-start.10 = (bf16[256,256]{1,0:T(8,128)(2,1)S(1)}, bf16[256,256]{1,0:T(8,128)(2,1)S(1)}, u32[]{:S(2)}, u32[]{:S(2)}) collective-permute-start(bf16[256,256]{1,0:T(8,128)(2,1)S(1)} %get-tuple-element.38.refs_1_.refs_2_), channel_id=1, source_target_pairs={{0,56},{8,0},{16,8},{24,16},{32,24},{40,32},{48,40},{56,48},{64,12... | collective-permute-start | bytes 393224 | tf_op jit(solution)/shard_map/ppermute | solution.py:401
  41.1 12.9 %collective-permute-start.15 = (bf16[128,1024]{1,0:T(8,128)(2,1)S(1)}, bf16[128,1024]{1,0:T(8,128)(2,1)S(1)}, u32[]{:S(2)}, u32[]{:S(2)}) collective-permute-start(bf16[128,1024]{1,0:T(8,128)(2,1)S(1)} %get-tuple-element.50.refs_0_), channel_id=1, source_target_pairs={{0,192},{8,200},{16,208},{24,216},{32,224},{40,232},{48,240},{56,2... | collective-permute-start | bytes 786440 | tf_op jit(solution)/shard_map/ppermute | solution.py:395
  43.8 6.2 %collective-permute-start.7 = (bf16[256,256]{1,0:T(8,128)(2,1)S(1)}, bf16[256,256]{1,0:T(8,128)(2,1)S(1)}, u32[]{:S(2)}, u32[]{:S(2)}) collective-permute-start(bf16[256,256]{1,0:T(8,128)(2,1)S(1)} %get-tuple-element.38.refs_1_.refs_2_), channel_id=1, source_target_pairs={{0,8},{8,16},{16,24},{24,32},{32,40},{40,48},{48,56},{56,0},{64,72... | collective-permute-start | bytes 393224 | tf_op jit(solution)/shard_map/ppermute | solution.py:401
  44.1 6.2 %collective-permute-start.11 = (bf16[256,256]{1,0:T(8,128)(2,1)S(1)}, bf16[256,256]{1,0:T(8,128)(2,1)S(1)}, u32[]{:S(2)}, u32[]{:S(2)}) collective-permute-start(bf16[256,256]{1,0:T(8,128)(2,1)S(1)} %collective-permute-done.10.refs_5_.refs_6_), channel_id=1, source_target_pairs={{0,56},{8,0},{16,8},{24,16},{32,24},{40,32},{48,40},{56,48},{64,12... | collective-permute-start | bytes 393224 | tf_op jit(solution)/shard_map/ppermute | solution.py:401
  47.8 12.9 %collective-permute-start.14 = (bf16[128,1024]{1,0:T(8,128)(2,1)S(1)}, bf16[128,1024]{1,0:T(8,128)(2,1)S(1)}, u32[]{:S(2)}, u32[]{:S(2)}) collective-permute-start(bf16[128,1024]{1,0:T(8,128)(2,1)S(1)} %get-tuple-element.50.refs_0_), channel_id=1, source_target_pairs={{0,64},{8,72},{16,80},{24,88},{32,96},{40,104},{48,112},{56,120},{... | collective-permute-start | bytes 786440 | tf_op jit(solution)/shard_map/ppermute | solution.py:395
  50.0 7.5 %collective-permute-start.8 = (bf16[256,256]{1,0:T(8,128)(2,1)S(1)}, bf16[256,256]{1,0:T(8,128)(2,1)S(1)}, u32[]{:S(2)}, u32[]{:S(2)}) collective-permute-start(bf16[256,256]{1,0:T(8,128)(2,1)S(1)} %collective-permute-done.7.refs_2_.refs_3_), channel_id=1, source_target_pairs={{0,8},{8,16},{16,24},{24,32},{32,40},{40,48},{48,56},{56,0},{64,72... | collective-permute-start | bytes 393224 | tf_op jit(solution)/shard_map/ppermute | solution.py:401
  50.3 7.1 %collective-permute-start.12 = (bf16[256,256]{1,0:T(8,128)(2,1)S(1)}, bf16[256,256]{1,0:T(8,128)(2,1)S(1)}, u32[]{:S(2)}, u32[]{:S(2)}) collective-permute-start(bf16[256,256]{1,0:T(8,128)(2,1)S(1)} %collective-permute-done.11.refs_6_.refs_7_), channel_id=1, source_target_pairs={{0,56},{8,0},{16,8},{24,16},{32,24},{40,32},{48,40},{56,48},{64,12... | collective-permute-start | bytes 393224 | tf_op jit(solution)/shard_map/ppermute | solution.py:401
  54.0 9.7 %collective-permute-start.16 = (bf16[128,1024]{1,0:T(8,128)(2,1)S(1)}, bf16[128,1024]{1,0:T(8,128)(2,1)S(1)}, u32[]{:S(2)}, u32[]{:S(2)}) collective-permute-start(bf16[128,1024]{1,0:T(8,128)(2,1)S(1)} %collective-permute-done.15.refs_1_), channel_id=1, source_target_pairs={{0,192},{8,200},{16,208},{24,216},{32,224},{40,232},{48,240},{56,2... | collective-permute-start | bytes 786440 | tf_op jit(solution)/shard_map/ppermute | solution.py:395
  56.8 0.7 copy-start.1
  57.5 6.2 %collective-permute-start.9 = (bf16[256,256]{1,0:T(8,128)(2,1)S(1)}, bf16[256,256]{1,0:T(8,128)(2,1)S(1)}, u32[]{:S(2)}, u32[]{:S(2)}) collective-permute-start(bf16[256,256]{1,0:T(8,128)(2,1)S(1)} %collective-permute-done.8.refs_3_.refs_4_), channel_id=1, source_target_pairs={{0,8},{8,16},{16,24},{24,32},{32,40},{40,48},{48,56},{56,0},{64,72... | collective-permute-start | bytes 393224 | tf_op jit(solution)/shard_map/ppermute | solution.py:401
  57.5 6.2 %collective-permute-start.13 = (bf16[256,256]{1,0:T(8,128)(2,1)S(1)}, bf16[256,256]{1,0:T(8,128)(2,1)S(1)}, u32[]{:S(2)}, u32[]{:S(2)}) collective-permute-start(bf16[256,256]{1,0:T(8,128)(2,1)S(1)} %collective-permute-done.12.refs_7_.refs_8_), channel_id=1, source_target_pairs={{0,56},{8,0},{16,8},{24,16},{32,24},{40,32},{48,40},{56,48},{64,12... | collective-permute-start | bytes 393224 | tf_op jit(solution)/shard_map/ppermute | solution.py:401
  60.7 0.7 copy-start.3
  63.6 0.7 copy-start.5
  64.4 34.7 %all-to-all-start.1 = ((bf16[32,4,32,128]{3,2,1,0:T(8,128)(2,1)}), bf16[32,4,32,128]{3,2,1,0:T(8,128)(2,1)S(1)}, u32[]{:S(2)}, u32[]{:S(2)}) async-start(bf16[32,4,32,128]{3,2,1,0:T(8,128)(2,1)} %get-tuple-element.53), calls=%async_computation.1 | async-start | bytes 2097152 | tf_op jit(solution)/shard_map/all_to_all | solution.py:407
  71.7 1.0 copy-start.6
  75.1 18.3 %collective-permute-start.17 = (bf16[144,1024]{1,0:T(8,128)(2,1)S(1)}, bf16[144,1024]{1,0:T(8,128)(2,1)S(1)}, u32[]{:S(2)}, u32[]{:S(2)}) collective-permute-start(bf16[144,1024]{1,0:T(8,128)(2,1)S(1)} %attend.3), channel_id=1, source_target_pairs={{0,128},{8,136},{16,144},{24,152},{32,160},{40,168},{48,176},{56,1... | collective-permute-start | bytes 884744 | tf_op jit(solution)/shard_map/ppermute | solution.py:395
  78.5 0.9 copy-start.2
  79.5 0.9 copy-start.4
  85.9 11.7 %collective-permute-start.18 = (bf16[144,1024]{1,0:T(8,128)(2,1)S(1)}, bf16[144,1024]{1,0:T(8,128)(2,1)S(1)}, u32[]{:S(2)}, u32[]{:S(2)}) collective-permute-start(bf16[144,1024]{1,0:T(8,128)(2,1)S(1)} %get-tuple-element.48), channel_id=1, source_target_pairs={{0,192},{8,200},{16,208},{24,216},{32,224},{40,232},{48,240},{56,2... | collective-permute-start | bytes 884744 | tf_op jit(solution)/shard_map/ppermute | solution.py:395
  89.8 8.3 %collective-permute-start.19 = (bf16[144,1024]{1,0:T(8,128)(2,1)S(1)}, bf16[144,1024]{1,0:T(8,128)(2,1)S(1)}, u32[]{:S(2)}, u32[]{:S(2)}) collective-permute-start(bf16[144,1024]{1,0:T(8,128)(2,1)S(1)} %get-tuple-element.49), channel_id=1, source_target_pairs={{0,64},{8,72},{16,80},{24,88},{32,96},{40,104},{48,112},{56,120},{... | collective-permute-start | bytes 884744 | tf_op jit(solution)/shard_map/ppermute | solution.py:395

commit v4 on v3

--- a/solution.py
+++ b/solution.py
@@ -423,8 +423,7 @@
     other = [across(block) for block in same]
     query, cache, message = project(gain, cosine, sine, w_qkv, same + other)
 
-    from_up = along_y(query, -1)
-    queries = [query, along_y(query, 1), from_up, along_y(from_up, -1)]
+    queries = [query] + [along_y(query, -step) for step in STEPS_Y[1:]]
 
     up, down = [message], [message]
     for _ in range(3):

time: 102 us -> 103 us (level); the launches traced: 102 us -> 101 us
  waiting for transfers between devices: 18.9 us -> 23.8 us
  starting transfers between devices: 51.2 us -> 47.4 us
  Pallas kernels: 24.2 us -> 22.1 us
    ppermute x7, waiting for transfers between devices: 3.58 us -> 6.81 us  [along_z(): lax.ppermute(value, 'ctx', [(i, i // NZ * NZ + (i % NZ + step) % NZ) for...]
    ppermute x6, starting transfers between devices: 14.2 us -> 11.5 us  [along_y(): lax.ppermute(value, 'ctx', [(i, (i // NZ + step) % NY * NZ + i % NZ) for...]
    pallas_call x3, Pallas kernels: 11.6 us -> 9.48 us  [attend(): pl.pallas_call(functools.partial(attend_kernel, steps), out_shape=(part,)...]
    ppermute x6, waiting for transfers between devices: 4.65 us -> 6.33 us  [along_y(): lax.ppermute(value, 'ctx', [(i, (i // NZ + step) % NY * NZ + i % NZ) for...]
  transfers between devices with their start and end apart: 22 -> 22, of which waited for: 11 -> 9; matrix products, arithmetic and copies ran while one was open for 1% -> 1% of each run, Pallas kernels for 17% -> 15%
where the time goes in v4:
time: 103 us; the launch traced here: 101 us
  starting transfers between devices  47.4 us (46%)
  waiting for transfers between devices  23.8 us (23%)
  Pallas kernels  22.1 us (21%)
  local copies, waits for them, and re-layouts  4.99 us (5%)
  between operations  1.64 us (2%)
  other arithmetic  1.2 us (1%)
    all_to_all x2, starting transfers between devices, to_owners(): return lax.all_to_all(value, 'ctx', split_axis=0, concat_axis=0, tiled=True)  18.2 us
    ppermute x7, starting transfers between devices, along_z(): lax.ppermute(value, 'ctx', [(i, i // NZ * NZ + (i % NZ + step) % NZ) for...  13 us
    ppermute x6, starting transfers between devices, along_y(): lax.ppermute(value, 'ctx', [(i, (i // NZ + step) % NY * NZ + i % NZ) for...  11.5 us
    pallas_call x3, Pallas kernels, attend(): pl.pallas_call(functools.partial(attend_kernel, steps), out_shape=(part,)...  9.48 us
    ppermute x3, waiting for transfers between devices, along_x(): lax.ppermute(value, 'kvh', [(i, (i // 2 + step) % 4 * 2 + i % 2) for i in...  8.9 us
    ppermute x7, waiting for transfers between devices, along_z(): lax.ppermute(value, 'ctx', [(i, i // NZ * NZ + (i % NZ + step) % NZ) for...  6.81 us
    ppermute x6, waiting for transfers between devices, along_y(): lax.ppermute(value, 'ctx', [(i, (i // NZ + step) % NY * NZ + i % NZ) for...  6.33 us
    pallas_call x1, Pallas kernels, project(): pl.pallas_call(project_kernel, out_shape=(jax.ShapeDtypeStruct((HD, ROWS)...  5.1 us
  transfers between devices with their start and end apart: 22, of which 9 were waited for; matrix products, arithmetic and copies ran while one was open for 1% of the time, Pallas kernels for 15%

profile of v4, /device:TPU:2, one launch (start us, length us, event | category | flops | bytes accessed | tf_op | source)
XLA Modules:
  0.0 101.1 jit_solution(874526289884724487)
XLA Ops:
  0.6 0.0 copy-start
  0.6 0.0 copy-start.7
  0.7 0.0 copy-start.8
  0.7 3.6 %bucket.1 = (bf16[32,4,32,128]{3,2,1,0:T(8,128)(2,1)}, bf16[32,4,32,128]{3,2,1,0:T(8,128)(2,1)}) custom-call(s32[256]{0:T(256)} %dest_hbm.1, bf16[256,32,128]{2,1,0:T(8,128)(2,1)} %bitcast.5), custom_call_target="tpu_custom_call" | custom-call | bytes 18874368 | tf_op jit(solution)/shard_map/bucket/pallas_call | solution.py:92
  4.3 11.5 %all-to-all-start = ((bf16[32,4,32,128]{3,2,1,0:T(8,128)(2,1)}), bf16[32,4,32,128]{3,2,1,0:T(8,128)(2,1)S(1)}, u32[]{:S(2)}, u32[]{:S(2)}) async-start(bf16[32,4,32,128]{3,2,1,0:T(8,128)(2,1)} %get-tuple-element.52), calls=%async_computation | async-start | bytes 2097152 | tf_op jit(solution)/shard_map/all_to_all | solution.py:407
  15.8 0.0 copy-done
  15.8 2.2 %collective-permute-start = (bf16[256,512]{1,0:T(8,128)(2,1)S(1)}, bf16[256,512]{1,0:T(8,128)(2,1)S(1)}, u32[]{:S(2)}, u32[]{:S(2)}) collective-permute-start(bf16[256,512]{1,0:T(8,128)(2,1)S(1)} %copy-done), channel_id=1, source_target_pairs={{0,4},{1,5},{2,6},{3,7},{4,0},{5,1},{6,2},{7,3},{8,12},{9,13},{10,... | collective-permute-start | bytes 786440 | tf_op jit(solution)/shard_map/ppermute | solution.py:387
  18.0 0.0 collective-permute-start.1
  18.0 2.0 %collective-permute-start.2 = (bf16[256,512]{1,0:T(8,128)(2,1)S(1)}, bf16[256,512]{1,0:T(8,128)(2,1)S(1)}, u32[]{:S(2)}, u32[]{:S(2)}) collective-permute-start(bf16[256,512]{1,0:T(8,128)(2,1)S(1)} %copy-done), channel_id=1, source_target_pairs={{0,6},{1,7},{2,0},{3,1},{4,2},{5,3},{6,4},{7,5},{8,14},{9,15},{10,... | collective-permute-start | bytes 786440 | tf_op jit(solution)/shard_map/ppermute | solution.py:387
  20.1 0.0 collective-permute-start.3
  20.1 0.6 fusion
  21.4 0.5 negate_select_fusion
  22.0 4.7 %collective-permute-done.refs_3_ = bf16[256,512]{1,0:T(8,128)(2,1)S(1)} collective-permute-done((bf16[256,512]{1,0:T(8,128)(2,1)S(1)}, bf16[256,512]{1,0:T(8,128)(2,1)S(1)}, u32[]{:S(2)}, u32[]{:S(2)}) %collective-permute-start) | collective-permute-done | bytes 262176 | tf_op jit(solution)/shard_map/ppermute | solution.py:387
  26.7 4.2 %collective-permute-done.1.refs_1_ = bf16[256,512]{1,0:T(8,128)(2,1)S(1)} collective-permute-done((bf16[256,512]{1,0:T(8,128)(2,1)S(1)}, bf16[256,512]{1,0:T(8,128)(2,1)S(1)}, u32[]{:S(2)}, u32[]{:S(2)}) %collective-permute-start.1) | collective-permute-done | bytes 262176 | tf_op jit(solution)/shard_map/ppermute | solution.py:387
  30.9 0.0 collective-permute-start.4
  30.9 0.0 collective-permute-done.2.refs_2_
  30.9 0.5 collective-permute-start.5
  31.4 0.0 collective-permute-start.6
  31.4 0.0 collective-permute-done.3.refs_4_
  31.4 1.0 %collective-permute-done.4.refs_5_ = bf16[256,512]{1,0:T(8,128)(2,1)S(1)} collective-permute-done((bf16[256,512]{1,0:T(8,128)(2,1)S(1)}, bf16[256,512]{1,0:T(8,128)(2,1)S(1)}, u32[]{:S(2)}, u32[]{:S(2)}) %collective-permute-start.4) | collective-permute-done | bytes 262176 | tf_op jit(solution)/shard_map/ppermute | solution.py:391
  32.4 0.4 collective-permute-done.5.refs_6_
  32.8 0.4 collective-permute-done.6.refs_7_
  33.1 5.1 %project.1 = (bf16[128,1024]{1,0:T(8,128)(2,1)S(1)}, bf16[256,256]{1,0:T(8,128)(2,1)}, bf16[256,256]{1,0:T(8,128)(2,1)S(1)}) custom-call(f32[8,512]{1,0:T(8,128)S(1)} %reshape.53.gain_ref, f32[256,128]{1,0:T(8,128)S(1)} %get-tuple-element.32.cos_ref, f32[256,128]{1,0:T(8,128)S(1)} %get-tuple-element.33.sin_ref, bf16[4096,768]{1,0:T(8,128)(2,1)} %w_hbm.1, ...), custom_call_target="tpu_custom_call" | custom-call | bytes 16777216 | tf_op jit(solution)/shard_map/project/pallas_call | solution.py:216
  38.3 2.8 %collective-permute-start.10 = (bf16[256,256]{1,0:T(8,128)(2,1)S(1)}, bf16[256,256]{1,0:T(8,128)(2,1)S(1)}, u32[]{:S(2)}, u32[]{:S(2)}) collective-permute-start(bf16[256,256]{1,0:T(8,128)(2,1)S(1)} %get-tuple-element.38.refs_1_.refs_2_), channel_id=1, source_target_pairs={{0,56},{8,0},{16,8},{24,16},{32,24},{40,32},{48,40},{56,48},{64,12... | collective-permute-start | bytes 393224 | tf_op jit(solution)/shard_map/ppermute | solution.py:401
  41.1 0.0 collective-permute-start.7
  41.1 3.1 %collective-permute-done.10.refs_5_.refs_6_ = bf16[256,256]{1,0:T(8,128)(2,1)S(1)} collective-permute-done((bf16[256,256]{1,0:T(8,128)(2,1)S(1)}, bf16[256,256]{1,0:T(8,128)(2,1)S(1)}, u32[]{:S(2)}, u32[]{:S(2)}) %collective-permute-start.10) | collective-permute-done | bytes 131104 | tf_op jit(solution)/shard_map/ppermute | solution.py:401
  44.1 3.7 %collective-permute-start.11 = (bf16[256,256]{1,0:T(8,128)(2,1)S(1)}, bf16[256,256]{1,0:T(8,128)(2,1)S(1)}, u32[]{:S(2)}, u32[]{:S(2)}) collective-permute-start(bf16[256,256]{1,0:T(8,128)(2,1)S(1)} %collective-permute-done.10.refs_5_.refs_6_), channel_id=1, source_target_pairs={{0,56},{8,0},{16,8},{24,16},{32,24},{40,32},{48,40},{56,48},{64,12... | collective-permute-start | bytes 393224 | tf_op jit(solution)/shard_map/ppermute | solution.py:401
  47.8 1.5 %collective-permute-start.14 = (bf16[128,1024]{1,0:T(8,128)(2,1)S(1)}, bf16[128,1024]{1,0:T(8,128)(2,1)S(1)}, u32[]{:S(2)}, u32[]{:S(2)}) collective-permute-start(bf16[128,1024]{1,0:T(8,128)(2,1)S(1)} %get-tuple-element.50.refs_0_), channel_id=1, source_target_pairs={{0,64},{8,72},{16,80},{24,88},{32,96},{40,104},{48,112},{56,120},{... | collective-permute-start | bytes 786440 | tf_op jit(solution)/shard_map/ppermute | solution.py:395
  49.3 1.8 %collective-permute-start.15 = (bf16[128,1024]{1,0:T(8,128)(2,1)S(1)}, bf16[128,1024]{1,0:T(8,128)(2,1)S(1)}, u32[]{:S(2)}, u32[]{:S(2)}) collective-permute-start(bf16[128,1024]{1,0:T(8,128)(2,1)S(1)} %get-tuple-element.50.refs_0_), channel_id=1, source_target_pairs={{0,192},{8,200},{16,208},{24,216},{32,224},{40,232},{48,240},{56,2... | collective-permute-start | bytes 786440 | tf_op jit(solution)/shard_map/ppermute | solution.py:395
  51.0 1.8 %collective-permute-start.16 = (bf16[128,1024]{1,0:T(8,128)(2,1)S(1)}, bf16[128,1024]{1,0:T(8,128)(2,1)S(1)}, u32[]{:S(2)}, u32[]{:S(2)}) collective-permute-start(bf16[128,1024]{1,0:T(8,128)(2,1)S(1)} %get-tuple-element.50.refs_0_), channel_id=1, source_target_pairs={{0,128},{8,136},{16,144},{24,152},{32,160},{40,168},{48,176},{56,1... | collective-permute-start | bytes 786440 | tf_op jit(solution)/shard_map/ppermute | solution.py:395
  52.8 0.0 collective-permute-done.7.refs_2_.refs_3_
  52.8 0.0 collective-permute-start.8
  52.8 0.0 collective-permute-done.11.refs_6_.refs_7_
  52.8 3.2 %collective-permute-start.12 = (bf16[256,256]{1,0:T(8,128)(2,1)S(1)}, bf16[256,256]{1,0:T(8,128)(2,1)S(1)}, u32[]{:S(2)}, u32[]{:S(2)}) collective-permute-start(bf16[256,256]{1,0:T(8,128)(2,1)S(1)} %collective-permute-done.11.refs_6_.refs_7_), channel_id=1, source_target_pairs={{0,56},{8,0},{16,8},{24,16},{32,24},{40,32},{48,40},{56,48},{64,12... | collective-permute-start | bytes 393224 | tf_op jit(solution)/shard_map/ppermute | solution.py:401
  56.1 2.9 %collective-permute-done.8.refs_3_.refs_4_ = bf16[256,256]{1,0:T(8,128)(2,1)S(1)} collective-permute-done((bf16[256,256]{1,0:T(8,128)(2,1)S(1)}, bf16[256,256]{1,0:T(8,128)(2,1)S(1)}, u32[]{:S(2)}, u32[]{:S(2)}) %collective-permute-start.8) | collective-permute-done | bytes 131104 | tf_op jit(solution)/shard_map/ppermute | solution.py:401
  59.0 0.0 collective-permute-start.9
  59.0 0.0 collective-permute-done.12.refs_7_.refs_8_
  59.0 3.2 %collective-permute-start.13 = (bf16[256,256]{1,0:T(8,128)(2,1)S(1)}, bf16[256,256]{1,0:T(8,128)(2,1)S(1)}, u32[]{:S(2)}, u32[]{:S(2)}) collective-permute-start(bf16[256,256]{1,0:T(8,128)(2,1)S(1)} %collective-permute-done.12.refs_7_.refs_8_), channel_id=1, source_target_pairs={{0,56},{8,0},{16,8},{24,16},{32,24},{40,32},{48,40},{56,48},{64,12... | collective-permute-start | bytes 393224 | tf_op jit(solution)/shard_map/ppermute | solution.py:401
  62.3 0.0 collective-permute-done.14.refs_0_
  62.3 0.7 copy-done.1
  63.0 0.0 collective-permute-done.15.refs_1_
  63.0 0.7 copy-done.3
  63.7 0.0 collective-permute-done.16.refs_0_
  63.7 0.7 copy-done.5
  64.4 0.8 collective-permute-done.9.refs_4_.refs_5_
  65.2 0.0 collective-permute-done.13.refs_8_.refs_9_
  65.2 0.0 all-to-all-done.first_ref
  65.2 6.7 %all-to-all-start.1 = ((bf16[32,4,32,128]{3,2,1,0:T(8,128)(2,1)}), bf16[32,4,32,128]{3,2,1,0:T(8,128)(2,1)S(1)}, u32[]{:S(2)}, u32[]{:S(2)}) async-start(bf16[32,4,32,128]{3,2,1,0:T(8,128)(2,1)} %get-tuple-element.53), calls=%async_computation.1 | async-start | bytes 2097152 | tf_op jit(solution)/shard_map/all_to_all | solution.py:407
  71.9 0.0 copy-start.6
  71.9 0.9 copy-done.6
  72.8 1.4 %attend.3 = bf16[144,1024]{1,0:T(8,128)(2,1)S(1)} custom-call(s32[32]{0:T(128)S(1)} %copy-done.7, bf16[128,1024]{1,0:T(8,128)(2,1)S(1)} %copy-done.6, bf16[256,256]{1,0:T(8,128)(2,1)S(1)} %get-tuple-element.38.refs_1_.refs_2_, bf16[256,256]{1,0:T(8,128)(2,1)S(1)} %collective-permute-done.7.refs_2_.refs_3_, ...), custom_call_target="tpu_custom_call" | custom-call | bytes 10485760 | tf_op jit(solution)/shard_map/attend/pallas_call | solution.py:325
  74.2 4.4 %collective-permute-start.17 = (bf16[144,1024]{1,0:T(8,128)(2,1)S(1)}, bf16[144,1024]{1,0:T(8,128)(2,1)S(1)}, u32[]{:S(2)}, u32[]{:S(2)}) collective-permute-start(bf16[144,1024]{1,0:T(8,128)(2,1)S(1)} %attend.3), channel_id=1, source_target_pairs={{0,128},{8,136},{16,144},{24,152},{32,160},{40,168},{48,176},{56,1... | collective-permute-start | bytes 884744 | tf_op jit(solution)/shard_map/ppermute | solution.py:395
  78.6 0.9 copy-done.2
  79.5 0.9 copy-done.4
  80.5 6.2 %attend.4 = (bf16[144,1024]{1,0:T(8,128)(2,1)S(1)}, bf16[144,1024]{1,0:T(8,128)(2,1)S(1)}) custom-call(s32[32]{0:T(128)S(1)} %copy-done.7, bf16[128,1024]{1,0:T(8,128)(2,1)S(1)} %copy-done.2, bf16[128,1024]{1,0:T(8,128)(2,1)S(1)} %copy-done.4, bf16[256,256]{1,0:T(8,128)(2,1)S(1)} %get-tuple-element.38.refs_1_.refs_2_, ...), custom_call_target="tpu_custom_call" | custom-call | bytes 20971520 | tf_op jit(solution)/shard_map/attend/pallas_call | solution.py:325
  86.7 0.1 collective-permute-start.18
  86.8 2.0 %collective-permute-start.19 = (bf16[144,1024]{1,0:T(8,128)(2,1)S(1)}, bf16[144,1024]{1,0:T(8,128)(2,1)S(1)}, u32[]{:S(2)}, u32[]{:S(2)}) collective-permute-start(bf16[144,1024]{1,0:T(8,128)(2,1)S(1)} %get-tuple-element.49), channel_id=1, source_target_pairs={{0,64},{8,72},{16,80},{24,88},{32,96},{40,104},{48,112},{56,120},{... | collective-permute-start | bytes 884744 | tf_op jit(solution)/shard_map/ppermute | solution.py:395
  88.8 1.9 %attend.5.refs_3_ = bf16[144,1024]{1,0:T(8,128)(2,1)S(1)} custom-call(s32[32]{0:T(128)S(1)} %copy-done.7, bf16[128,1024]{1,0:T(8,128)(2,1)S(1)} %get-tuple-element.50.refs_0_, bf16[256,256]{1,0:T(8,128)(2,1)S(1)} %get-tuple-element.38.refs_1_.refs_2_, bf16[256,256]{1,0:T(8,128)(2,1)S(1)} %collective-permute-done.7.refs_2_.refs_3_, ...), custom_call_target="tpu_custom_call" | custom-call | bytes 10485760 | tf_op jit(solution)/shard_map/attend/pallas_call | solution.py:325
  90.7 0.0 collective-permute-done.17.refs_0_
  90.7 6.3 %collective-permute-done.18.refs_1_ = bf16[144,1024]{1,0:T(8,128)(2,1)S(1)} collective-permute-done((bf16[144,1024]{1,0:T(8,128)(2,1)S(1)}, bf16[144,1024]{1,0:T(8,128)(2,1)S(1)}, u32[]{:S(2)}, u32[]{:S(2)}) %collective-permute-start.18) | collective-permute-done | bytes 294944 | tf_op jit(solution)/shard_map/ppermute | solution.py:395
  97.0 0.0 collective-permute-done.19.refs_2_
  97.1 1.0 %merge.1 = bf16[256,512]{1,0:T(8,128)(2,1)} custom-call(bf16[144,1024]{1,0:T(8,128)(2,1)S(1)} %collective-permute-done.17.refs_0_, bf16[144,1024]{1,0:T(8,128)(2,1)S(1)} %collective-permute-done.18.refs_1_, bf16[144,1024]{1,0:T(8,128)(2,1)S(1)} %collective-permute-done.19.refs_2_, bf16[144,1024]{1,0:T(8,128)(2,1)S(1)} %attend.5.refs_3_), custom_call_target="tpu_custom_call" | custom-call | bytes 4194304 | tf_op jit(solution)/shard_map/merge/pallas_call | solution.py:366
  98.1 0.0 all-to-all-done.1.second_ref
  98.1 2.9 %place.1 = (bf16[256,32,128]{2,1,0:T(8,128)(2,1)}, s32[1]{0:T(128)}) custom-call(bf16[32,4,32,128]{3,2,1,0:T(8,128)(2,1)S(1)} %all-to-all-done.first_ref, bf16[32,4,32,128]{3,2,1,0:T(8,128)(2,1)S(1)} %all-to-all-done.1.second_ref), custom_call_target="tpu_custom_call" | custom-call | bytes 10485760 | tf_op jit(solution)/shard_map/place/pallas_call | solution.py:145
  (11 shorter events, 0.1 us)
Async XLA Ops:
  0.6 15.2 %copy-start = (bf16[256,512]{1,0:T(8,128)(2,1)S(1)}, bf16[256,512]{1,0:T(8,128)(2,1)}, u32[]{:S(2)}) copy-start(bf16[256,512]{1,0:T(8,128)(2,1)} %refs_0_.1) | copy-start | bytes 786436
  0.6 19.4 %copy-start.7 = (s32[32]{0:T(128)S(1)}, s32[32]{0:T(128)}, u32[]{:S(2)}) copy-start(s32[32]{0:T(128)} %span_ref.5) | copy-start | bytes 388
  0.7 20.7 %copy-start.8 = (bf16[4096]{0:T(1024)(128)(2,1)S(1)}, bf16[4096]{0:T(1024)(128)(2,1)}, u32[]{:S(2)}) copy-start(bf16[4096]{0:T(1024)(128)(2,1)} %param.7) | copy-start | bytes 24580
  4.3 60.9 %all-to-all-start = ((bf16[32,4,32,128]{3,2,1,0:T(8,128)(2,1)}), bf16[32,4,32,128]{3,2,1,0:T(8,128)(2,1)S(1)}, u32[]{:S(2)}, u32[]{:S(2)}) async-start(bf16[32,4,32,128]{3,2,1,0:T(8,128)(2,1)} %get-tuple-element.52), calls=%async_computation | async-start | bytes 2097152 | tf_op jit(solution)/shard_map/all_to_all | solution.py:407
  15.8 10.9 %collective-permute-start = (bf16[256,512]{1,0:T(8,128)(2,1)S(1)}, bf16[256,512]{1,0:T(8,128)(2,1)S(1)}, u32[]{:S(2)}, u32[]{:S(2)}) collective-permute-start(bf16[256,512]{1,0:T(8,128)(2,1)S(1)} %copy-done), channel_id=1, source_target_pairs={{0,4},{1,5},{2,6},{3,7},{4,0},{5,1},{6,2},{7,3},{8,12},{9,13},{10,... | collective-permute-start | bytes 786440 | tf_op jit(solution)/shard_map/ppermute | solution.py:387
  18.0 12.8 %collective-permute-start.1 = (bf16[256,512]{1,0:T(8,128)(2,1)S(1)}, bf16[256,512]{1,0:T(8,128)(2,1)S(1)}, u32[]{:S(2)}, u32[]{:S(2)}) collective-permute-start(bf16[256,512]{1,0:T(8,128)(2,1)S(1)} %copy-done), channel_id=1, source_target_pairs={{0,2},{1,3},{2,4},{3,5},{4,6},{5,7},{6,0},{7,1},{8,10},{9,11},{10,... | collective-permute-start | bytes 786440 | tf_op jit(solution)/shard_map/ppermute | solution.py:387
  18.0 12.8 %collective-permute-start.2 = (bf16[256,512]{1,0:T(8,128)(2,1)S(1)}, bf16[256,512]{1,0:T(8,128)(2,1)S(1)}, u32[]{:S(2)}, u32[]{:S(2)}) collective-permute-start(bf16[256,512]{1,0:T(8,128)(2,1)S(1)} %copy-done), channel_id=1, source_target_pairs={{0,6},{1,7},{2,0},{3,1},{4,2},{5,3},{6,4},{7,5},{8,14},{9,15},{10,... | collective-permute-start | bytes 786440 | tf_op jit(solution)/shard_map/ppermute | solution.py:387
  20.1 11.3 %collective-permute-start.3 = (bf16[256,512]{1,0:T(8,128)(2,1)S(1)}, bf16[256,512]{1,0:T(8,128)(2,1)S(1)}, u32[]{:S(2)}, u32[]{:S(2)}) collective-permute-start(bf16[256,512]{1,0:T(8,128)(2,1)S(1)} %copy-done), channel_id=1, source_target_pairs={{0,1},{1,0},{2,3},{3,2},{4,5},{5,4},{6,7},{7,6},{8,9},{9,8},{10,11... | collective-permute-start | bytes 786440 | tf_op jit(solution)/shard_map/ppermute | solution.py:391
  30.9 1.5 %collective-permute-start.4 = (bf16[256,512]{1,0:T(8,128)(2,1)S(1)}, bf16[256,512]{1,0:T(8,128)(2,1)S(1)}, u32[]{:S(2)}, u32[]{:S(2)}) collective-permute-start(bf16[256,512]{1,0:T(8,128)(2,1)S(1)} %collective-permute-done.1.refs_1_), channel_id=1, source_target_pairs={{0,1},{1,0},{2,3},{3,2},{4,5},{5,4},{6,7},{7,6},{8,9},{9,8},{10,11... | collective-permute-start | bytes 786440 | tf_op jit(solution)/shard_map/ppermute | solution.py:391
  30.9 1.9 %collective-permute-start.5 = (bf16[256,512]{1,0:T(8,128)(2,1)S(1)}, bf16[256,512]{1,0:T(8,128)(2,1)S(1)}, u32[]{:S(2)}, u32[]{:S(2)}) collective-permute-start(bf16[256,512]{1,0:T(8,128)(2,1)S(1)} %collective-permute-done.2.refs_2_), channel_id=1, source_target_pairs={{0,1},{1,0},{2,3},{3,2},{4,5},{5,4},{6,7},{7,6},{8,9},{9,8},{10,11... | collective-permute-start | bytes 786440 | tf_op jit(solution)/shard_map/ppermute | solution.py:391
  31.4 1.8 %collective-permute-start.6 = (bf16[256,512]{1,0:T(8,128)(2,1)S(1)}, bf16[256,512]{1,0:T(8,128)(2,1)S(1)}, u32[]{:S(2)}, u32[]{:S(2)}) collective-permute-start(bf16[256,512]{1,0:T(8,128)(2,1)S(1)} %collective-permute-done.refs_3_), channel_id=1, source_target_pairs={{0,1},{1,0},{2,3},{3,2},{4,5},{5,4},{6,7},{7,6},{8,9},{9,8},{10,11... | collective-permute-start | bytes 786440 | tf_op jit(solution)/shard_map/ppermute | solution.py:391
  38.3 5.9 %collective-permute-start.10 = (bf16[256,256]{1,0:T(8,128)(2,1)S(1)}, bf16[256,256]{1,0:T(8,128)(2,1)S(1)}, u32[]{:S(2)}, u32[]{:S(2)}) collective-permute-start(bf16[256,256]{1,0:T(8,128)(2,1)S(1)} %get-tuple-element.38.refs_1_.refs_2_), channel_id=1, source_target_pairs={{0,56},{8,0},{16,8},{24,16},{32,24},{40,32},{48,40},{56,48},{64,12... | collective-permute-start | bytes 393224 | tf_op jit(solution)/shard_map/ppermute | solution.py:401
  41.1 11.8 %collective-permute-start.7 = (bf16[256,256]{1,0:T(8,128)(2,1)S(1)}, bf16[256,256]{1,0:T(8,128)(2,1)S(1)}, u32[]{:S(2)}, u32[]{:S(2)}) collective-permute-start(bf16[256,256]{1,0:T(8,128)(2,1)S(1)} %get-tuple-element.38.refs_1_.refs_2_), channel_id=1, source_target_pairs={{0,8},{8,16},{16,24},{24,32},{32,40},{40,48},{48,56},{56,0},{64,72... | collective-permute-start | bytes 393224 | tf_op jit(solution)/shard_map/ppermute | solution.py:401
  44.1 8.7 %collective-permute-start.11 = (bf16[256,256]{1,0:T(8,128)(2,1)S(1)}, bf16[256,256]{1,0:T(8,128)(2,1)S(1)}, u32[]{:S(2)}, u32[]{:S(2)}) collective-permute-start(bf16[256,256]{1,0:T(8,128)(2,1)S(1)} %collective-permute-done.10.refs_5_.refs_6_), channel_id=1, source_target_pairs={{0,56},{8,0},{16,8},{24,16},{32,24},{40,32},{48,40},{56,48},{64,12... | collective-permute-start | bytes 393224 | tf_op jit(solution)/shard_map/ppermute | solution.py:401
  47.8 14.5 %collective-permute-start.14 = (bf16[128,1024]{1,0:T(8,128)(2,1)S(1)}, bf16[128,1024]{1,0:T(8,128)(2,1)S(1)}, u32[]{:S(2)}, u32[]{:S(2)}) collective-permute-start(bf16[128,1024]{1,0:T(8,128)(2,1)S(1)} %get-tuple-element.50.refs_0_), channel_id=1, source_target_pairs={{0,64},{8,72},{16,80},{24,88},{32,96},{40,104},{48,112},{56,120},{... | collective-permute-start | bytes 786440 | tf_op jit(solution)/shard_map/ppermute | solution.py:395
  49.3 13.7 %collective-permute-start.15 = (bf16[128,1024]{1,0:T(8,128)(2,1)S(1)}, bf16[128,1024]{1,0:T(8,128)(2,1)S(1)}, u32[]{:S(2)}, u32[]{:S(2)}) collective-permute-start(bf16[128,1024]{1,0:T(8,128)(2,1)S(1)} %get-tuple-element.50.refs_0_), channel_id=1, source_target_pairs={{0,192},{8,200},{16,208},{24,216},{32,224},{40,232},{48,240},{56,2... | collective-permute-start | bytes 786440 | tf_op jit(solution)/shard_map/ppermute | solution.py:395
  51.0 12.6 %collective-permute-start.16 = (bf16[128,1024]{1,0:T(8,128)(2,1)S(1)}, bf16[128,1024]{1,0:T(8,128)(2,1)S(1)}, u32[]{:S(2)}, u32[]{:S(2)}) collective-permute-start(bf16[128,1024]{1,0:T(8,128)(2,1)S(1)} %get-tuple-element.50.refs_0_), channel_id=1, source_target_pairs={{0,128},{8,136},{16,144},{24,152},{32,160},{40,168},{48,176},{56,1... | collective-permute-start | bytes 786440 | tf_op jit(solution)/shard_map/ppermute | solution.py:395
  52.8 6.2 %collective-permute-start.8 = (bf16[256,256]{1,0:T(8,128)(2,1)S(1)}, bf16[256,256]{1,0:T(8,128)(2,1)S(1)}, u32[]{:S(2)}, u32[]{:S(2)}) collective-permute-start(bf16[256,256]{1,0:T(8,128)(2,1)S(1)} %collective-permute-done.7.refs_2_.refs_3_), channel_id=1, source_target_pairs={{0,8},{8,16},{16,24},{24,32},{32,40},{40,48},{48,56},{56,0},{64,72... | collective-permute-start | bytes 393224 | tf_op jit(solution)/shard_map/ppermute | solution.py:401
  52.8 6.2 %collective-permute-start.12 = (bf16[256,256]{1,0:T(8,128)(2,1)S(1)}, bf16[256,256]{1,0:T(8,128)(2,1)S(1)}, u32[]{:S(2)}, u32[]{:S(2)}) collective-permute-start(bf16[256,256]{1,0:T(8,128)(2,1)S(1)} %collective-permute-done.11.refs_6_.refs_7_), channel_id=1, source_target_pairs={{0,56},{8,0},{16,8},{24,16},{32,24},{40,32},{48,40},{56,48},{64,12... | collective-permute-start | bytes 393224 | tf_op jit(solution)/shard_map/ppermute | solution.py:401
  59.0 6.2 %collective-permute-start.9 = (bf16[256,256]{1,0:T(8,128)(2,1)S(1)}, bf16[256,256]{1,0:T(8,128)(2,1)S(1)}, u32[]{:S(2)}, u32[]{:S(2)}) collective-permute-start(bf16[256,256]{1,0:T(8,128)(2,1)S(1)} %collective-permute-done.8.refs_3_.refs_4_), channel_id=1, source_target_pairs={{0,8},{8,16},{16,24},{24,32},{32,40},{40,48},{48,56},{56,0},{64,72... | collective-permute-start | bytes 393224 | tf_op jit(solution)/shard_map/ppermute | solution.py:401
  59.0 6.2 %collective-permute-start.13 = (bf16[256,256]{1,0:T(8,128)(2,1)S(1)}, bf16[256,256]{1,0:T(8,128)(2,1)S(1)}, u32[]{:S(2)}, u32[]{:S(2)}) collective-permute-start(bf16[256,256]{1,0:T(8,128)(2,1)S(1)} %collective-permute-done.12.refs_7_.refs_8_), channel_id=1, source_target_pairs={{0,56},{8,0},{16,8},{24,16},{32,24},{40,32},{48,40},{56,48},{64,12... | collective-permute-start | bytes 393224 | tf_op jit(solution)/shard_map/ppermute | solution.py:401
  62.3 0.7 copy-start.1
  63.0 0.7 copy-start.3
  63.7 0.7 copy-start.5
  65.2 32.9 %all-to-all-start.1 = ((bf16[32,4,32,128]{3,2,1,0:T(8,128)(2,1)}), bf16[32,4,32,128]{3,2,1,0:T(8,128)(2,1)S(1)}, u32[]{:S(2)}, u32[]{:S(2)}) async-start(bf16[32,4,32,128]{3,2,1,0:T(8,128)(2,1)} %get-tuple-element.53), calls=%async_computation.1 | async-start | bytes 2097152 | tf_op jit(solution)/shard_map/all_to_all | solution.py:407
  71.9 1.0 copy-start.6
  74.2 16.5 %collective-permute-start.17 = (bf16[144,1024]{1,0:T(8,128)(2,1)S(1)}, bf16[144,1024]{1,0:T(8,128)(2,1)S(1)}, u32[]{:S(2)}, u32[]{:S(2)}) collective-permute-start(bf16[144,1024]{1,0:T(8,128)(2,1)S(1)} %attend.3), channel_id=1, source_target_pairs={{0,128},{8,136},{16,144},{24,152},{32,160},{40,168},{48,176},{56,1... | collective-permute-start | bytes 884744 | tf_op jit(solution)/shard_map/ppermute | solution.py:395
  78.6 0.9 copy-start.2
  79.5 0.9 copy-start.4
  86.7 10.3 %collective-permute-start.18 = (bf16[144,1024]{1,0:T(8,128)(2,1)S(1)}, bf16[144,1024]{1,0:T(8,128)(2,1)S(1)}, u32[]{:S(2)}, u32[]{:S(2)}) collective-permute-start(bf16[144,1024]{1,0:T(8,128)(2,1)S(1)} %get-tuple-element.48), channel_id=1, source_target_pairs={{0,192},{8,200},{16,208},{24,216},{32,224},{40,232},{48,240},{56,2... | collective-permute-start | bytes 884744 | tf_op jit(solution)/shard_map/ppermute | solution.py:395
  86.8 10.3 %collective-permute-start.19 = (bf16[144,1024]{1,0:T(8,128)(2,1)S(1)}, bf16[144,1024]{1,0:T(8,128)(2,1)S(1)}, u32[]{:S(2)}, u32[]{:S(2)}) collective-permute-start(bf16[144,1024]{1,0:T(8,128)(2,1)S(1)} %get-tuple-element.49), channel_id=1, source_target_pairs={{0,64},{8,72},{16,80},{24,88},{32,96},{40,104},{48,112},{56,120},{... | collective-permute-start | bytes 884744 | tf_op jit(solution)/shard_map/ppermute | solution.py:395
